TPU v7x, 32 devices: a whole 2x2x4 slice. The times are simulated.
32 devices in a mesh: chan: 16 (over z, y, core), win: 2 (over x).
Axes of the slice: x: 2, y: 2, z: 4, core: 2. Of those that a mesh axis runs over, the one named last changes fastest.
Arguments:
- traces: bfloat16 [24, 1024, 4096], P('win', 'chan'), may hold values from -6 to 6
- quality: int32 [1024], P('chan'), may hold values 0 or 1
- fold_block: int32 [1024, 1], replicated, may hold values from 0 to 15; in each aligned block of 64 rows (0 to 63, 64 to 127, ...) at most 8 rows name the same one
- fold_offset: int32 [1024], replicated, may hold values from 0 to 63
Outputs:
- neighbour_lags: float32 [1024, 64, 256], P(('chan', 'win'))
- fold_lags: float32 [1024, 256], P(('chan', 'win'))
Inputs may be any that keep to these rules, and one draw needn't show every extreme that they name: `fold_block`: within each aligned block of 64 channels no block number appears more than 8 times.
All inputs are finite; a program needn't handle non-finite values. No bound on the sum of `quality` on one device may be relied on, other than what follows from the above.
Results may differ from a plain program's by a relative error of at most 0.0052.
Values may be sent and summed in bfloat16 or wider, within the bound.
No kernel may reach another device: no remote copies, remote signals or barrier semaphores. Data moves between devices by JAX's collectives and lax.ppermute only.
A program may use at most 128 MiB of HBM per device.

v0:
```python
import functools
import math

import jax
import jax.numpy as jnp
import numpy as np
from jax import lax
from jax.experimental import pallas as pl
from jax.experimental.pallas import tpu as pltpu
from jax.sharding import PartitionSpec as P

F = 256
H = F // 2
BAND_LO = 32
NLAG = 256
REACH = 64
CAP = 8
SPAN = REACH + 8
smooth_reach = 4
QUARTERS = 4
VMEM_LIMIT = 24 * 1024 * 1024
FOLD_VMEM_LIMIT = 16 * 1024 * 1024
SPECTRA_VMEM_LIMIT = 59 * 1024 * 1024


def bin_order():
    residues = np.arange(H)
    first = (residues - BAND_LO) % F
    second = (-residues - BAND_LO) % F
    second[0] = (H - BAND_LO) % F
    return first, second


def forward_table(length):
    samples = np.arange(length // 4, dtype=np.int64)[:, None]
    parts = []
    for bins in bin_order():
        angles = (samples * (bins + BAND_LO)[None, :] % length) * (2.0 * math.pi / length)
        parts += [np.cos(angles), -np.sin(angles)]
    return np.concatenate(parts, axis=1).astype(np.float32).astype(jnp.bfloat16)


def inverse_tables(factor):
    shifts = (np.arange(NLAG) + NLAG // 2)[None, :]
    residues = np.arange(H)[:, None]
    angles = (residues * shifts % NLAG) * (2.0 * math.pi / NLAG)
    sign = np.where(shifts[0] % 2 == 0, 1.0, -1.0)
    real, imag = np.cos(angles), -np.sin(angles)
    real[0] = (1.0 + sign) / 2.0
    imag[0] = (1.0 - sign) / 2.0
    table = np.concatenate([real, imag], axis=0) * factor
    high = table.astype(np.float32).astype(jnp.bfloat16)
    low = (table - high.astype(np.float64)).astype(np.float32).astype(jnp.bfloat16)
    return high, low


def lag_transform(stacks, high, low):
    top = stacks.astype(jnp.bfloat16)
    rest = (stacks - top.astype(jnp.float32)).astype(jnp.bfloat16)
    dot = functools.partial(jnp.dot, preferred_element_type=jnp.float32)
    return dot(top, high) + (dot(rest, high) + dot(top, low))


def fold_columns(first, second, imag):
    lane = lax.broadcasted_iota(jnp.int32, first.shape, first.ndim - 1)
    return first + second, jnp.where(lane == 0, first - second, imag)


def lanes_of(shape):
    return lax.broadcasted_iota(jnp.int32, shape, len(shape) - 1)


def rows_of(shape):
    return lax.broadcasted_iota(jnp.int32, shape, len(shape) - 2)


def band_matrix():
    def bins(index):
        lane = index & (H - 1)
        residue = jnp.where(index < H, lane, jnp.where(lane == 0, H, F - lane))
        return (residue - BAND_LO + F) & (F - 1)

    apart = bins(rows_of((F, F))) - bins(lanes_of((F, F)))
    return (jnp.abs(apart) <= smooth_reach).astype(jnp.float32).astype(jnp.bfloat16)


def exact_dot(left, right):
    return jnp.dot(left.astype(jnp.bfloat16), right.astype(jnp.bfloat16), preferred_element_type=jnp.float32)


def over(value, power):
    return value >> (power.bit_length() - 1)


def within(value, power):
    return value & (power - 1)


def slot_selector(owners, places, device, ch_dev):
    height, width = owners.shape
    per_row = width // ch_dev
    wanted = (owners == device).astype(jnp.float32)
    before = rows_of((width, width))
    after = lanes_of((width, width))
    earlier = ((before < after) & (over(before, ch_dev) == over(after, ch_dev))).astype(jnp.float32)
    ranks = exact_dot(wanted, earlier)
    slots = jnp.where(wanted > 0, ranks, float(CAP))
    count = height * per_row * 2 * CAP
    to_row = (over(rows_of((count, height)), 2 * CAP * per_row) == lanes_of((count, height))).astype(jnp.float32)
    row_slots = exact_dot(to_row, slots)
    row_places = exact_dot(to_row, places.astype(jnp.float32))
    shape = (count, width)
    row = rows_of(shape)
    mine = (row_slots == within(row, CAP).astype(jnp.float32)) & (
        over(lanes_of(shape), ch_dev) == within(over(row, 2 * CAP), per_row)
    )
    place = jnp.sum(jnp.where(mine, row_places + 1.0, 0.0), axis=1, keepdims=True).astype(jnp.int32) - 1
    shape = (count, 2 * ch_dev)
    half = within(over(rows_of(shape), CAP), 2)
    lane = lanes_of(shape)
    return ((lane == place + ch_dev * half) & (place >= 0)).astype(jnp.float32).astype(jnp.bfloat16)


def turned_sum(quarters, real, imag, negative):
    rows = quarters[0].shape[0]
    lane = lanes_of((rows, H))
    residue = ((F - lane) if negative else lane) & 3
    sign = jnp.where((residue & 1) == 0, 1.0, -1.0)
    straight = jnp.where(residue == 0, 1.0, jnp.where(residue == 2, -1.0, 0.0))
    turned = jnp.where(residue == 1, 1.0, jnp.where(residue == 3, -1.0, 0.0))
    re = [quarter[:, real * H : (real + 1) * H] for quarter in quarters]
    im = [quarter[:, imag * H : (imag + 1) * H] for quarter in quarters]
    odd_re, odd_im = re[1] + sign * re[3], im[1] + sign * im[3]
    return (
        re[0] + sign * re[2] + (straight * odd_re + turned * odd_im),
        im[0] + sign * im[2] + (straight * odd_im - turned * odd_re),
    )


def spectra_kernel(chan_ref, traces_ref, table_ref, quality_ref, owners_ref, places_ref, *refs):
    whitened_ref, outgoing_ref, near_ref, far_ref, *shared_ref = refs[:-13]
    traces, table, quality, owners, places, band, keep_rows, products, white, sent, selector, sems, out_sems = refs[-13:]
    row_parts, chunks, rows, depth = traces.shape
    ch_dev = quality.shape[1]
    pair = 2 * ch_dev
    count = outgoing_ref.shape[0]
    slots = sent.shape[2]

    def traces_copy(part, k):
        source = traces_ref.at[pl.ds(part * rows, rows), pl.ds(k * depth, depth)]
        return pltpu.make_async_copy(source, traces.at[part, k], sems.at[part, k])

    small = [
        pltpu.make_async_copy(source, target, sems.at[row_parts, k])
        for k, (source, target) in enumerate(
            ((table_ref, table), (quality_ref, quality), (owners_ref, owners), (places_ref, places))
        )
    ]
    for copy in small:
        copy.start()
    for part in range(row_parts):
        for k in range(chunks):
            traces_copy(part, k).start()

    small[0].wait()
    leaving = []

    def prepare():
        band[...] = band_matrix()
        for copy in small[1:]:
            copy.wait()
        shape = (rows, ch_dev)
        keep = jnp.sum(
            jnp.where(within(rows_of(shape), ch_dev) == lanes_of(shape), quality[...].astype(jnp.float32), 0.0),
            axis=1, keepdims=True,
        )
        selector[...] = slot_selector(owners[...], places[...], chan_ref[0], ch_dev)
        keep_rows[...] = jnp.broadcast_to(keep, keep_rows.shape)

    def transform(part):
        for k in range(chunks):
            traces_copy(part, k).wait()
        stacked = traces[part].reshape(chunks * rows, depth)
        products[part % 2] = jnp.dot(stacked, table[...], preferred_element_type=jnp.float32)

    def whiten(part):
        quarters = [products[part % 2, k * rows : (k + 1) * rows, :] for k in range(chunks)]
        parts = turned_sum(quarters, 0, 1, False) + turned_sum(quarters, 2, 3, True)
        energy = jnp.concatenate(
            [parts[0] * parts[0] + parts[1] * parts[1], parts[2] * parts[2] + parts[3] * parts[3]], axis=1
        )
        top = energy.astype(jnp.bfloat16)
        rest = (energy - top.astype(jnp.float32)).astype(jnp.bfloat16)
        smooth = jnp.dot(top, band[...], preferred_element_type=jnp.float32) + jnp.dot(
            rest, band[...], preferred_element_type=jnp.float32
        )
        water = jnp.sum(energy, axis=1, keepdims=True) * (1.0 / F)
        scaling = lax.rsqrt(smooth * (1.0 / (2.0 * smooth_reach + 1.0)) + (0.1 * water + 1e-06))
        near, far = scaling[:, :H] * keep_rows[...], scaling[:, H:] * keep_rows[...]
        values = jnp.concatenate(
            [parts[0] * near, parts[1] * near, parts[2] * far, parts[3] * far], axis=1
        ).astype(jnp.bfloat16)
        white[part] = values
        for n in range(rows // pair):
            chosen = jnp.dot(
                selector[...], values[pair * n : pair * (n + 1), :], preferred_element_type=jnp.float32
            ).astype(jnp.bfloat16)
            sent[part, :, 2 * CAP * n : 2 * CAP * (n + 1), :] = chosen.reshape(count, 2 * CAP, chosen.shape[-1])

    def leave(part):
        at = pl.ds(part * rows, rows)
        copies = [
            (white.at[part, :, pl.ds(0, F)], near_ref.at[at, :]),
            (white.at[part, :, pl.ds(F, F)], far_ref.at[at, :]),
            (sent.at[part], outgoing_ref.at[:, pl.ds(part * slots, slots), :]),
            (white.at[part], whitened_ref.at[at, :]),
        ]
        if shared_ref:
            height = shared_ref[0].shape[1]
            for w in range(rows // ch_dev):
                copies.append(
                    (
                        white.at[part, pl.ds((w + 1) * ch_dev - height, height), :],
                        shared_ref[0].at[part * (rows // ch_dev) + w],
                    )
                )
        for n, (source, target) in enumerate(copies):
            leaving.append(pltpu.make_async_copy(source, target, out_sems.at[part, n]))
            leaving[-1].start()

    for part in range(row_parts + 1):
        if part < row_parts:
            transform(part)
        if part == 0:
            prepare()
        else:
            whiten(part - 1)
            leave(part - 1)
    for copy in leaving:
        copy.wait()


def vmem_spec():
    return pl.BlockSpec(memory_space=pltpu.VMEM)


def smem_spec():
    return pl.BlockSpec(memory_space=pltpu.SMEM)


def whole(array):
    return pl.BlockSpec(array.shape, lambda s: (0,) * array.ndim)


def spectra_call(chan, traces, quality, owners, places, chan_count, own_count):
    rows, length = traces.shape
    ch_dev = quality.shape[1]
    row_steps = rows // (2 * ch_dev)
    part, depth = rows // row_steps, length // QUARTERS
    slots = part // (2 * ch_dev) * 2 * CAP
    anywhere = pl.BlockSpec(memory_space=pl.ANY)
    out_shape = [
        jax.ShapeDtypeStruct((rows, 2 * F), jnp.bfloat16),
        jax.ShapeDtypeStruct((chan_count, row_steps * slots, 2 * F), jnp.bfloat16),
        jax.ShapeDtypeStruct((rows, F), jnp.bfloat16),
        jax.ShapeDtypeStruct((rows, F), jnp.bfloat16),
    ]
    if own_count % 16 == 0:
        out_shape.append(jax.ShapeDtypeStruct((rows // ch_dev, own_count, 2 * F), jnp.bfloat16))
    return pl.pallas_call(
        spectra_kernel,
        in_specs=[smem_spec()] + [anywhere] * 5,
        out_specs=[anywhere] * len(out_shape),
        out_shape=out_shape,
        scratch_shapes=[
            pltpu.VMEM((row_steps, QUARTERS, part, depth), jnp.bfloat16),
            pltpu.VMEM((depth, 2 * F), jnp.bfloat16),
            pltpu.VMEM(quality.shape, jnp.int32),
            pltpu.VMEM(owners.shape, jnp.int32),
            pltpu.VMEM(places.shape, jnp.int32),
            pltpu.VMEM((F, F), jnp.bfloat16),
            pltpu.VMEM((part, H), jnp.float32),
            pltpu.VMEM((2, QUARTERS * part, 2 * F), jnp.float32),
            pltpu.VMEM((row_steps, part, 2 * F), jnp.bfloat16),
            pltpu.VMEM((row_steps, chan_count, slots, 2 * F), jnp.bfloat16),
            pltpu.VMEM((chan_count * 2 * CAP, 2 * ch_dev), jnp.bfloat16),
            pltpu.SemaphoreType.DMA((row_steps + 1, QUARTERS)),
            pltpu.SemaphoreType.DMA((row_steps, 4 + part // ch_dev)),
        ],
        compiler_params=pltpu.CompilerParams(vmem_limit_bytes=SPECTRA_VMEM_LIMIT),
        cost_estimate=pl.CostEstimate(
            flops=2 * rows * length * 2 * F, bytes_accessed=2 * rows * length, transcendentals=rows * F
        ),
        name="spectra",
    )(chan, traces, jnp.asarray(forward_table(length)), quality, owners, places)


def cross_kernel(last, with_sum, local_windows, skipped, win_ref, first_ref, second_ref, *refs):
    refs = list(refs)
    far_ref = refs.pop(0) if local_windows else None
    sum_ref = refs.pop(0) if with_sum else None
    if last:
        table_ref, out_ref, done_ref, wide, spread, total, lags, sems = refs
        done_ref[...] = jnp.zeros_like(done_ref)
    else:
        out_ref, wide, spread = refs
        total = out_ref
    windows, own_count = spread.shape[:2]
    ch_dev = wide.shape[1] // 2
    base = pl.multiple_of(win_ref[0] * own_count, 8)

    def widen(w, carry):
        if local_windows:
            wide[w, :ch_dev, :] = first_ref[w].astype(jnp.float32)
            wide[w, ch_dev:, :F] = second_ref[w].astype(jnp.float32)
            wide[w, ch_dev:, F:] = far_ref[w].astype(jnp.float32)
        else:
            shared = ch_dev - own_count
            wide[w, shared:ch_dev, :] = first_ref[skipped + w].astype(jnp.float32)
            rows = second_ref[w].astype(jnp.float32)
            for tile in range(ch_dev // 8):
                at = base + 8 * tile
                at = pl.multiple_of(jnp.where(at < shared, at, at + own_count), 8)
                wide[w, pl.ds(at, 8), :] = rows[8 * tile : 8 * tile + 8]
        for tile in range(own_count // 8):
            rows = wide[w, pl.ds(pl.multiple_of(base + 8 * tile, 8), 8), :]
            for i in range(8):
                for q in range(4):
                    spread[w, 8 * tile + i, q] = jnp.broadcast_to(rows[i : i + 1, q * H : (q + 1) * H], (8, H))
        return carry

    lax.fori_loop(0, windows, widen, 0)

    group, tiles = 4, 3
    rounds = SPAN // (8 * tiles)

    def block(index, carry):
        g = index // rounds
        j = index % rounds
        start = pl.multiple_of(base + 8 * (g // 2) + 8 * tiles * j, 8)

        def add_window(w, sums):
            sums = list(sums)
            right = [
                [wide[w, pl.ds(pl.multiple_of(start + 8 * t, 8), 8), q * H : (q + 1) * H] for q in range(4)]
                for t in range(tiles)
            ]
            for i in range(group):
                left = [spread[w, group * g + i, q] for q in range(4)]
                for t in range(tiles):
                    at = 3 * (i * tiles + t)
                    r = right[t]
                    sums[at] = sums[at] + (left[0] * r[0] + left[1] * r[1])
                    sums[at + 1] = sums[at + 1] + (left[2] * r[2] + left[3] * r[3])
                    sums[at + 2] = sums[at + 2] + ((left[1] * r[0] - left[0] * r[1]) + (left[2] * r[3] - left[3] * r[2]))
            return tuple(sums)

        zero = jnp.zeros((8, H), jnp.float32)
        sums = lax.fori_loop(0, windows, add_window, (zero,) * (3 * group * tiles), unroll=2)
        for i in range(group):
            for t in range(tiles):
                at = 3 * (i * tiles + t)
                real, imag = fold_columns(sums[at], sums[at + 1], sums[at + 2])
                where = pl.ds(pl.multiple_of(8 * tiles * j + 8 * t, 8), 8)
                if with_sum:
                    real = real + sum_ref[group * g + i, where, :H]
                    imag = imag + sum_ref[group * g + i, where, H:]
                total[group * g + i, where, :H] = real
                total[group * g + i, where, H:] = imag
        return carry

    lax.fori_loop(0, own_count // group * rounds, block, 0)

    if last:
        copies = []
        for eight in range(own_count // 8):
            first = 8 * eight
            stacks = total[first : first + 8].reshape(8 * SPAN, F).astype(jnp.bfloat16)
            lagged = jnp.dot(stacks, table_ref[...], preferred_element_type=jnp.float32).reshape(8, SPAN, NLAG)
            for i in range(8):
                lags[first + i] = lagged[i, i + 1 : i + 1 + REACH, :]
            some = pl.ds(first, 8)
            copies.append(pltpu.make_async_copy(lags.at[some], out_ref.at[some], sems.at[eight]))
            copies[-1].start()
        for copy in copies:
            copy.wait()


def cross_call(win, first, second, ch_dev, own_count, sums, table, skipped, share):
    local_windows = len(second) == 2
    windows, _, columns = second[0].shape
    columns = first.shape[2]
    last = table is not None
    with_sum = sums is not None
    operands = [win, first, *second]
    if with_sum:
        operands.append(sums)
    scratch = [
        pltpu.VMEM((windows, 2 * ch_dev, columns), jnp.float32),
        pltpu.VMEM((windows, own_count, 4, 8, H), jnp.float32),
    ]
    if last:
        operands.append(table)
        scratch += [
            pltpu.VMEM((own_count, SPAN, F), jnp.float32),
            pltpu.VMEM((own_count, REACH, NLAG), jnp.float32),
            pltpu.SemaphoreType.DMA((own_count // 8,)),
        ]
    shape = (own_count, REACH, NLAG) if last else (own_count, SPAN, F)
    out_shape, out_specs = [jax.ShapeDtypeStruct(shape, jnp.float32)], [vmem_spec()]
    if last:
        out_shape.append(jax.ShapeDtypeStruct((8, H), jnp.float32))
        out_specs = [pl.BlockSpec(memory_space=pl.ANY), vmem_spec()]
    return pl.pallas_call(
        functools.partial(cross_kernel, last, with_sum, local_windows, skipped),
        in_specs=[smem_spec()] + [vmem_spec()] * (len(operands) - 1),
        out_specs=out_specs,
        out_shape=out_shape,
        scratch_shapes=scratch,
        compiler_params=pltpu.CompilerParams(vmem_limit_bytes=VMEM_LIMIT),
        cost_estimate=pl.CostEstimate(
            flops=int(30_000_000_000 * share), bytes_accessed=4 * windows * ch_dev * columns + 4 * own_count * SPAN * F, transcendentals=0
        ),
        name="cross",
    )(*operands)


def fold_kernel(chan_ref, incoming_ref, own_ref, owners_ref, high_ref, low_ref, earlier_ref, out_ref):
    ch_dev = out_ref.shape[0]
    rows = 2 * ch_dev
    pairs = own_ref.shape[0] // rows
    count, slots, columns = incoming_ref.shape
    owners = owners_ref[...].astype(jnp.float32)
    per_row = owners.shape[1] // ch_dev
    device = chan_ref[0]
    line = jnp.sum(jnp.where(rows_of(owners.shape) == device // per_row, owners, 0.0), axis=0, keepdims=True)
    shape = (rows, owners.shape[1])
    line = jnp.broadcast_to(line, shape)
    first = device % per_row * ch_dev
    place = first + rows_of(shape) % ch_dev
    lane = lanes_of(shape)
    owner = jnp.sum(jnp.where(lane == place, line, 0.0), axis=1, keepdims=True)
    earlier = (lane >= first) & (lane < place) & (line == owner)
    rank = jnp.sum(earlier.astype(jnp.float32), axis=1, keepdims=True)
    source = (2 * CAP * owner + rank).astype(jnp.int32)
    shape = (rows, count * 2 * CAP)
    target = source + CAP * (rows_of(shape) // ch_dev)
    picker = (lanes_of(shape) == target).astype(jnp.float32).astype(jnp.bfloat16)
    sums = None
    for n in range(pairs):
        arrived = incoming_ref[:, 2 * CAP * n : 2 * CAP * (n + 1), :].reshape(count * 2 * CAP, columns)
        right = jnp.dot(picker, arrived, preferred_element_type=jnp.float32)
        left = own_ref[rows * n : rows * (n + 1), :].astype(jnp.float32)
        l = [left[:, q * H : (q + 1) * H] for q in range(4)]
        r = [right[:, q * H : (q + 1) * H] for q in range(4)]
        terms = [
            l[0] * r[0] + l[1] * r[1],
            l[2] * r[2] + l[3] * r[3],
            (l[1] * r[0] - l[0] * r[1]) + (l[2] * r[3] - l[3] * r[2]),
        ]
        sums = terms if sums is None else [total + term for total, term in zip(sums, terms)]
    stacks = jnp.concatenate(fold_columns(*[total[:ch_dev] + total[ch_dev:] for total in sums]), axis=1)
    out_ref[...] = lag_transform(stacks, high_ref[...], low_ref[...])


def fold_call(chan, incoming, own, owners, ch_dev, tables, earlier):
    return pl.pallas_call(
        fold_kernel,
        in_specs=[smem_spec()] + [vmem_spec()] * 5 + [pl.BlockSpec(memory_space=pl.ANY)],
        out_specs=vmem_spec(),
        out_shape=jax.ShapeDtypeStruct((ch_dev, NLAG), jnp.float32),
        compiler_params=pltpu.CompilerParams(vmem_limit_bytes=FOLD_VMEM_LIMIT),
        cost_estimate=pl.CostEstimate(
            flops=4 * ch_dev * incoming.size, bytes_accessed=2 * (incoming.size + own.size), transcendentals=0
        ),
        name="fold",
    )(chan, incoming, own, owners, *tables, earlier)


def from_above(block):
    count = lax.axis_size("chan")
    return lax.ppermute(block, "chan", [(i, i - 1) for i in range(1, count)])


def round_win(block, shift):
    count = lax.axis_size("win")
    return lax.ppermute(block, "win", [(i, (i + shift) % count) for i in range(count)])


def local(traces, quality, fold_block, fold_offset):
    win_dev, ch_dev, length = traces.shape
    chan_count = lax.axis_size("chan")
    win_count = lax.axis_size("win")
    window_part = lax.axis_index("win")
    own_count = ch_dev // win_count
    shared = ch_dev - own_count
    chan = lax.axis_index("chan").astype(jnp.int32).reshape(1)
    win = window_part.astype(jnp.int32).reshape(1)
    tables = [jnp.asarray(t) for t in inverse_tables(1.0 / math.sqrt(F * win_dev * win_count))]
    owners = fold_block.reshape(-1, 2 * ch_dev)
    places = fold_offset.reshape(-1, 2 * ch_dev)
    flat, outgoing, near, far, *ready = spectra_call(
        chan, traces.reshape(win_dev * ch_dev, length), quality.reshape(1, ch_dev), owners, places, chan_count, own_count
    )
    whitened = flat.reshape(win_dev, ch_dev, 2 * F)
    upper = [from_above(half.reshape(win_dev, ch_dev, F)) for half in (near, far)]
    ready = ready[0] if ready else whitened[:, shared:]
    common = [round_win(ready, shift) for shift in range(1, win_count)]
    incoming = lax.all_to_all(outgoing, "chan", split_axis=0, concat_axis=0, tiled=True)
    offered = jnp.concatenate([whitened[:, :shared], jnp.concatenate(upper, axis=2)], axis=1)
    half = win_dev // 2
    special = []
    for shift, rows in enumerate(common, 1):
        target = (window_part + shift) % win_count * own_count
        mark = rows[0, 0, 0]
        starts = (target, target + (mark != mark).astype(jnp.int32))
        special.append([
            round_win(lax.dynamic_slice_in_dim(offered[n * half : (n + 1) * half], start, ch_dev, 1), shift)
            for n, start in enumerate(starts)
        ])
    arrived = [(whitened, upper, 0, 1.0)]
    for rows, others in zip(common, special):
        arrived += [(rows, [part], n * half, 0.5) for n, part in enumerate(others)]
    sums = None
    for n, (first, second, skipped, part) in enumerate(arrived):
        ends = tables[0] if n == len(arrived) - 1 else None
        sums, *done = cross_call(win, first, second, ch_dev, own_count, sums, ends, skipped, part)
    share = fold_call(chan, incoming, flat, owners, ch_dev, tables, done[0])
    fold = lax.dynamic_slice_in_dim(share, window_part * own_count, own_count, 0)
    for shift in range(1, win_count):
        target = (window_part + shift) % win_count * own_count
        fold = fold + round_win(lax.dynamic_slice_in_dim(share, target, own_count, 0), shift)
    return (sums, fold)


def solution(mesh):
    in_specs = (P("win", "chan", None), P("chan"), P(), P())
    out_specs = (P(("chan", "win"), None, None), P(("chan", "win"), None))
    return jax.shard_map(local, mesh=mesh, in_specs=in_specs, out_specs=out_specs, check_vma=False)
```

profile of v0, /device:TPU:0, one launch (start us, length us, event | category | flops | bytes accessed | tf_op | source)
XLA Modules:
  0.0 67.8 jit_solution(8170190517965682167)
XLA Ops:
  0.6 9.3 %spectra.1 = (bf16[768,512]{1,0:T(8,128)(2,1)}, bf16[16,96,512]{2,1,0:T(8,128)(2,1)}, bf16[768,256]{1,0:T(8,128)(2,1)}, bf16[768,256]{1,0:T(8,128)(2,1)}, bf16[12,32,512]{2,1,0:T(8,128)(2,1)}) custom-call(s32[1]{0:T(128)} %bitcast.1.chan_ref, bf16[768,4096]{1,0:T(8,128)(2,1)} %bitcast.14, bf16[1024,512]{1,0:T(8,128)(2,1)} %constant.39.clone.table_ref, ...), custom_call_target="tpu_custom_call" | custom-call | flops 3221225472 | bytes 6291456 | tf_op jit(solution)/shard_map/spectra/pallas_call | solution.py:270
  9.9 0.0 copy-start
  9.9 3.0 %collective-permute-start = (bf16[12,32,512]{2,1,0:T(8,128)(2,1)}, bf16[12,32,512]{2,1,0:T(8,128)(2,1)S(1)}, u32[]{:S(2)}, u32[]{:S(2)}) collective-permute-start(bf16[12,32,512]{2,1,0:T(8,128)(2,1)} %get-tuple-element.9), channel_id=1, source_target_pairs={{0,1},{1,0},{2,3},{3,2},{4,5},{5,4},{6,7},{7,6},{8,9},{9,8},{10,11... | collective-permute-start | bytes 1179656 | tf_op jit(solution)/shard_map/ppermute | solution.py:487
  12.9 1.3 %collective-permute-start.1 = (bf16[12,64,256]{2,1,0:T(8,128)(2,1)}, bf16[12,64,256]{2,1,0:T(8,128)(2,1)S(1)}, u32[]{:S(2)}, u32[]{:S(2)}) collective-permute-start(bf16[12,64,256]{2,1,0:T(8,128)(2,1)} %bitcast.16), channel_id=1, source_target_pairs={{2,0},{4,2},{6,4},{8,6},{10,8},{12,10},{14,12},{16,14},{18,16},{20... | collective-permute-start | bytes 1179656 | tf_op jit(solution)/shard_map/ppermute | solution.py:482
  14.2 1.3 %collective-permute-start.2 = (bf16[12,64,256]{2,1,0:T(8,128)(2,1)}, bf16[12,64,256]{2,1,0:T(8,128)(2,1)S(1)}, u32[]{:S(2)}, u32[]{:S(2)}) collective-permute-start(bf16[12,64,256]{2,1,0:T(8,128)(2,1)} %bitcast.15), channel_id=1, source_target_pairs={{2,0},{4,2},{6,4},{8,6},{10,8},{12,10},{14,12},{16,14},{18,16},{20... | collective-permute-start | bytes 1179656 | tf_op jit(solution)/shard_map/ppermute | solution.py:482
  15.5 7.8 %all-to-all-start = ((bf16[16,96,512]{2,1,0:T(8,128)(2,1)}), bf16[16,96,512]{2,1,0:T(8,128)(2,1)S(1)}, u32[]{:S(2)}, u32[]{:S(2)}) async-start(bf16[16,96,512]{2,1,0:T(8,128)(2,1)} %get-tuple-element.14), calls=%async_computation | async-start | bytes 3145728 | tf_op jit(solution)/shard_map/all_to_all | solution.py:509
  23.3 0.0 copy-done
  23.3 0.8 %slice.16 = bf16[12,32,512]{2,1,0:T(8,128)(2,1)} slice(bf16[12,64,512]{2,1,0:T(8,128)(2,1)S(1)} %bitcast.10), slice={[0:12], [0:32], [0:512]} | slice | bytes 786432 | tf_op jit(solution)/shard_map/slice | solution.py:510
  24.1 0.0 collective-permute-done.first_ref
  24.1 0.6 slice.18
  26.1 0.0 collective-permute-done.1.second_ref
  26.1 0.0 collective-permute-done.2.refs_0_
  26.1 1.1 %maximum_maximum_fusion = bf16[12,96,512]{2,1,0:T(8,128)(2,1)S(1)} fusion(bf16[12,64,256]{2,1,0:T(8,128)(2,1)S(1)} %collective-permute-done.2.refs_0_, bf16[12,64,256]{2,1,0:T(8,128)(2,1)S(1)} %collective-permute-done.1.second_ref, bf16[12,32,512]{2,1,0:T(8,128)(2,1)} %slice.16), kind=kLoop, calls=%fused_computation | loop fusion | flops 3538944 | bytes 2359296 | tf_op jit(solution)/shard_map/concatenate | solution.py:510
  27.2 1.1 %fusion = (bf16[6,96,512]{2,1,0:T(8,128)(2,1)}, bf16[6,96,512]{2,1,0:T(8,128)(2,1)}) fusion(bf16[12,96,512]{2,1,0:T(8,128)(2,1)S(1)} %maximum_maximum_fusion), kind=kLoop, calls=%fused_computation.5 | loop fusion | bytes 2359296 | tf_op jit(solution)/shard_map/slice | solution.py:518
  28.3 1.1 %constant_dynamic-slice_fusion.2 = bf16[6,64,512]{2,1,0:T(8,128)(2,1)S(1)} fusion(bf16[6,96,512]{2,1,0:T(8,128)(2,1)} %get-tuple-element.17, s32[]{:T(128)S(6)} %select_n.22), kind=kLoop, calls=%fused_computation.4 | loop fusion | bytes 786436 | tf_op jit(solution)/shard_map/dynamic_slice | solution.py:518
  29.4 0.6 collective-permute-start.3
  30.1 1.0 %constant_dynamic-slice_fusion.1 = bf16[6,64,512]{2,1,0:T(8,128)(2,1)S(1)} fusion(bf16[6,96,512]{2,1,0:T(8,128)(2,1)} %get-tuple-element.16, s32[]{:T(128)S(6)} %select_n.23), kind=kLoop, calls=%fused_computation.3 | loop fusion | bytes 786436 | tf_op jit(solution)/shard_map/dynamic_slice | solution.py:518
  31.1 1.5 %collective-permute-start.4 = (bf16[6,64,512]{2,1,0:T(8,128)(2,1)S(1)}, bf16[6,64,512]{2,1,0:T(8,128)(2,1)S(1)}, u32[]{:S(2)}, u32[]{:S(2)}) collective-permute-start(bf16[6,64,512]{2,1,0:T(8,128)(2,1)S(1)} %constant_dynamic-slice_fusion.1), channel_id=1, source_target_pairs={{0,1},{1,0},{2,3},{3,2},{4,5},{5,4},{6,7},{7,6},{8,9},{9,8},{10,11... | collective-permute-start | bytes 1179656 | tf_op jit(solution)/shard_map/ppermute | solution.py:487
  32.6 10.5 %cross.3.refs_0_ = f32[32,72,256]{2,1,0:T(8,128)S(1)} custom-call(s32[1]{0:T(128)} %bitcast.win_ref, bf16[12,64,512]{2,1,0:T(8,128)(2,1)S(1)} %bitcast.11, bf16[12,64,256]{2,1,0:T(8,128)(2,1)S(1)} %collective-permute-done.1.second_ref, bf16[12,64,256]{2,1,0:T(8,128)(2,1)S(1)} %collective-permute-done.2.refs_0_), custom_call_target="tpu_custom_call" | custom-call | flops 30000001024 | bytes 3932160 | tf_op jit(solution)/shard_map/cross/pallas_call | solution.py:414
  43.1 0.0 copy-start.1
  43.1 6.2 %collective-permute-done.4.second_ref = bf16[6,64,512]{2,1,0:T(8,128)(2,1)S(1)} collective-permute-done((bf16[6,64,512]{2,1,0:T(8,128)(2,1)S(1)}, bf16[6,64,512]{2,1,0:T(8,128)(2,1)S(1)}, u32[]{:S(2)}, u32[]{:S(2)}) %collective-permute-start.4) | collective-permute-done | bytes 393248 | tf_op jit(solution)/shard_map/ppermute | solution.py:487
  49.3 5.6 %cross.4.refs_0_ = f32[32,72,256]{2,1,0:T(8,128)S(1)} custom-call(s32[1]{0:T(128)} %bitcast.win_ref, bf16[12,32,512]{2,1,0:T(8,128)(2,1)S(1)} %collective-permute-done.first_ref, bf16[6,64,512]{2,1,0:T(8,128)(2,1)S(1)} %collective-permute-done.4.second_ref, f32[32,72,256]{2,1,0:T(8,128)S(1)} %cross.3.refs_0_), custom_call_target="tpu_custom_call" | custom-call | flops 15000000512 | bytes 3145728 | tf_op jit(solution)/shard_map/cross/pallas_call | solution.py:414
  55.0 0.0 copy-start.2
  55.0 0.0 copy-start.3
  55.0 0.0 collective-permute-done.3.second_ref
  55.0 0.0 copy-done.1
  55.0 7.3 %cross.5 = (f32[32,64,256]{2,1,0:T(8,128)}, f32[8,128]{1,0:T(8,128)S(1)}) custom-call(s32[1]{0:T(128)} %bitcast.win_ref, bf16[12,32,512]{2,1,0:T(8,128)(2,1)S(1)} %collective-permute-done.first_ref, bf16[6,64,512]{2,1,0:T(8,128)(2,1)S(1)} %collective-permute-done.3.second_ref, f32[32,72,256]{2,1,0:T(8,128)S(1)} %cross.4.refs_0_, bf16[256,256]{1,0:T(8,128)(2,1)S(1)} %copy-done.1), custom_call_target="tpu_custom_call" | custom-call | flops 15000000512 | bytes 3145728 | tf_op jit(solution)/shard_map/cross/pallas_call | solution.py:414
  62.3 0.0 all-to-all-done.incoming_ref
  62.3 0.0 copy-done.2
  62.4 0.0 copy-done.3
  62.4 0.8 %fold.1 = f32[64,256]{1,0:T(8,128)S(1)} custom-call(s32[1]{0:T(128)} %bitcast.1.chan_ref, bf16[16,96,512]{2,1,0:T(8,128)(2,1)S(1)} %all-to-all-done.incoming_ref, bf16[768,512]{1,0:T(8,128)(2,1)S(1)} %copy-done, s32[8,128]{1,0:T(8,128)S(1)} %bitcast.13, bf16[256,256]{1,0:T(8,128)(2,1)S(1)} %copy-done.1, bf16[256,256]{1,0:T(8,128)(2,1)S(1)} %copy-done.2, ...), custom_call_target="tpu_custom_call" | custom-call | flops 201326592 | bytes 2359296 | tf_op jit(solution)/shard_map/fold/pallas_call | solution.py:467
  63.2 0.6 collective-permute-start.5
  63.8 3.4 %collective-permute-done.5 = f32[32,256]{1,0:T(8,128)S(1)} collective-permute-done((f32[32,256]{1,0:T(8,128)S(1)}, f32[32,256]{1,0:T(8,128)S(1)}, u32[]{:S(2)}, u32[]{:S(2)}) %collective-permute-start.5) | collective-permute-done | bytes 32800 | tf_op jit(solution)/shard_map/ppermute | solution.py:487
  67.2 0.6 dynamic-slice_add_fusion
  (1 shorter events, 0.0 us)
Async XLA Ops:
  9.9 13.4 %copy-start = (bf16[768,512]{1,0:T(8,128)(2,1)S(1)}, bf16[768,512]{1,0:T(8,128)(2,1)}, u32[]{:S(2)}) copy-start(bf16[768,512]{1,0:T(8,128)(2,1)} %get-tuple-element.10.own_ref) | copy-start | bytes 2359300
  9.9 14.2 %collective-permute-start = (bf16[12,32,512]{2,1,0:T(8,128)(2,1)}, bf16[12,32,512]{2,1,0:T(8,128)(2,1)S(1)}, u32[]{:S(2)}, u32[]{:S(2)}) collective-permute-start(bf16[12,32,512]{2,1,0:T(8,128)(2,1)} %get-tuple-element.9), channel_id=1, source_target_pairs={{0,1},{1,0},{2,3},{3,2},{4,5},{5,4},{6,7},{7,6},{8,9},{9,8},{10,11... | collective-permute-start | bytes 1179656 | tf_op jit(solution)/shard_map/ppermute | solution.py:487
  12.9 13.2 %collective-permute-start.1 = (bf16[12,64,256]{2,1,0:T(8,128)(2,1)}, bf16[12,64,256]{2,1,0:T(8,128)(2,1)S(1)}, u32[]{:S(2)}, u32[]{:S(2)}) collective-permute-start(bf16[12,64,256]{2,1,0:T(8,128)(2,1)} %bitcast.16), channel_id=1, source_target_pairs={{2,0},{4,2},{6,4},{8,6},{10,8},{12,10},{14,12},{16,14},{18,16},{20... | collective-permute-start | bytes 1179656 | tf_op jit(solution)/shard_map/ppermute | solution.py:482
  14.2 11.9 %collective-permute-start.2 = (bf16[12,64,256]{2,1,0:T(8,128)(2,1)}, bf16[12,64,256]{2,1,0:T(8,128)(2,1)S(1)}, u32[]{:S(2)}, u32[]{:S(2)}) collective-permute-start(bf16[12,64,256]{2,1,0:T(8,128)(2,1)} %bitcast.15), channel_id=1, source_target_pairs={{2,0},{4,2},{6,4},{8,6},{10,8},{12,10},{14,12},{16,14},{18,16},{20... | collective-permute-start | bytes 1179656 | tf_op jit(solution)/shard_map/ppermute | solution.py:482
  15.5 46.8 %all-to-all-start = ((bf16[16,96,512]{2,1,0:T(8,128)(2,1)}), bf16[16,96,512]{2,1,0:T(8,128)(2,1)S(1)}, u32[]{:S(2)}, u32[]{:S(2)}) async-start(bf16[16,96,512]{2,1,0:T(8,128)(2,1)} %get-tuple-element.14), calls=%async_computation | async-start | bytes 3145728 | tf_op jit(solution)/shard_map/all_to_all | solution.py:509
  29.4 25.6 %collective-permute-start.3 = (bf16[6,64,512]{2,1,0:T(8,128)(2,1)S(1)}, bf16[6,64,512]{2,1,0:T(8,128)(2,1)S(1)}, u32[]{:S(2)}, u32[]{:S(2)}) collective-permute-start(bf16[6,64,512]{2,1,0:T(8,128)(2,1)S(1)} %constant_dynamic-slice_fusion.2), channel_id=1, source_target_pairs={{0,1},{1,0},{2,3},{3,2},{4,5},{5,4},{6,7},{7,6},{8,9},{9,8},{10,11... | collective-permute-start | bytes 1179656 | tf_op jit(solution)/shard_map/ppermute | solution.py:487
  31.1 18.2 %collective-permute-start.4 = (bf16[6,64,512]{2,1,0:T(8,128)(2,1)S(1)}, bf16[6,64,512]{2,1,0:T(8,128)(2,1)S(1)}, u32[]{:S(2)}, u32[]{:S(2)}) collective-permute-start(bf16[6,64,512]{2,1,0:T(8,128)(2,1)S(1)} %constant_dynamic-slice_fusion.1), channel_id=1, source_target_pairs={{0,1},{1,0},{2,3},{3,2},{4,5},{5,4},{6,7},{7,6},{8,9},{9,8},{10,11... | collective-permute-start | bytes 1179656 | tf_op jit(solution)/shard_map/ppermute | solution.py:487
  43.1 11.9 %copy-start.1 = (bf16[256,256]{1,0:T(8,128)(2,1)S(1)}, bf16[256,256]{1,0:T(8,128)(2,1)}, u32[]{:S(2)}) copy-start(bf16[256,256]{1,0:T(8,128)(2,1)} %constant.37.clone.refs_1_.high_ref) | copy-start | bytes 393220
  55.0 7.4 %copy-start.2 = (bf16[256,256]{1,0:T(8,128)(2,1)S(1)}, bf16[256,256]{1,0:T(8,128)(2,1)}, u32[]{:S(2)}) copy-start(bf16[256,256]{1,0:T(8,128)(2,1)} %constant.38.clone.low_ref) | copy-start | bytes 393220
  55.0 7.4 %copy-start.3 = (s32[1024,1]{0,1:T(1,128)S(1)}, s32[1024,1]{0,1:T(1,128)}, u32[]{:S(2)}) copy-start(s32[1024,1]{0,1:T(1,128)} %param.9) | copy-start | bytes 12292
  63.2 4.0 %collective-permute-start.5 = (f32[32,256]{1,0:T(8,128)S(1)}, f32[32,256]{1,0:T(8,128)S(1)}, u32[]{:S(2)}, u32[]{:S(2)}) collective-permute-start(f32[32,256]{1,0:T(8,128)S(1)} %constant_dynamic-slice_fusion), channel_id=1, source_target_pairs={{0,1},{1,0},{2,3},{3,2},{4,5},{5,4},{6,7},{7,6},{8,9},{9,8},{10,11... | collective-permute-start | bytes 98312 | tf_op jit(solution)/shard_map/ppermute | solution.py:487
where the time goes:
time: 68.1 us; the launch traced here: 67.8 us
  Pallas kernels  33.5 us (49%)
  starting transfers between devices  16.2 us (24%)
  waiting for transfers between devices  9.57 us (14%)
  local copies, waits for them, and re-layouts  4.62 us (7%)
  between operations  2.23 us (3%)
  other arithmetic  1.71 us (3%)
    pallas_call x3, Pallas kernels, cross_call(): pl.pallas_call(functools.partial(cross_kernel, last, with_sum, local_wind...  23.4 us
    ppermute x4, waiting for transfers between devices, round_win(): lax.ppermute(block, 'win', [(i, (i + shift) % count) for i in range(count)])  9.56 us
    pallas_call x1, Pallas kernels, spectra_call(): pl.pallas_call(spectra_kernel, in_specs=[smem_spec()] + [anywhere] * 5, o...  9.26 us
    all_to_all x1, starting transfers between devices, local(): lax.all_to_all(outgoing, 'chan', split_axis=0, concat_axis=0, tiled=True)  7.81 us
    ppermute x4, starting transfers between devices, round_win(): lax.ppermute(block, 'win', [(i, (i + shift) % count) for i in range(count)])  5.8 us
    ppermute x2, starting transfers between devices, from_above(): return lax.ppermute(block, 'chan', [(i, i - 1) for i in range(1, count)])  2.57 us
    dynamic_slice x2, local copies, waits for them, and re-layouts, local(): lax.dynamic_slice_in_dim(offered[n * half:(n + 1) * half], start, ch_dev, 1)  2.11 us
  transfers between devices with their start and end apart: 7, of which 2 were waited for; matrix products, arithmetic and copies ran while one was open for 8% of the time, Pallas kernels for 35%

commit v1 on v0

--- a/solution.py
+++ b/solution.py
@@ -138,7 +138,7 @@
 
 
 def spectra_kernel(chan_ref, traces_ref, table_ref, quality_ref, owners_ref, places_ref, *refs):
-    whitened_ref, outgoing_ref, near_ref, far_ref, *shared_ref = refs[:-13]
+    early_ref, late_ref, outgoing_ref, *shared_ref = refs[:-13]
     traces, table, quality, owners, places, band, keep_rows, products, white, sent, selector, sems, out_sems = refs[-13:]
     row_parts, chunks, rows, depth = traces.shape
     ch_dev = quality.shape[1]
@@ -208,12 +208,10 @@
             sent[part, :, 2 * CAP * n : 2 * CAP * (n + 1), :] = chosen.reshape(count, 2 * CAP, chosen.shape[-1])
 
     def leave(part):
-        at = pl.ds(part * rows, rows)
+        late, place = divmod(part, row_parts // 2)
         copies = [
-            (white.at[part, :, pl.ds(0, F)], near_ref.at[at, :]),
-            (white.at[part, :, pl.ds(F, F)], far_ref.at[at, :]),
+            (white.at[part], (early_ref, late_ref)[late].at[pl.ds(place * rows, rows), :]),
             (sent.at[part], outgoing_ref.at[:, pl.ds(part * slots, slots), :]),
-            (white.at[part], whitened_ref.at[at, :]),
         ]
         if shared_ref:
             height = shared_ref[0].shape[1]
@@ -260,10 +258,9 @@
     slots = part // (2 * ch_dev) * 2 * CAP
     anywhere = pl.BlockSpec(memory_space=pl.ANY)
     out_shape = [
-        jax.ShapeDtypeStruct((rows, 2 * F), jnp.bfloat16),
+        jax.ShapeDtypeStruct((rows // 2, 2 * F), jnp.bfloat16),
+        jax.ShapeDtypeStruct((rows // 2, 2 * F), jnp.bfloat16),
         jax.ShapeDtypeStruct((chan_count, row_steps * slots, 2 * F), jnp.bfloat16),
-        jax.ShapeDtypeStruct((rows, F), jnp.bfloat16),
-        jax.ShapeDtypeStruct((rows, F), jnp.bfloat16),
     ]
     if own_count % 16 == 0:
         out_shape.append(jax.ShapeDtypeStruct((rows // ch_dev, own_count, 2 * F), jnp.bfloat16))
@@ -285,7 +282,7 @@
             pltpu.VMEM((row_steps, chan_count, slots, 2 * F), jnp.bfloat16),
             pltpu.VMEM((chan_count * 2 * CAP, 2 * ch_dev), jnp.bfloat16),
             pltpu.SemaphoreType.DMA((row_steps + 1, QUARTERS)),
-            pltpu.SemaphoreType.DMA((row_steps, 4 + part // ch_dev)),
+            pltpu.SemaphoreType.DMA((row_steps, 2 + part // ch_dev)),
         ],
         compiler_params=pltpu.CompilerParams(vmem_limit_bytes=SPECTRA_VMEM_LIMIT),
         cost_estimate=pl.CostEstimate(
@@ -295,33 +292,38 @@
     )(chan, traces, jnp.asarray(forward_table(length)), quality, owners, places)
 
 
-def cross_kernel(last, with_sum, local_windows, skipped, win_ref, first_ref, second_ref, *refs):
+def cross_kernel(last, with_sum, skipped, win_ref, *refs):
     refs = list(refs)
-    far_ref = refs.pop(0) if local_windows else None
+    blocks = [refs.pop(0) for _ in range(2 if with_sum else 4)]
     sum_ref = refs.pop(0) if with_sum else None
     if last:
-        table_ref, out_ref, done_ref, wide, spread, total, lags, sems = refs
-        done_ref[...] = jnp.zeros_like(done_ref)
+        table_ref, out_ref, zero_ref, wide, spread, total, lags, sems = refs
     else:
-        out_ref, wide, spread = refs
-        total = out_ref
+        total, zero_ref, wide, spread = refs
+    zero_ref[0] = 0
     windows, own_count = spread.shape[:2]
     ch_dev = wide.shape[1] // 2
     base = pl.multiple_of(win_ref[0] * own_count, 8)
 
     def widen(w, carry):
-        if local_windows:
-            wide[w, :ch_dev, :] = first_ref[w].astype(jnp.float32)
-            wide[w, ch_dev:, :F] = second_ref[w].astype(jnp.float32)
-            wide[w, ch_dev:, F:] = far_ref[w].astype(jnp.float32)
-        else:
+        if with_sum:
             shared = ch_dev - own_count
-            wide[w, shared:ch_dev, :] = first_ref[skipped + w].astype(jnp.float32)
-            rows = second_ref[w].astype(jnp.float32)
+            wide[w, shared:ch_dev, :] = blocks[0][skipped + w].astype(jnp.float32)
+            rows = blocks[1][w].astype(jnp.float32)
             for tile in range(ch_dev // 8):
                 at = base + 8 * tile
                 at = pl.multiple_of(jnp.where(at < shared, at, at + own_count), 8)
                 wide[w, pl.ds(at, 8), :] = rows[8 * tile : 8 * tile + 8]
+        else:
+            for half in range(2):
+                place = half * (windows // 2) + w
+                wide[place, :ch_dev, :] = blocks[half][w].astype(jnp.float32)
+                wide[place, ch_dev:, :] = blocks[2 + half][w].astype(jnp.float32)
+        return carry
+
+    lax.fori_loop(0, windows if with_sum else windows // 2, widen, 0)
+
+    def repeat(w, carry):
         for tile in range(own_count // 8):
             rows = wide[w, pl.ds(pl.multiple_of(base + 8 * tile, 8), 8), :]
             for i in range(8):
@@ -329,7 +331,7 @@
                     spread[w, 8 * tile + i, q] = jnp.broadcast_to(rows[i : i + 1, q * H : (q + 1) * H], (8, H))
         return carry
 
-    lax.fori_loop(0, windows, widen, 0)
+    lax.fori_loop(0, windows, repeat, 0)
 
     group, tiles = 4, 3
     rounds = SPAN // (8 * tiles)
@@ -386,13 +388,11 @@
             copy.wait()
 
 
-def cross_call(win, first, second, ch_dev, own_count, sums, table, skipped, share):
-    local_windows = len(second) == 2
-    windows, _, columns = second[0].shape
-    columns = first.shape[2]
+def cross_call(win, blocks, windows, ch_dev, own_count, sums, table, skipped, share):
+    columns = 2 * F
     last = table is not None
     with_sum = sums is not None
-    operands = [win, first, *second]
+    operands = [win, *blocks]
     if with_sum:
         operands.append(sums)
     scratch = [
@@ -407,12 +407,10 @@
             pltpu.SemaphoreType.DMA((own_count // 8,)),
         ]
     shape = (own_count, REACH, NLAG) if last else (own_count, SPAN, F)
-    out_shape, out_specs = [jax.ShapeDtypeStruct(shape, jnp.float32)], [vmem_spec()]
-    if last:
-        out_shape.append(jax.ShapeDtypeStruct((8, H), jnp.float32))
-        out_specs = [pl.BlockSpec(memory_space=pl.ANY), vmem_spec()]
+    out_shape = [jax.ShapeDtypeStruct(shape, jnp.float32), jax.ShapeDtypeStruct((1,), jnp.int32)]
+    out_specs = [pl.BlockSpec(memory_space=pl.ANY) if last else vmem_spec(), smem_spec()]
     return pl.pallas_call(
-        functools.partial(cross_kernel, last, with_sum, local_windows, skipped),
+        functools.partial(cross_kernel, last, with_sum, skipped),
         in_specs=[smem_spec()] + [vmem_spec()] * (len(operands) - 1),
         out_specs=out_specs,
         out_shape=out_shape,
@@ -425,10 +423,10 @@
     )(*operands)
 
 
-def fold_kernel(chan_ref, incoming_ref, own_ref, owners_ref, high_ref, low_ref, earlier_ref, out_ref):
+def fold_kernel(chan_ref, incoming_ref, early_ref, late_ref, owners_ref, high_ref, low_ref, earlier_ref, out_ref):
     ch_dev = out_ref.shape[0]
     rows = 2 * ch_dev
-    pairs = own_ref.shape[0] // rows
+    pairs = 2 * early_ref.shape[0] // rows
     count, slots, columns = incoming_ref.shape
     owners = owners_ref[...].astype(jnp.float32)
     per_row = owners.shape[1] // ch_dev
@@ -450,7 +448,8 @@
     for n in range(pairs):
         arrived = incoming_ref[:, 2 * CAP * n : 2 * CAP * (n + 1), :].reshape(count * 2 * CAP, columns)
         right = jnp.dot(picker, arrived, preferred_element_type=jnp.float32)
-        left = own_ref[rows * n : rows * (n + 1), :].astype(jnp.float32)
+        late, place = divmod(n, pairs // 2)
+        left = (early_ref, late_ref)[late][rows * place : rows * (place + 1), :].astype(jnp.float32)
         l = [left[:, q * H : (q + 1) * H] for q in range(4)]
         r = [right[:, q * H : (q + 1) * H] for q in range(4)]
         terms = [
@@ -463,18 +462,18 @@
     out_ref[...] = lag_transform(stacks, high_ref[...], low_ref[...])
 
 
-def fold_call(chan, incoming, own, owners, ch_dev, tables, earlier):
+def fold_call(chan, incoming, early, late, owners, ch_dev, tables, earlier):
     return pl.pallas_call(
         fold_kernel,
-        in_specs=[smem_spec()] + [vmem_spec()] * 5 + [pl.BlockSpec(memory_space=pl.ANY)],
+        in_specs=[smem_spec()] + [vmem_spec()] * 6 + [smem_spec()],
         out_specs=vmem_spec(),
         out_shape=jax.ShapeDtypeStruct((ch_dev, NLAG), jnp.float32),
         compiler_params=pltpu.CompilerParams(vmem_limit_bytes=FOLD_VMEM_LIMIT),
         cost_estimate=pl.CostEstimate(
-            flops=4 * ch_dev * incoming.size, bytes_accessed=2 * (incoming.size + own.size), transcendentals=0
+            flops=4 * ch_dev * incoming.size, bytes_accessed=2 * (incoming.size + 2 * early.size), transcendentals=0
         ),
         name="fold",
-    )(chan, incoming, own, owners, *tables, earlier)
+    )(chan, incoming, early, late, owners, *tables, earlier)
 
 
 def from_above(block):
@@ -499,33 +498,34 @@
     tables = [jnp.asarray(t) for t in inverse_tables(1.0 / math.sqrt(F * win_dev * win_count))]
     owners = fold_block.reshape(-1, 2 * ch_dev)
     places = fold_offset.reshape(-1, 2 * ch_dev)
-    flat, outgoing, near, far, *ready = spectra_call(
+    early, late, outgoing, *ready = spectra_call(
         chan, traces.reshape(win_dev * ch_dev, length), quality.reshape(1, ch_dev), owners, places, chan_count, own_count
     )
-    whitened = flat.reshape(win_dev, ch_dev, 2 * F)
-    upper = [from_above(half.reshape(win_dev, ch_dev, F)) for half in (near, far)]
-    ready = ready[0] if ready else whitened[:, shared:]
+    half = win_dev // 2
+    halves = [rows.reshape(half, ch_dev, 2 * F) for rows in (early, late)]
+    ready = ready[0] if ready else jnp.concatenate([block[:, shared:] for block in halves], axis=0)
+    upper = [from_above(block) for block in halves]
     common = [round_win(ready, shift) for shift in range(1, win_count)]
     incoming = lax.all_to_all(outgoing, "chan", split_axis=0, concat_axis=0, tiled=True)
-    offered = jnp.concatenate([whitened[:, :shared], jnp.concatenate(upper, axis=2)], axis=1)
-    half = win_dev // 2
-    special = []
-    for shift, rows in enumerate(common, 1):
-        target = (window_part + shift) % win_count * own_count
-        mark = rows[0, 0, 0]
-        starts = (target, target + (mark != mark).astype(jnp.int32))
-        special.append([
-            round_win(lax.dynamic_slice_in_dim(offered[n * half : (n + 1) * half], start, ch_dev, 1), shift)
-            for n, start in enumerate(starts)
-        ])
-    arrived = [(whitened, upper, 0, 1.0)]
-    for rows, others in zip(common, special):
-        arrived += [(rows, [part], n * half, 0.5) for n, part in enumerate(others)]
-    sums = None
-    for n, (first, second, skipped, part) in enumerate(arrived):
+    targets = [(window_part + shift) % win_count * own_count for shift in range(1, win_count)]
+
+    def offer(part, start):
+        rows = jnp.concatenate([halves[part][:, :shared], upper[part]], axis=1)
+        return [
+            round_win(lax.dynamic_slice_in_dim(rows, target + start, ch_dev, 1), shift)
+            for shift, target in enumerate(targets, 1)
+        ]
+
+    sooner = offer(0, 0)
+    sums, zero = cross_call(win, halves + upper, win_dev, ch_dev, own_count, None, None, 0, 1.0)
+    later = offer(1, zero[0])
+    arrived = []
+    for rows, *others in zip(common, sooner, later):
+        arrived += [([rows, block], n * half) for n, block in enumerate(others)]
+    for n, (blocks, skipped) in enumerate(arrived):
         ends = tables[0] if n == len(arrived) - 1 else None
-        sums, *done = cross_call(win, first, second, ch_dev, own_count, sums, ends, skipped, part)
-    share = fold_call(chan, incoming, flat, owners, ch_dev, tables, done[0])
+        sums, done = cross_call(win, blocks, half, ch_dev, own_count, sums, ends, skipped, 0.5)
+    share = fold_call(chan, incoming, early, late, owners, ch_dev, tables, done)
     fold = lax.dynamic_slice_in_dim(share, window_part * own_count, own_count, 0)
     for shift in range(1, win_count):
         target = (window_part + shift) % win_count * own_count

time: 68.1 us -> 65.4 us (0.960)
  waiting for transfers between devices: 9.57 us -> 2.88 us
  Pallas kernels: 33.5 us -> 36.5 us
  starting transfers between devices: 16.2 us -> 18.1 us
  between operations: 2.23 us -> 1.42 us
    ppermute x4, waiting for transfers between devices: 9.56 us -> 2.87 us  [round_win(): lax.ppermute(block, 'win', [(i, (i + shift) % count) for i in range(count)])]
    pallas_call x4, Pallas kernels: 24.2 us -> 27.4 us  [the longest x3 26.1 us: cross_call(): pl.pallas_call(functools.partial(cross_kernel, last, with_sum, skipped),...]
    unnamed x8 -> x14, local copies, waits for them, and re-layouts: 0.03 us -> 3.11 us
    dynamic_slice x2 -> x0, local copies, waits for them, and re-layouts: 2.11 us -> none  [local(): lax.dynamic_slice_in_dim(offered[n * half:(n + 1) * half], start, ch_dev, 1)]
    all_to_all x1, starting transfers between devices: 7.81 us -> 9.26 us  [local(): lax.all_to_all(outgoing, 'chan', split_axis=0, concat_axis=0, tiled=True)]
    slice x3 -> x2, local copies, waits for them, and re-layouts: 2.47 us -> 1.4 us  [offer(): rows = jnp.concatenate([halves[part][:, :shared], upper[part]], axis=1)]
  transfers between devices with their start and end apart: 7 -> 7, of which waited for: 2 -> 3; matrix products, arithmetic and copies ran while one was open for 8% -> 4% of each run, Pallas kernels for 35% -> 40%
where the time goes in v1:
time: 65.4 us; the launch traced here: 65.1 us
  Pallas kernels  36.5 us (56%)
  starting transfers between devices  18.1 us (28%)
  local copies, waits for them, and re-layouts  4.52 us (7%)
  waiting for transfers between devices  2.88 us (4%)
  other arithmetic  1.64 us (3%)
  between operations  1.42 us (2%)
    pallas_call x3, Pallas kernels, cross_call(): pl.pallas_call(functools.partial(cross_kernel, last, with_sum, skipped),...  26.1 us
    all_to_all x1, starting transfers between devices, local(): lax.all_to_all(outgoing, 'chan', split_axis=0, concat_axis=0, tiled=True)  9.26 us
    pallas_call x1, Pallas kernels, spectra_call(): pl.pallas_call(spectra_kernel, in_specs=[smem_spec()] + [anywhere] * 5, o...  9.13 us
    ppermute x4, starting transfers between devices, round_win(): lax.ppermute(block, 'win', [(i, (i + shift) % count) for i in range(count)])  6.11 us
    unnamed x14, local copies, waits for them, and re-layouts  3.11 us
    ppermute x4, waiting for transfers between devices, round_win(): lax.ppermute(block, 'win', [(i, (i + shift) % count) for i in range(count)])  2.87 us
    ppermute x2, starting transfers between devices, from_above(): return lax.ppermute(block, 'chan', [(i, i - 1) for i in range(1, count)])  2.72 us
    slice x2, local copies, waits for them, and re-layouts, offer(): rows = jnp.concatenate([halves[part][:, :shared], upper[part]], axis=1)  1.4 us
  transfers between devices with their start and end apart: 7, of which 3 were waited for; matrix products, arithmetic and copies ran while one was open for 4% of the time, Pallas kernels for 40%

profile of v1, /device:TPU:0, one launch (start us, length us, event | category | flops | bytes accessed | tf_op | source)
XLA Modules:
  0.0 65.1 jit_solution(17883192138438560361)
XLA Ops:
  0.6 9.1 %spectra.1 = (bf16[384,512]{1,0:T(8,128)(2,1)}, bf16[384,512]{1,0:T(8,128)(2,1)}, bf16[16,96,512]{2,1,0:T(8,128)(2,1)}, bf16[12,32,512]{2,1,0:T(8,128)(2,1)}) custom-call(s32[1]{0:T(128)} %bitcast.1.chan_ref, bf16[768,4096]{1,0:T(8,128)(2,1)} %bitcast.17, bf16[1024,512]{1,0:T(8,128)(2,1)} %constant.39.clone.table_ref, s32[1,64]{1,0:T(1,128)} %bitcast.19, ...), custom_call_target="tpu_custom_call" | custom-call | flops 3221225472 | bytes 6291456 | tf_op jit(solution)/shard_map/spectra/pallas_call | solution.py:267
  9.8 0.0 copy-start.1
  9.8 0.0 copy-start
  9.8 1.4 %collective-permute-start.2 = (bf16[6,64,512]{2,1,0:T(8,128)(2,1)}, bf16[6,64,512]{2,1,0:T(8,128)(2,1)S(1)}, u32[]{:S(2)}, u32[]{:S(2)}) collective-permute-start(bf16[6,64,512]{2,1,0:T(8,128)(2,1)} %bitcast.9), channel_id=1, source_target_pairs={{2,0},{4,2},{6,4},{8,6},{10,8},{12,10},{14,12},{16,14},{18,16},{20... | collective-permute-start | bytes 1179656 | tf_op jit(solution)/shard_map/ppermute | solution.py:481
  11.2 1.3 %collective-permute-start.1 = (bf16[6,64,512]{2,1,0:T(8,128)(2,1)}, bf16[6,64,512]{2,1,0:T(8,128)(2,1)S(1)}, u32[]{:S(2)}, u32[]{:S(2)}) collective-permute-start(bf16[6,64,512]{2,1,0:T(8,128)(2,1)} %bitcast.12), channel_id=1, source_target_pairs={{2,0},{4,2},{6,4},{8,6},{10,8},{12,10},{14,12},{16,14},{18,16},{20... | collective-permute-start | bytes 1179656 | tf_op jit(solution)/shard_map/ppermute | solution.py:481
  12.5 9.3 %all-to-all-start = ((bf16[16,96,512]{2,1,0:T(8,128)(2,1)}), bf16[16,96,512]{2,1,0:T(8,128)(2,1)S(1)}, u32[]{:S(2)}, u32[]{:S(2)}) async-start(bf16[16,96,512]{2,1,0:T(8,128)(2,1)} %get-tuple-element.18), calls=%async_computation | async-start | bytes 3145728 | tf_op jit(solution)/shard_map/all_to_all | solution.py:509
  21.8 1.5 %collective-permute-start = (bf16[12,32,512]{2,1,0:T(8,128)(2,1)}, bf16[12,32,512]{2,1,0:T(8,128)(2,1)S(1)}, u32[]{:S(2)}, u32[]{:S(2)}) collective-permute-start(bf16[12,32,512]{2,1,0:T(8,128)(2,1)} %get-tuple-element.11), channel_id=1, source_target_pairs={{0,1},{1,0},{2,3},{3,2},{4,5},{5,4},{6,7},{7,6},{8,9},{9,8},{10,11... | collective-permute-start | bytes 1179656 | tf_op jit(solution)/shard_map/ppermute | solution.py:486
  23.3 0.0 copy-done.1
  23.3 0.7 %slice.8 = bf16[6,32,512]{2,1,0:T(8,128)(2,1)} slice(bf16[6,64,512]{2,1,0:T(8,128)(2,1)S(1)} %bitcast.13), slice={[0:6], [0:32], [0:512]} | slice | bytes 393216 | tf_op jit(solution)/shard_map/slice | solution.py:513
  24.0 0.0 copy-done
  24.0 0.7 %slice.9 = bf16[6,32,512]{2,1,0:T(8,128)(2,1)} slice(bf16[6,64,512]{2,1,0:T(8,128)(2,1)S(1)} %bitcast.10), slice={[0:6], [0:32], [0:512]} | slice | bytes 393216 | tf_op jit(solution)/shard_map/slice | solution.py:513
  24.7 0.0 collective-permute-done.2.refs_2_
  24.8 0.8 %fusion = bf16[6,64,512]{2,1,0:T(8,128)(2,1)} fusion(s32[]{:T(128)S(6)} %select_n.23, bf16[6,32,512]{2,1,0:T(8,128)(2,1)} %slice.9, bf16[6,64,512]{2,1,0:T(8,128)(2,1)S(1)} %collective-permute-done.2.refs_2_), kind=kLoop, calls=%fused_computation.4 | loop fusion | flops 786432 | bytes 983044 | tf_op jit(solution)/shard_map/concatenate | solution.py:513
  25.6 1.5 %collective-permute-start.4 = (bf16[6,64,512]{2,1,0:T(8,128)(2,1)}, bf16[6,64,512]{2,1,0:T(8,128)(2,1)}, u32[]{:S(2)}, u32[]{:S(2)}) collective-permute-start(bf16[6,64,512]{2,1,0:T(8,128)(2,1)} %fusion), channel_id=1, source_target_pairs={{0,1},{1,0},{2,3},{3,2},{4,5},{5,4},{6,7},{7,6},{8,9},{9,8},{10,11... | collective-permute-start | bytes 1179656 | tf_op jit(solution)/shard_map/ppermute | solution.py:486
  27.1 0.0 collective-permute-done.1.refs_3_
  27.1 11.0 %cross.3 = (f32[32,72,256]{2,1,0:T(8,128)S(1)}, s32[1]{0:T(128)}) custom-call(s32[1]{0:T(128)} %bitcast.win_ref, bf16[6,64,512]{2,1,0:T(8,128)(2,1)S(1)} %bitcast.11, bf16[6,64,512]{2,1,0:T(8,128)(2,1)S(1)} %bitcast.14, bf16[6,64,512]{2,1,0:T(8,128)(2,1)S(1)} %collective-permute-done.2.refs_2_, bf16[6,64,512]{2,1,0:T(8,128)(2,1)S(1)} %collective-permute-done.1.refs_3_), custom_call_target="tpu_custom_call" | custom-call | flops 30000001024 | bytes 3932160 | tf_op jit(solution)/shard_map/cross/pallas_call | solution.py:412
  38.1 0.0 copy-start.5
  38.1 1.4 %copy-done.5 = f32[32,72,256]{2,1,0:T(8,128)} copy-done((f32[32,72,256]{2,1,0:T(8,128)}, f32[32,72,256]{2,1,0:T(8,128)S(1)}, u32[]{:S(2)}) %copy-start.5) | copy-done | bytes 2359320
  40.1 0.2 fusion.1
  40.3 1.5 %collective-permute-start.3 = (bf16[6,64,512]{2,1,0:T(8,128)(2,1)S(1)}, bf16[6,64,512]{2,1,0:T(8,128)(2,1)S(1)}, u32[]{:S(2)}, u32[]{:S(2)}) collective-permute-start(bf16[6,64,512]{2,1,0:T(8,128)(2,1)S(1)} %fusion.1), channel_id=1, source_target_pairs={{0,1},{1,0},{2,3},{3,2},{4,5},{5,4},{6,7},{7,6},{8,9},{9,8},{10,11... | collective-permute-start | bytes 1179656 | tf_op jit(solution)/shard_map/ppermute | solution.py:486
  41.9 0.0 collective-permute-done.refs_0_
  41.9 0.1 collective-permute-done.4.refs_1_
  42.0 0.0 copy-start.6
  42.0 1.7 %copy-done.6 = f32[32,72,256]{2,1,0:T(8,128)S(1)} copy-done((f32[32,72,256]{2,1,0:T(8,128)S(1)}, f32[32,72,256]{2,1,0:T(8,128)}, u32[]{:S(2)}) %copy-start.6) | copy-done | bytes 2359320
  43.6 0.0 copy-start.2
  43.6 7.2 %cross.4 = (f32[32,72,256]{2,1,0:T(8,128)S(1)}, s32[1]{0:T(128)}) custom-call(s32[1]{0:T(128)} %bitcast.win_ref, bf16[12,32,512]{2,1,0:T(8,128)(2,1)S(1)} %collective-permute-done.refs_0_, bf16[6,64,512]{2,1,0:T(8,128)(2,1)} %collective-permute-done.4.refs_1_, f32[32,72,256]{2,1,0:T(8,128)S(1)} %copy-done.6), custom_call_target="tpu_custom_call" | custom-call | flops 15000000512 | bytes 3145728 | tf_op jit(solution)/shard_map/cross/pallas_call | solution.py:412
  50.8 0.4 collective-permute-done.3.refs_1_
  51.2 0.0 copy-done.2
  51.2 0.0 copy-start.3
  51.2 0.0 copy-start.4
  51.2 7.8 %cross.5 = (f32[32,64,256]{2,1,0:T(8,128)}, s32[1]{0:T(128)}) custom-call(s32[1]{0:T(128)} %bitcast.win_ref, bf16[12,32,512]{2,1,0:T(8,128)(2,1)S(1)} %collective-permute-done.refs_0_, bf16[6,64,512]{2,1,0:T(8,128)(2,1)S(1)} %collective-permute-done.3.refs_1_, f32[32,72,256]{2,1,0:T(8,128)S(1)} %get-tuple-element.16.refs_2_, bf16[256,256]{1,0:T(8,128)(2,1)S(1)} %copy-done.2), custom_call_target="tpu_custom_call" | custom-call | flops 15000000512 | bytes 3145728 | tf_op jit(solution)/shard_map/cross/pallas_call | solution.py:412
  59.1 0.0 all-to-all-done.incoming_ref
  59.1 0.0 copy-done.3
  59.1 0.0 copy-done.4
  59.1 1.4 %fold.1 = f32[64,256]{1,0:T(8,128)S(1)} custom-call(s32[1]{0:T(128)} %bitcast.1.chan_ref, bf16[16,96,512]{2,1,0:T(8,128)(2,1)S(1)} %all-to-all-done.incoming_ref, bf16[384,512]{1,0:T(8,128)(2,1)S(1)} %copy-done, bf16[384,512]{1,0:T(8,128)(2,1)S(1)} %copy-done.1, s32[8,128]{1,0:T(8,128)S(1)} %bitcast.16, bf16[256,256]{1,0:T(8,128)(2,1)S(1)} %copy-done.2, ...), custom_call_target="tpu_custom_call" | custom-call | flops 201326592 | bytes 2359296 | tf_op jit(solution)/shard_map/fold/pallas_call | solution.py:466
  60.5 1.5 %collective-permute-start.5 = (f32[32,256]{1,0:T(8,128)S(1)}, f32[32,256]{1,0:T(8,128)S(1)}, u32[]{:S(2)}, u32[]{:S(2)}) collective-permute-start(f32[32,256]{1,0:T(8,128)S(1)} %constant_dynamic-slice_fusion), channel_id=1, source_target_pairs={{0,1},{1,0},{2,3},{3,2},{4,5},{5,4},{6,7},{7,6},{8,9},{9,8},{10,11... | collective-permute-start | bytes 98312 | tf_op jit(solution)/shard_map/ppermute | solution.py:486
  62.0 2.4 %collective-permute-done.5 = f32[32,256]{1,0:T(8,128)S(1)} collective-permute-done((f32[32,256]{1,0:T(8,128)S(1)}, f32[32,256]{1,0:T(8,128)S(1)}, u32[]{:S(2)}, u32[]{:S(2)}) %collective-permute-start.5) | collective-permute-done | bytes 32800 | tf_op jit(solution)/shard_map/ppermute | solution.py:486
  64.5 0.6 dynamic-slice_add_fusion
  (1 shorter events, 0.0 us)
Async XLA Ops:
  9.8 13.6 %copy-start.1 = (bf16[384,512]{1,0:T(8,128)(2,1)S(1)}, bf16[384,512]{1,0:T(8,128)(2,1)}, u32[]{:S(2)}) copy-start(bf16[384,512]{1,0:T(8,128)(2,1)} %get-tuple-element.12.late_ref) | copy-start | bytes 1179652
  9.8 14.3 %copy-start = (bf16[384,512]{1,0:T(8,128)(2,1)S(1)}, bf16[384,512]{1,0:T(8,128)(2,1)}, u32[]{:S(2)}) copy-start(bf16[384,512]{1,0:T(8,128)(2,1)} %get-tuple-element.13.early_ref) | copy-start | bytes 1179652
  9.8 15.0 %collective-permute-start.2 = (bf16[6,64,512]{2,1,0:T(8,128)(2,1)}, bf16[6,64,512]{2,1,0:T(8,128)(2,1)S(1)}, u32[]{:S(2)}, u32[]{:S(2)}) collective-permute-start(bf16[6,64,512]{2,1,0:T(8,128)(2,1)} %bitcast.9), channel_id=1, source_target_pairs={{2,0},{4,2},{6,4},{8,6},{10,8},{12,10},{14,12},{16,14},{18,16},{20... | collective-permute-start | bytes 1179656 | tf_op jit(solution)/shard_map/ppermute | solution.py:481
  11.2 15.8 %collective-permute-start.1 = (bf16[6,64,512]{2,1,0:T(8,128)(2,1)}, bf16[6,64,512]{2,1,0:T(8,128)(2,1)S(1)}, u32[]{:S(2)}, u32[]{:S(2)}) collective-permute-start(bf16[6,64,512]{2,1,0:T(8,128)(2,1)} %bitcast.12), channel_id=1, source_target_pairs={{2,0},{4,2},{6,4},{8,6},{10,8},{12,10},{14,12},{16,14},{18,16},{20... | collective-permute-start | bytes 1179656 | tf_op jit(solution)/shard_map/ppermute | solution.py:481
  12.5 46.6 %all-to-all-start = ((bf16[16,96,512]{2,1,0:T(8,128)(2,1)}), bf16[16,96,512]{2,1,0:T(8,128)(2,1)S(1)}, u32[]{:S(2)}, u32[]{:S(2)}) async-start(bf16[16,96,512]{2,1,0:T(8,128)(2,1)} %get-tuple-element.18), calls=%async_computation | async-start | bytes 3145728 | tf_op jit(solution)/shard_map/all_to_all | solution.py:509
  21.8 20.1 %collective-permute-start = (bf16[12,32,512]{2,1,0:T(8,128)(2,1)}, bf16[12,32,512]{2,1,0:T(8,128)(2,1)S(1)}, u32[]{:S(2)}, u32[]{:S(2)}) collective-permute-start(bf16[12,32,512]{2,1,0:T(8,128)(2,1)} %get-tuple-element.11), channel_id=1, source_target_pairs={{0,1},{1,0},{2,3},{3,2},{4,5},{5,4},{6,7},{7,6},{8,9},{9,8},{10,11... | collective-permute-start | bytes 1179656 | tf_op jit(solution)/shard_map/ppermute | solution.py:486
  25.6 16.4 %collective-permute-start.4 = (bf16[6,64,512]{2,1,0:T(8,128)(2,1)}, bf16[6,64,512]{2,1,0:T(8,128)(2,1)}, u32[]{:S(2)}, u32[]{:S(2)}) collective-permute-start(bf16[6,64,512]{2,1,0:T(8,128)(2,1)} %fusion), channel_id=1, source_target_pairs={{0,1},{1,0},{2,3},{3,2},{4,5},{5,4},{6,7},{7,6},{8,9},{9,8},{10,11... | collective-permute-start | bytes 1179656 | tf_op jit(solution)/shard_map/ppermute | solution.py:486
  38.1 1.4 %copy-start.5 = (f32[32,72,256]{2,1,0:T(8,128)}, f32[32,72,256]{2,1,0:T(8,128)S(1)}, u32[]{:S(2)}) copy-start(f32[32,72,256]{2,1,0:T(8,128)S(1)} %get-tuple-element.15.refs_2_) | copy-start | bytes 7077892
  40.3 10.9 %collective-permute-start.3 = (bf16[6,64,512]{2,1,0:T(8,128)(2,1)S(1)}, bf16[6,64,512]{2,1,0:T(8,128)(2,1)S(1)}, u32[]{:S(2)}, u32[]{:S(2)}) collective-permute-start(bf16[6,64,512]{2,1,0:T(8,128)(2,1)S(1)} %fusion.1), channel_id=1, source_target_pairs={{0,1},{1,0},{2,3},{3,2},{4,5},{5,4},{6,7},{7,6},{8,9},{9,8},{10,11... | collective-permute-start | bytes 1179656 | tf_op jit(solution)/shard_map/ppermute | solution.py:486
  42.0 1.7 %copy-start.6 = (f32[32,72,256]{2,1,0:T(8,128)S(1)}, f32[32,72,256]{2,1,0:T(8,128)}, u32[]{:S(2)}) copy-start(f32[32,72,256]{2,1,0:T(8,128)} %copy-done.5) | copy-start | bytes 7077892
  43.6 7.6 %copy-start.2 = (bf16[256,256]{1,0:T(8,128)(2,1)S(1)}, bf16[256,256]{1,0:T(8,128)(2,1)}, u32[]{:S(2)}) copy-start(bf16[256,256]{1,0:T(8,128)(2,1)} %constant.37.clone.refs_3_.high_ref) | copy-start | bytes 393220
  51.2 7.9 %copy-start.3 = (bf16[256,256]{1,0:T(8,128)(2,1)S(1)}, bf16[256,256]{1,0:T(8,128)(2,1)}, u32[]{:S(2)}) copy-start(bf16[256,256]{1,0:T(8,128)(2,1)} %constant.38.clone.low_ref) | copy-start | bytes 393220
  51.2 7.9 %copy-start.4 = (s32[1024,1]{0,1:T(1,128)S(1)}, s32[1024,1]{0,1:T(1,128)}, u32[]{:S(2)}) copy-start(s32[1024,1]{0,1:T(1,128)} %param.9) | copy-start | bytes 12292
  60.5 4.0 %collective-permute-start.5 = (f32[32,256]{1,0:T(8,128)S(1)}, f32[32,256]{1,0:T(8,128)S(1)}, u32[]{:S(2)}, u32[]{:S(2)}) collective-permute-start(f32[32,256]{1,0:T(8,128)S(1)} %constant_dynamic-slice_fusion), channel_id=1, source_target_pairs={{0,1},{1,0},{2,3},{3,2},{4,5},{5,4},{6,7},{7,6},{8,9},{9,8},{10,11... | collective-permute-start | bytes 98312 | tf_op jit(solution)/shard_map/ppermute | solution.py:486

commit v2 on v1

--- a/solution.py
+++ b/solution.py
@@ -138,7 +138,7 @@
 
 
 def spectra_kernel(chan_ref, traces_ref, table_ref, quality_ref, owners_ref, places_ref, *refs):
-    early_ref, late_ref, outgoing_ref, *shared_ref = refs[:-13]
+    early_ref, late_ref, outgoing_ref, *row_refs = refs[:-13]
     traces, table, quality, owners, places, band, keep_rows, products, white, sent, selector, sems, out_sems = refs[-13:]
     row_parts, chunks, rows, depth = traces.shape
     ch_dev = quality.shape[1]
@@ -213,15 +213,22 @@
             (white.at[part], (early_ref, late_ref)[late].at[pl.ds(place * rows, rows), :]),
             (sent.at[part], outgoing_ref.at[:, pl.ds(part * slots, slots), :]),
         ]
-        if shared_ref:
-            height = shared_ref[0].shape[1]
+        if row_refs:
+            shared_ref, *lower_refs = row_refs
+            height = shared_ref.shape[1]
+            split = ch_dev - height
             for w in range(rows // ch_dev):
-                copies.append(
+                first = w * ch_dev
+                copies += [
                     (
-                        white.at[part, pl.ds((w + 1) * ch_dev - height, height), :],
-                        shared_ref[0].at[part * (rows // ch_dev) + w],
-                    )
-                )
+                        white.at[part, pl.ds(first + split, height), :],
+                        shared_ref.at[part * (rows // ch_dev) + w],
+                    ),
+                    (
+                        white.at[part, pl.ds(first, split), :],
+                        lower_refs[late].at[place * (rows // ch_dev) + w],
+                    ),
+                ]
         for n, (source, target) in enumerate(copies):
             leaving.append(pltpu.make_async_copy(source, target, out_sems.at[part, n]))
             leaving[-1].start()
@@ -263,7 +270,12 @@
         jax.ShapeDtypeStruct((chan_count, row_steps * slots, 2 * F), jnp.bfloat16),
     ]
     if own_count % 16 == 0:
-        out_shape.append(jax.ShapeDtypeStruct((rows // ch_dev, own_count, 2 * F), jnp.bfloat16))
+        windows, lower = rows // ch_dev, ch_dev - own_count
+        out_shape += [
+            jax.ShapeDtypeStruct((windows, own_count, 2 * F), jnp.bfloat16),
+            jax.ShapeDtypeStruct((windows // 2, lower, 2 * F), jnp.bfloat16),
+            jax.ShapeDtypeStruct((windows // 2, lower, 2 * F), jnp.bfloat16),
+        ]
     return pl.pallas_call(
         spectra_kernel,
         in_specs=[smem_spec()] + [anywhere] * 5,
@@ -282,7 +294,7 @@
             pltpu.VMEM((row_steps, chan_count, slots, 2 * F), jnp.bfloat16),
             pltpu.VMEM((chan_count * 2 * CAP, 2 * ch_dev), jnp.bfloat16),
             pltpu.SemaphoreType.DMA((row_steps + 1, QUARTERS)),
-            pltpu.SemaphoreType.DMA((row_steps, 2 + part // ch_dev)),
+            pltpu.SemaphoreType.DMA((row_steps, 2 + 2 * (part // ch_dev))),
         ],
         compiler_params=pltpu.CompilerParams(vmem_limit_bytes=SPECTRA_VMEM_LIMIT),
         cost_estimate=pl.CostEstimate(
@@ -292,14 +304,16 @@
     )(chan, traces, jnp.asarray(forward_table(length)), quality, owners, places)
 
 
-def cross_kernel(last, with_sum, skipped, win_ref, *refs):
+def cross_kernel(last, with_sum, skipped, through, win_ref, *refs):
     refs = list(refs)
     blocks = [refs.pop(0) for _ in range(2 if with_sum else 4)]
+    refs = refs[through:]
     sum_ref = refs.pop(0) if with_sum else None
     if last:
         table_ref, out_ref, zero_ref, wide, spread, total, lags, sems = refs
     else:
-        total, zero_ref, wide, spread = refs
+        total, zero_ref, *refs = refs
+        wide, spread = refs[through:]
     zero_ref[0] = 0
     windows, own_count = spread.shape[:2]
     ch_dev = wide.shape[1] // 2
@@ -388,11 +402,13 @@
             copy.wait()
 
 
-def cross_call(win, blocks, windows, ch_dev, own_count, sums, table, skipped, share):
+def cross_call(win, blocks, windows, ch_dev, own_count, sums, table, skipped, share, through=()):
     columns = 2 * F
     last = table is not None
     with_sum = sums is not None
-    operands = [win, *blocks]
+    operands = [win, *blocks, *through]
+    anywhere = [pl.BlockSpec(memory_space=pl.ANY)] * len(through)
+    in_specs = [smem_spec()] + [vmem_spec()] * len(blocks) + anywhere
     if with_sum:
         operands.append(sums)
     scratch = [
@@ -408,10 +424,12 @@
         ]
     shape = (own_count, REACH, NLAG) if last else (own_count, SPAN, F)
     out_shape = [jax.ShapeDtypeStruct(shape, jnp.float32), jax.ShapeDtypeStruct((1,), jnp.int32)]
-    out_specs = [pl.BlockSpec(memory_space=pl.ANY) if last else vmem_spec(), smem_spec()]
+    out_specs = [pl.BlockSpec(memory_space=pl.ANY) if last else vmem_spec(), smem_spec()] + anywhere
+    out_shape += [jax.ShapeDtypeStruct(array.shape, array.dtype) for array in through]
     return pl.pallas_call(
-        functools.partial(cross_kernel, last, with_sum, skipped),
-        in_specs=[smem_spec()] + [vmem_spec()] * (len(operands) - 1),
+        functools.partial(cross_kernel, last, with_sum, skipped, len(through)),
+        in_specs=in_specs + [vmem_spec()] * (len(operands) - len(in_specs)),
+        input_output_aliases={1 + len(blocks) + n: 2 + n for n in range(len(through))},
         out_specs=out_specs,
         out_shape=out_shape,
         scratch_shapes=scratch,
@@ -498,27 +516,31 @@
     tables = [jnp.asarray(t) for t in inverse_tables(1.0 / math.sqrt(F * win_dev * win_count))]
     owners = fold_block.reshape(-1, 2 * ch_dev)
     places = fold_offset.reshape(-1, 2 * ch_dev)
-    early, late, outgoing, *ready = spectra_call(
+    early, late, outgoing, *row_parts = spectra_call(
         chan, traces.reshape(win_dev * ch_dev, length), quality.reshape(1, ch_dev), owners, places, chan_count, own_count
     )
     half = win_dev // 2
     halves = [rows.reshape(half, ch_dev, 2 * F) for rows in (early, late)]
-    ready = ready[0] if ready else jnp.concatenate([block[:, shared:] for block in halves], axis=0)
+    if not row_parts:
+        row_parts = [jnp.concatenate([block[:, shared:] for block in halves], axis=0)]
+        row_parts += [block[:, :shared] for block in halves]
+    ready, *lower = row_parts
     upper = [from_above(block) for block in halves]
     common = [round_win(ready, shift) for shift in range(1, win_count)]
     incoming = lax.all_to_all(outgoing, "chan", split_axis=0, concat_axis=0, tiled=True)
-    targets = [(window_part + shift) % win_count * own_count for shift in range(1, win_count)]
-
-    def offer(part, start):
-        rows = jnp.concatenate([halves[part][:, :shared], upper[part]], axis=1)
+
+    def offers(part):
+        rows = jnp.concatenate([lower[part], upper[part]], axis=1)
         return [
-            round_win(lax.dynamic_slice_in_dim(rows, target + start, ch_dev, 1), shift)
-            for shift, target in enumerate(targets, 1)
+            lax.dynamic_slice_in_dim(rows, (window_part + shift) % win_count * own_count, ch_dev, 1)
+            for shift in range(1, win_count)
         ]
 
-    sooner = offer(0, 0)
-    sums, zero = cross_call(win, halves + upper, win_dev, ch_dev, own_count, None, None, 0, 1.0)
-    later = offer(1, zero[0])
+    sooner = [round_win(block, shift) for shift, block in enumerate(offers(0), 1)]
+    sums, _, *waiting = cross_call(
+        win, halves + upper, win_dev, ch_dev, own_count, None, None, 0, 1.0, through=offers(1)
+    )
+    later = [round_win(block, shift) for shift, block in enumerate(waiting, 1)]
     arrived = []
     for rows, *others in zip(common, sooner, later):
         arrived += [([rows, block], n * half) for n, block in enumerate(others)]

time: 65.4 us -> 64.7 us (0.989)
  waiting for transfers between devices: 2.88 us -> 8.87 us
  local copies, waits for them, and re-layouts: 4.52 us -> 0.03 us
  other arithmetic: 1.64 us -> 0.79 us
  Pallas kernels: 36.5 us -> 35.8 us
    ppermute x4, waiting for transfers between devices: 2.87 us -> 8.87 us  [round_win(): lax.ppermute(block, 'win', [(i, (i + shift) % count) for i in range(count)])]
    unnamed x14 -> x10, local copies, waits for them, and re-layouts: 3.11 us -> 0.02 us
    slice x2 -> x0, local copies, waits for them, and re-layouts: 1.4 us -> none  [offer(): rows = jnp.concatenate([halves[part][:, :shared], upper[part]], axis=1)]
    pallas_call x3, Pallas kernels: 26.1 us -> 25 us  [cross_call(): pl.pallas_call(functools.partial(cross_kernel, last, with_sum, skipped, l...]
    concatenate x2, other arithmetic: 1.02 us -> 0.17 us  [offers(): rows = jnp.concatenate([lower[part], upper[part]], axis=1)]
  transfers between devices with their start and end apart: 7 -> 7, of which waited for: 3 -> 3; matrix products, arithmetic and copies ran while one was open for 4% -> 0% of each run, Pallas kernels for 40% -> 39%
where the time goes in v2:
time: 64.7 us; the launch traced here: 64.4 us
  Pallas kernels  35.8 us (55%)
  starting transfers between devices  18.2 us (28%)
  waiting for transfers between devices  8.87 us (14%)
  other arithmetic  0.79 us (1%)
  between operations  0.78 us (1%)
    pallas_call x3, Pallas kernels, cross_call(): pl.pallas_call(functools.partial(cross_kernel, last, with_sum, skipped, l...  25 us
    all_to_all x1, starting transfers between devices, local(): lax.all_to_all(outgoing, 'chan', split_axis=0, concat_axis=0, tiled=True)  9.39 us
    pallas_call x1, Pallas kernels, spectra_call(): pl.pallas_call(spectra_kernel, in_specs=[smem_spec()] + [anywhere] * 5, o...  9.27 us
    ppermute x4, waiting for transfers between devices, round_win(): lax.ppermute(block, 'win', [(i, (i + shift) % count) for i in range(count)])  8.87 us
    ppermute x4, starting transfers between devices, round_win(): lax.ppermute(block, 'win', [(i, (i + shift) % count) for i in range(count)])  6.18 us
    ppermute x2, starting transfers between devices, from_above(): return lax.ppermute(block, 'chan', [(i, i - 1) for i in range(1, count)])  2.58 us
    pallas_call x1, Pallas kernels, fold_call(): pl.pallas_call(fold_kernel, in_specs=[smem_spec()] + [vmem_spec()] * 6 +...  1.48 us
  transfers between devices with their start and end apart: 7, of which 3 were waited for; matrix products, arithmetic and copies ran while one was open for 0% of the time, Pallas kernels for 39%

profile of v2, /device:TPU:0, one launch (start us, length us, event | category | flops | bytes accessed | tf_op | source)
XLA Modules:
  0.0 64.4 jit_solution(9027759575783295554)
XLA Ops:
  0.6 9.3 %spectra.1 = (bf16[384,512]{1,0:T(8,128)(2,1)}, bf16[384,512]{1,0:T(8,128)(2,1)}, bf16[16,96,512]{2,1,0:T(8,128)(2,1)}, bf16[12,32,512]{2,1,0:T(8,128)(2,1)}, bf...) custom-call(s32[1]{0:T(128)} %bitcast.1.chan_ref, bf16[768,4096]{1,0:T(8,128)(2,1)} %bitcast.14, ...), custom_call_target="tpu_custom_call" | custom-call | flops 3221225472 | bytes 6291456 | tf_op jit(solution)/shard_map/spectra/pallas_call | solution.py:279
  9.9 1.3 %collective-permute-start.1 = (bf16[6,64,512]{2,1,0:T(8,128)(2,1)}, bf16[6,64,512]{2,1,0:T(8,128)(2,1)S(1)}, u32[]{:S(2)}, u32[]{:S(2)}) collective-permute-start(bf16[6,64,512]{2,1,0:T(8,128)(2,1)} %bitcast.8), channel_id=1, source_target_pairs={{2,0},{4,2},{6,4},{8,6},{10,8},{12,10},{14,12},{16,14},{18,16},{20... | collective-permute-start | bytes 1179656 | tf_op jit(solution)/shard_map/ppermute | solution.py:499
  11.2 1.3 %collective-permute-start.2 = (bf16[6,64,512]{2,1,0:T(8,128)(2,1)}, bf16[6,64,512]{2,1,0:T(8,128)(2,1)S(1)}, u32[]{:S(2)}, u32[]{:S(2)}) collective-permute-start(bf16[6,64,512]{2,1,0:T(8,128)(2,1)} %bitcast.10), channel_id=1, source_target_pairs={{2,0},{4,2},{6,4},{8,6},{10,8},{12,10},{14,12},{16,14},{18,16},{20... | collective-permute-start | bytes 1179656 | tf_op jit(solution)/shard_map/ppermute | solution.py:499
  12.5 0.0 copy-start
  12.5 0.0 copy-start.1
  12.5 9.4 %all-to-all-start = ((bf16[16,96,512]{2,1,0:T(8,128)(2,1)}), bf16[16,96,512]{2,1,0:T(8,128)(2,1)S(1)}, u32[]{:S(2)}, u32[]{:S(2)}) async-start(bf16[16,96,512]{2,1,0:T(8,128)(2,1)} %get-tuple-element.22), calls=%async_computation | async-start | bytes 3145728 | tf_op jit(solution)/shard_map/all_to_all | solution.py:530
  21.9 1.6 %collective-permute-start = (bf16[12,32,512]{2,1,0:T(8,128)(2,1)}, bf16[12,32,512]{2,1,0:T(8,128)(2,1)S(1)}, u32[]{:S(2)}, u32[]{:S(2)}) collective-permute-start(bf16[12,32,512]{2,1,0:T(8,128)(2,1)} %get-tuple-element.13), channel_id=1, source_target_pairs={{0,1},{1,0},{2,3},{3,2},{4,5},{5,4},{6,7},{7,6},{8,9},{9,8},{10,11... | collective-permute-start | bytes 1179656 | tf_op jit(solution)/shard_map/ppermute | solution.py:504
  23.5 0.0 collective-permute-done.1.refs_2_
  23.5 0.1 fusion
  23.6 1.5 %collective-permute-start.4 = (bf16[6,64,512]{2,1,0:T(8,128)(2,1)S(1)}, bf16[6,64,512]{2,1,0:T(8,128)(2,1)S(1)}, u32[]{:S(2)}, u32[]{:S(2)}) collective-permute-start(bf16[6,64,512]{2,1,0:T(8,128)(2,1)S(1)} %fusion), channel_id=1, source_target_pairs={{0,1},{1,0},{2,3},{3,2},{4,5},{5,4},{6,7},{7,6},{8,9},{9,8},{10,11... | collective-permute-start | bytes 1179656 | tf_op jit(solution)/shard_map/ppermute | solution.py:504
  25.1 0.0 collective-permute-done.2.refs_3_
  25.1 0.1 fusion.1.refs_4_
  25.2 0.0 copy-done
  25.2 0.0 copy-done.1
  25.2 11.0 %cross.3 = (f32[32,72,256]{2,1,0:T(8,128)S(1)}, s32[1]{0:T(128)}, bf16[6,64,512]{2,1,0:T(8,128)(2,1)S(1)}) custom-call(s32[1]{0:T(128)} %bitcast.win_ref, bf16[6,64,512]{2,1,0:T(8,128)(2,1)S(1)} %bitcast.9, bf16[6,64,512]{2,1,0:T(8,128)(2,1)S(1)} %bitcast.11, ...), custom_call_target="tpu_custom_call", output_to_operand_aliasing={{2}: (5, {})} | custom-call | flops 30000001024 | bytes 3932160 | tf_op jit(solution)/shard_map/cross/pallas_call | solution.py:429
  36.2 1.6 %collective-permute-start.3 = (bf16[6,64,512]{2,1,0:T(8,128)(2,1)S(1)}, bf16[6,64,512]{2,1,0:T(8,128)(2,1)S(1)}, u32[]{:S(2)}, u32[]{:S(2)}) collective-permute-start(bf16[6,64,512]{2,1,0:T(8,128)(2,1)S(1)} %get-tuple-element.17), channel_id=1, source_target_pairs={{0,1},{1,0},{2,3},{3,2},{4,5},{5,4},{6,7},{7,6},{8,9},{9,8},{10,11... | collective-permute-start | bytes 1179656 | tf_op jit(solution)/shard_map/ppermute | solution.py:504
  37.8 0.0 collective-permute-done.refs_0_
  37.8 4.8 %collective-permute-done.4.refs_1_ = bf16[6,64,512]{2,1,0:T(8,128)(2,1)S(1)} collective-permute-done((bf16[6,64,512]{2,1,0:T(8,128)(2,1)S(1)}, bf16[6,64,512]{2,1,0:T(8,128)(2,1)S(1)}, u32[]{:S(2)}, u32[]{:S(2)}) %collective-permute-start.4) | collective-permute-done | bytes 393248 | tf_op jit(solution)/shard_map/ppermute | solution.py:504
  42.6 0.0 copy-start.2
  42.6 6.2 %cross.4 = (f32[32,72,256]{2,1,0:T(8,128)S(1)}, s32[1]{0:T(128)}) custom-call(s32[1]{0:T(128)} %bitcast.win_ref, bf16[12,32,512]{2,1,0:T(8,128)(2,1)S(1)} %collective-permute-done.refs_0_, bf16[6,64,512]{2,1,0:T(8,128)(2,1)S(1)} %collective-permute-done.4.refs_1_, f32[32,72,256]{2,1,0:T(8,128)S(1)} %get-tuple-element.19.refs_2_), custom_call_target="tpu_custom_call" | custom-call | flops 15000000512 | bytes 3145728 | tf_op jit(solution)/shard_map/cross/pallas_call | solution.py:429
  48.8 1.7 %collective-permute-done.3.refs_1_ = bf16[6,64,512]{2,1,0:T(8,128)(2,1)S(1)} collective-permute-done((bf16[6,64,512]{2,1,0:T(8,128)(2,1)S(1)}, bf16[6,64,512]{2,1,0:T(8,128)(2,1)S(1)}, u32[]{:S(2)}, u32[]{:S(2)}) %collective-permute-start.3) | collective-permute-done | bytes 393248 | tf_op jit(solution)/shard_map/ppermute | solution.py:504
  50.4 0.0 copy-done.2
  50.4 0.0 copy-start.3
  50.4 0.0 copy-start.4
  50.4 7.8 %cross.5 = (f32[32,64,256]{2,1,0:T(8,128)}, s32[1]{0:T(128)}) custom-call(s32[1]{0:T(128)} %bitcast.win_ref, bf16[12,32,512]{2,1,0:T(8,128)(2,1)S(1)} %collective-permute-done.refs_0_, bf16[6,64,512]{2,1,0:T(8,128)(2,1)S(1)} %collective-permute-done.3.refs_1_, f32[32,72,256]{2,1,0:T(8,128)S(1)} %get-tuple-element.20.refs_2_, bf16[256,256]{1,0:T(8,128)(2,1)S(1)} %copy-done.2), custom_call_target="tpu_custom_call" | custom-call | flops 15000000512 | bytes 3145728 | tf_op jit(solution)/shard_map/cross/pallas_call | solution.py:429
  58.3 0.0 all-to-all-done.incoming_ref
  58.3 0.0 copy-done.3
  58.3 0.0 copy-done.4
  58.3 1.5 %fold.1 = f32[64,256]{1,0:T(8,128)S(1)} custom-call(s32[1]{0:T(128)} %bitcast.1.chan_ref, bf16[16,96,512]{2,1,0:T(8,128)(2,1)S(1)} %all-to-all-done.incoming_ref, bf16[384,512]{1,0:T(8,128)(2,1)S(1)} %copy-done, bf16[384,512]{1,0:T(8,128)(2,1)S(1)} %copy-done.1, s32[8,128]{1,0:T(8,128)S(1)} %bitcast.13, bf16[256,256]{1,0:T(8,128)(2,1)S(1)} %copy-done.2, ...), custom_call_target="tpu_custom_call" | custom-call | flops 201326592 | bytes 2359296 | tf_op jit(solution)/shard_map/fold/pallas_call | solution.py:484
  59.8 1.6 %collective-permute-start.5 = (f32[32,256]{1,0:T(8,128)S(1)}, f32[32,256]{1,0:T(8,128)S(1)}, u32[]{:S(2)}, u32[]{:S(2)}) collective-permute-start(f32[32,256]{1,0:T(8,128)S(1)} %constant_dynamic-slice_fusion), channel_id=1, source_target_pairs={{0,1},{1,0},{2,3},{3,2},{4,5},{5,4},{6,7},{7,6},{8,9},{9,8},{10,11... | collective-permute-start | bytes 98312 | tf_op jit(solution)/shard_map/ppermute | solution.py:504
  61.4 2.4 %collective-permute-done.5 = f32[32,256]{1,0:T(8,128)S(1)} collective-permute-done((f32[32,256]{1,0:T(8,128)S(1)}, f32[32,256]{1,0:T(8,128)S(1)}, u32[]{:S(2)}, u32[]{:S(2)}) %collective-permute-start.5) | collective-permute-done | bytes 32800 | tf_op jit(solution)/shard_map/ppermute | solution.py:504
  63.8 0.6 dynamic-slice_add_fusion
  (1 shorter events, 0.0 us)
Async XLA Ops:
  9.9 13.6 %collective-permute-start.1 = (bf16[6,64,512]{2,1,0:T(8,128)(2,1)}, bf16[6,64,512]{2,1,0:T(8,128)(2,1)S(1)}, u32[]{:S(2)}, u32[]{:S(2)}) collective-permute-start(bf16[6,64,512]{2,1,0:T(8,128)(2,1)} %bitcast.8), channel_id=1, source_target_pairs={{2,0},{4,2},{6,4},{8,6},{10,8},{12,10},{14,12},{16,14},{18,16},{20... | collective-permute-start | bytes 1179656 | tf_op jit(solution)/shard_map/ppermute | solution.py:499
  11.2 13.9 %collective-permute-start.2 = (bf16[6,64,512]{2,1,0:T(8,128)(2,1)}, bf16[6,64,512]{2,1,0:T(8,128)(2,1)S(1)}, u32[]{:S(2)}, u32[]{:S(2)}) collective-permute-start(bf16[6,64,512]{2,1,0:T(8,128)(2,1)} %bitcast.10), channel_id=1, source_target_pairs={{2,0},{4,2},{6,4},{8,6},{10,8},{12,10},{14,12},{16,14},{18,16},{20... | collective-permute-start | bytes 1179656 | tf_op jit(solution)/shard_map/ppermute | solution.py:499
  12.5 12.7 %copy-start = (bf16[384,512]{1,0:T(8,128)(2,1)S(1)}, bf16[384,512]{1,0:T(8,128)(2,1)}, u32[]{:S(2)}) copy-start(bf16[384,512]{1,0:T(8,128)(2,1)} %get-tuple-element.14.early_ref) | copy-start | bytes 1179652
  12.5 12.7 %copy-start.1 = (bf16[384,512]{1,0:T(8,128)(2,1)S(1)}, bf16[384,512]{1,0:T(8,128)(2,1)}, u32[]{:S(2)}) copy-start(bf16[384,512]{1,0:T(8,128)(2,1)} %get-tuple-element.15.late_ref) | copy-start | bytes 1179652
  12.5 45.8 %all-to-all-start = ((bf16[16,96,512]{2,1,0:T(8,128)(2,1)}), bf16[16,96,512]{2,1,0:T(8,128)(2,1)S(1)}, u32[]{:S(2)}, u32[]{:S(2)}) async-start(bf16[16,96,512]{2,1,0:T(8,128)(2,1)} %get-tuple-element.22), calls=%async_computation | async-start | bytes 3145728 | tf_op jit(solution)/shard_map/all_to_all | solution.py:530
  21.9 15.9 %collective-permute-start = (bf16[12,32,512]{2,1,0:T(8,128)(2,1)}, bf16[12,32,512]{2,1,0:T(8,128)(2,1)S(1)}, u32[]{:S(2)}, u32[]{:S(2)}) collective-permute-start(bf16[12,32,512]{2,1,0:T(8,128)(2,1)} %get-tuple-element.13), channel_id=1, source_target_pairs={{0,1},{1,0},{2,3},{3,2},{4,5},{5,4},{6,7},{7,6},{8,9},{9,8},{10,11... | collective-permute-start | bytes 1179656 | tf_op jit(solution)/shard_map/ppermute | solution.py:504
  23.6 19.0 %collective-permute-start.4 = (bf16[6,64,512]{2,1,0:T(8,128)(2,1)S(1)}, bf16[6,64,512]{2,1,0:T(8,128)(2,1)S(1)}, u32[]{:S(2)}, u32[]{:S(2)}) collective-permute-start(bf16[6,64,512]{2,1,0:T(8,128)(2,1)S(1)} %fusion), channel_id=1, source_target_pairs={{0,1},{1,0},{2,3},{3,2},{4,5},{5,4},{6,7},{7,6},{8,9},{9,8},{10,11... | collective-permute-start | bytes 1179656 | tf_op jit(solution)/shard_map/ppermute | solution.py:504
  36.2 14.2 %collective-permute-start.3 = (bf16[6,64,512]{2,1,0:T(8,128)(2,1)S(1)}, bf16[6,64,512]{2,1,0:T(8,128)(2,1)S(1)}, u32[]{:S(2)}, u32[]{:S(2)}) collective-permute-start(bf16[6,64,512]{2,1,0:T(8,128)(2,1)S(1)} %get-tuple-element.17), channel_id=1, source_target_pairs={{0,1},{1,0},{2,3},{3,2},{4,5},{5,4},{6,7},{7,6},{8,9},{9,8},{10,11... | collective-permute-start | bytes 1179656 | tf_op jit(solution)/shard_map/ppermute | solution.py:504
  42.6 7.9 %copy-start.2 = (bf16[256,256]{1,0:T(8,128)(2,1)S(1)}, bf16[256,256]{1,0:T(8,128)(2,1)}, u32[]{:S(2)}) copy-start(bf16[256,256]{1,0:T(8,128)(2,1)} %constant.39.clone.refs_3_.high_ref) | copy-start | bytes 393220
  50.4 7.9 %copy-start.3 = (bf16[256,256]{1,0:T(8,128)(2,1)S(1)}, bf16[256,256]{1,0:T(8,128)(2,1)}, u32[]{:S(2)}) copy-start(bf16[256,256]{1,0:T(8,128)(2,1)} %constant.40.clone.low_ref) | copy-start | bytes 393220
  50.4 7.9 %copy-start.4 = (s32[1024,1]{0,1:T(1,128)S(1)}, s32[1024,1]{0,1:T(1,128)}, u32[]{:S(2)}) copy-start(s32[1024,1]{0,1:T(1,128)} %param.9) | copy-start | bytes 12292
  59.8 4.0 %collective-permute-start.5 = (f32[32,256]{1,0:T(8,128)S(1)}, f32[32,256]{1,0:T(8,128)S(1)}, u32[]{:S(2)}, u32[]{:S(2)}) collective-permute-start(f32[32,256]{1,0:T(8,128)S(1)} %constant_dynamic-slice_fusion), channel_id=1, source_target_pairs={{0,1},{1,0},{2,3},{3,2},{4,5},{5,4},{6,7},{7,6},{8,9},{9,8},{10,11... | collective-permute-start | bytes 98312 | tf_op jit(solution)/shard_map/ppermute | solution.py:504

commit v3 on v2

--- a/solution.py
+++ b/solution.py
@@ -304,38 +304,33 @@
     )(chan, traces, jnp.asarray(forward_table(length)), quality, owners, places)
 
 
-def cross_kernel(last, with_sum, skipped, through, win_ref, *refs):
+def cross_kernel(last, with_sum, own_windows, skipped, win_ref, first_ref, second_ref, *refs):
     refs = list(refs)
-    blocks = [refs.pop(0) for _ in range(2 if with_sum else 4)]
-    refs = refs[through:]
     sum_ref = refs.pop(0) if with_sum else None
     if last:
         table_ref, out_ref, zero_ref, wide, spread, total, lags, sems = refs
     else:
-        total, zero_ref, *refs = refs
-        wide, spread = refs[through:]
+        total, zero_ref, wide, spread = refs
     zero_ref[0] = 0
     windows, own_count = spread.shape[:2]
     ch_dev = wide.shape[1] // 2
     base = pl.multiple_of(win_ref[0] * own_count, 8)
 
     def widen(w, carry):
-        if with_sum:
+        if own_windows:
+            wide[w, :ch_dev, :] = first_ref[w].astype(jnp.float32)
+            wide[w, ch_dev:, :] = second_ref[w].astype(jnp.float32)
+        else:
             shared = ch_dev - own_count
-            wide[w, shared:ch_dev, :] = blocks[0][skipped + w].astype(jnp.float32)
-            rows = blocks[1][w].astype(jnp.float32)
+            wide[w, shared:ch_dev, :] = first_ref[skipped + w].astype(jnp.float32)
+            rows = second_ref[w].astype(jnp.float32)
             for tile in range(ch_dev // 8):
                 at = base + 8 * tile
                 at = pl.multiple_of(jnp.where(at < shared, at, at + own_count), 8)
                 wide[w, pl.ds(at, 8), :] = rows[8 * tile : 8 * tile + 8]
-        else:
-            for half in range(2):
-                place = half * (windows // 2) + w
-                wide[place, :ch_dev, :] = blocks[half][w].astype(jnp.float32)
-                wide[place, ch_dev:, :] = blocks[2 + half][w].astype(jnp.float32)
         return carry
 
-    lax.fori_loop(0, windows if with_sum else windows // 2, widen, 0)
+    lax.fori_loop(0, windows, widen, 0)
 
     def repeat(w, carry):
         for tile in range(own_count // 8):
@@ -402,13 +397,11 @@
             copy.wait()
 
 
-def cross_call(win, blocks, windows, ch_dev, own_count, sums, table, skipped, share, through=()):
+def cross_call(win, first, second, windows, ch_dev, own_count, sums, table, own_windows, skipped=0):
     columns = 2 * F
     last = table is not None
     with_sum = sums is not None
-    operands = [win, *blocks, *through]
-    anywhere = [pl.BlockSpec(memory_space=pl.ANY)] * len(through)
-    in_specs = [smem_spec()] + [vmem_spec()] * len(blocks) + anywhere
+    operands = [win, first, second]
     if with_sum:
         operands.append(sums)
     scratch = [
@@ -424,25 +417,61 @@
         ]
     shape = (own_count, REACH, NLAG) if last else (own_count, SPAN, F)
     out_shape = [jax.ShapeDtypeStruct(shape, jnp.float32), jax.ShapeDtypeStruct((1,), jnp.int32)]
-    out_specs = [pl.BlockSpec(memory_space=pl.ANY) if last else vmem_spec(), smem_spec()] + anywhere
-    out_shape += [jax.ShapeDtypeStruct(array.shape, array.dtype) for array in through]
+    out_specs = [pl.BlockSpec(memory_space=pl.ANY) if last else vmem_spec(), smem_spec()]
     return pl.pallas_call(
-        functools.partial(cross_kernel, last, with_sum, skipped, len(through)),
-        in_specs=in_specs + [vmem_spec()] * (len(operands) - len(in_specs)),
-        input_output_aliases={1 + len(blocks) + n: 2 + n for n in range(len(through))},
+        functools.partial(cross_kernel, last, with_sum, own_windows, skipped),
+        in_specs=[smem_spec()] + [vmem_spec()] * (len(operands) - 1),
         out_specs=out_specs,
         out_shape=out_shape,
         scratch_shapes=scratch,
         compiler_params=pltpu.CompilerParams(vmem_limit_bytes=VMEM_LIMIT),
         cost_estimate=pl.CostEstimate(
-            flops=int(30_000_000_000 * share), bytes_accessed=4 * windows * ch_dev * columns + 4 * own_count * SPAN * F, transcendentals=0
+            flops=15_000_000_000, bytes_accessed=4 * windows * ch_dev * columns + 4 * own_count * SPAN * F, transcendentals=0
         ),
         name="cross",
     )(*operands)
 
 
-def fold_kernel(chan_ref, incoming_ref, early_ref, late_ref, owners_ref, high_ref, low_ref, earlier_ref, out_ref):
+def offer_kernel(win_count, shift, win_ref, after_ref, lower_ref, upper_ref, out_ref, same_ref):
+    same_ref[0] = win_ref[0]
+    shared, ch_dev = lower_ref.shape[1], upper_ref.shape[1]
+    own_count = ch_dev - shared
+    target = lax.rem(win_ref[0] + shift, win_count)
+    for number in range(win_count):
+        below = shared - number * own_count
+
+        @pl.when(target == number)
+        def _():
+            if below:
+                out_ref[:, :below, :] = lower_ref[:, shared - below :, :]
+            out_ref[:, below:, :] = upper_ref[:, : ch_dev - below, :]
+
+
+def offer_call(win, after, lower, upper, win_count, shift):
+    if (upper.shape[1] // win_count) % 16:
+        rows = jnp.concatenate([lower, upper], axis=1)
+        target = (win[0] + shift) % win_count * (upper.shape[1] - lower.shape[1])
+        return lax.dynamic_slice_in_dim(rows, target, upper.shape[1], 1), win
+    return pl.pallas_call(
+        functools.partial(offer_kernel, win_count, shift),
+        in_specs=[smem_spec(), smem_spec(), vmem_spec(), vmem_spec()],
+        out_specs=[vmem_spec(), smem_spec()],
+        out_shape=[jax.ShapeDtypeStruct(upper.shape, upper.dtype), jax.ShapeDtypeStruct((1,), jnp.int32)],
+        compiler_params=pltpu.CompilerParams(vmem_limit_bytes=FOLD_VMEM_LIMIT),
+        cost_estimate=pl.CostEstimate(flops=0, bytes_accessed=4 * upper.size, transcendentals=0),
+        name="offer",
+    )(win, after, lower, upper)
+
+
+def fold_kernel(
+    chan_ref, incoming_ref, early_ref, late_ref, owners_ref, high_ref, low_ref, earlier_ref, out_ref, own, sems
+):
     ch_dev = out_ref.shape[0]
+    copies = [
+        pltpu.make_async_copy(source, own.at[n], sems.at[n]) for n, source in enumerate((early_ref, late_ref))
+    ]
+    for copy in copies:
+        copy.start()
     rows = 2 * ch_dev
     pairs = 2 * early_ref.shape[0] // rows
     count, slots, columns = incoming_ref.shape
@@ -462,12 +491,20 @@
     shape = (rows, count * 2 * CAP)
     target = source + CAP * (rows_of(shape) // ch_dev)
     picker = (lanes_of(shape) == target).astype(jnp.float32).astype(jnp.bfloat16)
+    rights = [
+        jnp.dot(
+            picker,
+            incoming_ref[:, 2 * CAP * n : 2 * CAP * (n + 1), :].reshape(count * 2 * CAP, columns),
+            preferred_element_type=jnp.float32,
+        )
+        for n in range(pairs)
+    ]
+    for copy in copies:
+        copy.wait()
     sums = None
-    for n in range(pairs):
-        arrived = incoming_ref[:, 2 * CAP * n : 2 * CAP * (n + 1), :].reshape(count * 2 * CAP, columns)
-        right = jnp.dot(picker, arrived, preferred_element_type=jnp.float32)
+    for n, right in enumerate(rights):
         late, place = divmod(n, pairs // 2)
-        left = (early_ref, late_ref)[late][rows * place : rows * (place + 1), :].astype(jnp.float32)
+        left = own[late, rows * place : rows * (place + 1), :].astype(jnp.float32)
         l = [left[:, q * H : (q + 1) * H] for q in range(4)]
         r = [right[:, q * H : (q + 1) * H] for q in range(4)]
         terms = [
@@ -483,9 +520,13 @@
 def fold_call(chan, incoming, early, late, owners, ch_dev, tables, earlier):
     return pl.pallas_call(
         fold_kernel,
-        in_specs=[smem_spec()] + [vmem_spec()] * 6 + [smem_spec()],
+        in_specs=[smem_spec(), vmem_spec()]
+        + [pl.BlockSpec(memory_space=pl.ANY)] * 2
+        + [vmem_spec()] * 3
+        + [smem_spec()],
         out_specs=vmem_spec(),
         out_shape=jax.ShapeDtypeStruct((ch_dev, NLAG), jnp.float32),
+        scratch_shapes=[pltpu.VMEM((2,) + early.shape, jnp.bfloat16), pltpu.SemaphoreType.DMA((2,))],
         compiler_params=pltpu.CompilerParams(vmem_limit_bytes=FOLD_VMEM_LIMIT),
         cost_estimate=pl.CostEstimate(
             flops=4 * ch_dev * incoming.size, bytes_accessed=2 * (incoming.size + 2 * early.size), transcendentals=0
@@ -529,24 +570,18 @@
     common = [round_win(ready, shift) for shift in range(1, win_count)]
     incoming = lax.all_to_all(outgoing, "chan", split_axis=0, concat_axis=0, tiled=True)
 
-    def offers(part):
-        rows = jnp.concatenate([lower[part], upper[part]], axis=1)
-        return [
-            lax.dynamic_slice_in_dim(rows, (window_part + shift) % win_count * own_count, ch_dev, 1)
-            for shift in range(1, win_count)
-        ]
-
-    sooner = [round_win(block, shift) for shift, block in enumerate(offers(0), 1)]
-    sums, _, *waiting = cross_call(
-        win, halves + upper, win_dev, ch_dev, own_count, None, None, 0, 1.0, through=offers(1)
-    )
-    later = [round_win(block, shift) for shift, block in enumerate(waiting, 1)]
-    arrived = []
-    for rows, *others in zip(common, sooner, later):
-        arrived += [([rows, block], n * half) for n, block in enumerate(others)]
-    for n, (blocks, skipped) in enumerate(arrived):
+    sums, done = None, win
+    relayed = []
+    for part in range(2):
+        relayed.append([])
+        for shift in range(1, win_count):
+            block, win = offer_call(win, done, lower[part], upper[part], win_count, shift)
+            relayed[part].append(round_win(block, shift))
+        sums, done = cross_call(win, halves[part], upper[part], half, ch_dev, own_count, sums, None, True)
+    arrived = [(rows, block, n * half) for rows, *pair in zip(common, *relayed) for n, block in enumerate(pair)]
+    for n, (rows, block, skipped) in enumerate(arrived):
         ends = tables[0] if n == len(arrived) - 1 else None
-        sums, done = cross_call(win, blocks, half, ch_dev, own_count, sums, ends, skipped, 0.5)
+        sums, done = cross_call(win, rows, block, half, ch_dev, own_count, sums, ends, False, skipped)
     share = fold_call(chan, incoming, early, late, owners, ch_dev, tables, done)
     fold = lax.dynamic_slice_in_dim(share, window_part * own_count, own_count, 0)
     for shift in range(1, win_count):

time: 64.7 us -> 75.1 us (1.16)
  Pallas kernels: 35.8 us -> 42.6 us
  waiting for transfers between devices: 8.87 us -> 14.4 us
  starting transfers between devices: 18.2 us -> 16.2 us
    pallas_call x4 -> x7, Pallas kernels: 26.5 us -> 33.4 us  [the longest x4 28.9 us: cross_call(): pl.pallas_call(functools.partial(cross_kernel, last, with_sum, own_window...]
    ppermute x4, waiting for transfers between devices: 8.87 us -> 14.4 us  [round_win(): lax.ppermute(block, 'win', [(i, (i + shift) % count) for i in range(count)])]
    all_to_all x1, starting transfers between devices: 9.39 us -> 7.79 us  [local(): lax.all_to_all(outgoing, 'chan', split_axis=0, concat_axis=0, tiled=True)]
  transfers between devices with their start and end apart: 7 -> 7, of which waited for: 3 -> 2; matrix products, arithmetic and copies ran while one was open for 0% -> 0% of each run, Pallas kernels for 39% -> 42%
where the time goes in v3:
time: 75.1 us; the launch traced here: 74.8 us
  Pallas kernels  42.6 us (57%)
  starting transfers between devices  16.2 us (22%)
  waiting for transfers between devices  14.4 us (19%)
  between operations  0.89 us (1%)
    pallas_call x4, Pallas kernels, cross_call(): pl.pallas_call(functools.partial(cross_kernel, last, with_sum, own_window...  28.9 us
    ppermute x4, waiting for transfers between devices, round_win(): lax.ppermute(block, 'win', [(i, (i + shift) % count) for i in range(count)])  14.4 us
    pallas_call x1, Pallas kernels, spectra_call(): pl.pallas_call(spectra_kernel, in_specs=[smem_spec()] + [anywhere] * 5, o...  9.28 us
    all_to_all x1, starting transfers between devices, local(): lax.all_to_all(outgoing, 'chan', split_axis=0, concat_axis=0, tiled=True)  7.79 us
    ppermute x4, starting transfers between devices, round_win(): lax.ppermute(block, 'win', [(i, (i + shift) % count) for i in range(count)])  5.72 us
    ppermute x2, starting transfers between devices, from_above(): return lax.ppermute(block, 'chan', [(i, i - 1) for i in range(1, count)])  2.72 us
    pallas_call x2, Pallas kernels, offer_call(): pl.pallas_call(functools.partial(offer_kernel, win_count, shift), in_spec...  2.37 us
    pallas_call x1, Pallas kernels, fold_call(): pl.pallas_call(fold_kernel, in_specs=[smem_spec(), vmem_spec()] + [pl.Blo...  2.1 us
  transfers between devices with their start and end apart: 7, of which 2 were waited for; matrix products, arithmetic and copies ran while one was open for 0% of the time, Pallas kernels for 42%

profile of v3, /device:TPU:0, one launch (start us, length us, event | category | flops | bytes accessed | tf_op | source)
XLA Modules:
  0.0 74.8 jit_solution(13593563977435379537)
XLA Ops:
  0.6 9.3 %spectra.1 = (bf16[384,512]{1,0:T(8,128)(2,1)}, bf16[384,512]{1,0:T(8,128)(2,1)}, bf16[16,96,512]{2,1,0:T(8,128)(2,1)}, bf16[12,32,512]{2,1,0:T(8,128)(2,1)}, bf...) custom-call(s32[1]{0:T(128)} %bitcast.1.chan_ref, bf16[768,4096]{1,0:T(8,128)(2,1)} %bitcast.14, ...), custom_call_target="tpu_custom_call" | custom-call | flops 3221225472 | bytes 6291456 | tf_op jit(solution)/shard_map/spectra/pallas_call | solution.py:279
  9.9 0.0 copy-start.3
  9.9 0.0 copy-start
  9.9 1.4 %collective-permute-start = (bf16[6,64,512]{2,1,0:T(8,128)(2,1)}, bf16[6,64,512]{2,1,0:T(8,128)(2,1)S(1)}, u32[]{:S(2)}, u32[]{:S(2)}) collective-permute-start(bf16[6,64,512]{2,1,0:T(8,128)(2,1)} %bitcast.8), channel_id=1, source_target_pairs={{2,0},{4,2},{6,4},{8,6},{10,8},{12,10},{14,12},{16,14},{18,16},{20... | collective-permute-start | bytes 1179656 | tf_op jit(solution)/shard_map/ppermute | solution.py:540
  11.4 1.3 %collective-permute-start.1 = (bf16[6,64,512]{2,1,0:T(8,128)(2,1)}, bf16[6,64,512]{2,1,0:T(8,128)(2,1)S(1)}, u32[]{:S(2)}, u32[]{:S(2)}) collective-permute-start(bf16[6,64,512]{2,1,0:T(8,128)(2,1)} %bitcast.10), channel_id=1, source_target_pairs={{2,0},{4,2},{6,4},{8,6},{10,8},{12,10},{14,12},{16,14},{18,16},{20... | collective-permute-start | bytes 1179656 | tf_op jit(solution)/shard_map/ppermute | solution.py:540
  12.7 3.0 %collective-permute-start.2 = (bf16[12,32,512]{2,1,0:T(8,128)(2,1)}, bf16[12,32,512]{2,1,0:T(8,128)(2,1)S(1)}, u32[]{:S(2)}, u32[]{:S(2)}) collective-permute-start(bf16[12,32,512]{2,1,0:T(8,128)(2,1)} %get-tuple-element.25), channel_id=1, source_target_pairs={{0,1},{1,0},{2,3},{3,2},{4,5},{5,4},{6,7},{7,6},{8,9},{9,8},{10,11... | collective-permute-start | bytes 1179656 | tf_op jit(solution)/shard_map/ppermute | solution.py:545
  15.7 7.8 %all-to-all-start = ((bf16[16,96,512]{2,1,0:T(8,128)(2,1)}), bf16[16,96,512]{2,1,0:T(8,128)(2,1)S(1)}, u32[]{:S(2)}, u32[]{:S(2)}) async-start(bf16[16,96,512]{2,1,0:T(8,128)(2,1)} %get-tuple-element.32), calls=%async_computation | async-start | bytes 3145728 | tf_op jit(solution)/shard_map/all_to_all | solution.py:571
  23.5 0.0 collective-permute-done.upper_ref.second_ref
  23.5 0.0 copy-done.3
  23.5 0.6 offer.2
  24.1 0.0 copy-done
  24.1 0.0 copy-start.2
  24.1 0.0 copy-start.1
  24.1 6.8 %cross.4 = (f32[32,72,256]{2,1,0:T(8,128)S(1)}, s32[1]{0:T(128)}) custom-call(s32[1]{0:T(128)} %get-tuple-element.20.win_ref, bf16[6,64,512]{2,1,0:T(8,128)(2,1)S(1)} %bitcast.9, bf16[6,64,512]{2,1,0:T(8,128)(2,1)S(1)} %collective-permute-done.upper_ref.second_ref), custom_call_target="tpu_custom_call" | custom-call | flops 15000000512 | bytes 3145728 | tf_op jit(solution)/shard_map/cross/pallas_call | solution.py:421
  30.9 0.0 collective-permute-done.1.upper_ref.second_ref
  30.9 0.0 copy-done.2
  30.9 1.8 %offer.3 = (bf16[6,64,512]{2,1,0:T(8,128)(2,1)S(1)}, s32[1]{0:T(128)}) custom-call(s32[1]{0:T(128)} %get-tuple-element.20.win_ref, s32[1]{0:T(128)} %get-tuple-element.21.after_ref, bf16[6,32,512]{2,1,0:T(8,128)(2,1)S(1)} %copy-done.2, bf16[6,64,512]{2,1,0:T(8,128)(2,1)S(1)} %collective-permute-done.1.upper_ref.second_ref), custom_call_target="tpu_custom_call" | custom-call | bytes 786432 | tf_op jit(solution)/shard_map/offer/pallas_call | solution.py:455
  32.7 0.6 collective-permute-start.3
  33.4 1.5 %collective-permute-start.4 = (bf16[6,64,512]{2,1,0:T(8,128)(2,1)S(1)}, bf16[6,64,512]{2,1,0:T(8,128)(2,1)S(1)}, u32[]{:S(2)}, u32[]{:S(2)}) collective-permute-start(bf16[6,64,512]{2,1,0:T(8,128)(2,1)S(1)} %get-tuple-element.27), channel_id=1, source_target_pairs={{0,1},{1,0},{2,3},{3,2},{4,5},{5,4},{6,7},{7,6},{8,9},{9,8},{10,11... | collective-permute-start | bytes 1179656 | tf_op jit(solution)/shard_map/ppermute | solution.py:545
  34.8 0.0 copy-done.1
  34.8 6.8 %cross.5 = (f32[32,72,256]{2,1,0:T(8,128)S(1)}, s32[1]{0:T(128)}) custom-call(s32[1]{0:T(128)} %get-tuple-element.24.win_ref, bf16[6,64,512]{2,1,0:T(8,128)(2,1)S(1)} %bitcast.11, bf16[6,64,512]{2,1,0:T(8,128)(2,1)S(1)} %collective-permute-done.1.upper_ref.second_ref, f32[32,72,256]{2,1,0:T(8,128)S(1)} %get-tuple-element.28.refs_0_), custom_call_target="tpu_custom_call" | custom-call | flops 15000000512 | bytes 3145728 | tf_op jit(solution)/shard_map/cross/pallas_call | solution.py:421
  41.6 0.0 collective-permute-done.2.first_ref
  41.6 11.0 %collective-permute-done.4.second_ref = bf16[6,64,512]{2,1,0:T(8,128)(2,1)S(1)} collective-permute-done((bf16[6,64,512]{2,1,0:T(8,128)(2,1)S(1)}, bf16[6,64,512]{2,1,0:T(8,128)(2,1)S(1)}, u32[]{:S(2)}, u32[]{:S(2)}) %collective-permute-start.4) | collective-permute-done | bytes 393248 | tf_op jit(solution)/shard_map/ppermute | solution.py:545
  52.6 0.0 copy-start.4
  52.6 6.8 %cross.6 = (f32[32,72,256]{2,1,0:T(8,128)S(1)}, s32[1]{0:T(128)}) custom-call(s32[1]{0:T(128)} %get-tuple-element.24.win_ref, bf16[12,32,512]{2,1,0:T(8,128)(2,1)S(1)} %collective-permute-done.2.first_ref, bf16[6,64,512]{2,1,0:T(8,128)(2,1)S(1)} %collective-permute-done.4.second_ref, f32[32,72,256]{2,1,0:T(8,128)S(1)} %get-tuple-element.29.refs_0_), custom_call_target="tpu_custom_call" | custom-call | flops 15000000512 | bytes 3145728 | tf_op jit(solution)/shard_map/cross/pallas_call | solution.py:421
  59.5 0.0 collective-permute-done.3.second_ref
  59.5 0.0 copy-done.4
  59.5 0.0 copy-start.5
  59.5 0.0 copy-start.6
  59.5 8.5 %cross.7 = (f32[32,64,256]{2,1,0:T(8,128)}, s32[1]{0:T(128)}) custom-call(s32[1]{0:T(128)} %get-tuple-element.24.win_ref, bf16[12,32,512]{2,1,0:T(8,128)(2,1)S(1)} %collective-permute-done.2.first_ref, bf16[6,64,512]{2,1,0:T(8,128)(2,1)S(1)} %collective-permute-done.3.second_ref, f32[32,72,256]{2,1,0:T(8,128)S(1)} %get-tuple-element.30.refs_0_, ...), custom_call_target="tpu_custom_call" | custom-call | flops 15000000512 | bytes 3145728 | tf_op jit(solution)/shard_map/cross/pallas_call | solution.py:421
  68.0 0.0 all-to-all-done.incoming_ref
  68.1 0.0 copy-done.5
  68.1 0.0 copy-done.6
  68.1 2.1 %fold.1 = f32[64,256]{1,0:T(8,128)S(1)} custom-call(s32[1]{0:T(128)} %bitcast.1.chan_ref, bf16[16,96,512]{2,1,0:T(8,128)(2,1)S(1)} %all-to-all-done.incoming_ref, bf16[384,512]{1,0:T(8,128)(2,1)S(1)} %copy-done, bf16[384,512]{1,0:T(8,128)(2,1)S(1)} %copy-done.1, s32[8,128]{1,0:T(8,128)S(1)} %bitcast.13, bf16[256,256]{1,0:T(8,128)(2,1)S(1)} %copy-done.4, ...), custom_call_target="tpu_custom_call" | custom-call | flops 201326592 | bytes 2359296 | tf_op jit(solution)/shard_map/fold/pallas_call | solution.py:521
  70.2 0.6 collective-permute-start.5
  70.8 3.4 %collective-permute-done.5 = f32[32,256]{1,0:T(8,128)S(1)} collective-permute-done((f32[32,256]{1,0:T(8,128)S(1)}, f32[32,256]{1,0:T(8,128)S(1)}, u32[]{:S(2)}, u32[]{:S(2)}) %collective-permute-start.5) | collective-permute-done | bytes 32800 | tf_op jit(solution)/shard_map/ppermute | solution.py:545
  74.2 0.6 dynamic-slice_add_fusion
  (1 shorter events, 0.0 us)
Async XLA Ops:
  9.9 13.6 %copy-start.3 = (bf16[6,32,512]{2,1,0:T(8,128)(2,1)S(1)}, bf16[6,32,512]{2,1,0:T(8,128)(2,1)}, u32[]{:S(2)}) copy-start(bf16[6,32,512]{2,1,0:T(8,128)(2,1)} %get-tuple-element.18.lower_ref) | copy-start | bytes 589828
  9.9 14.2 %copy-start = (bf16[384,512]{1,0:T(8,128)(2,1)S(1)}, bf16[384,512]{1,0:T(8,128)(2,1)}, u32[]{:S(2)}) copy-start(bf16[384,512]{1,0:T(8,128)(2,1)} %get-tuple-element.19.early_ref) | copy-start | bytes 1179652
  9.9 13.6 %collective-permute-start = (bf16[6,64,512]{2,1,0:T(8,128)(2,1)}, bf16[6,64,512]{2,1,0:T(8,128)(2,1)S(1)}, u32[]{:S(2)}, u32[]{:S(2)}) collective-permute-start(bf16[6,64,512]{2,1,0:T(8,128)(2,1)} %bitcast.8), channel_id=1, source_target_pairs={{2,0},{4,2},{6,4},{8,6},{10,8},{12,10},{14,12},{16,14},{18,16},{20... | collective-permute-start | bytes 1179656 | tf_op jit(solution)/shard_map/ppermute | solution.py:540
  11.4 19.5 %collective-permute-start.1 = (bf16[6,64,512]{2,1,0:T(8,128)(2,1)}, bf16[6,64,512]{2,1,0:T(8,128)(2,1)S(1)}, u32[]{:S(2)}, u32[]{:S(2)}) collective-permute-start(bf16[6,64,512]{2,1,0:T(8,128)(2,1)} %bitcast.10), channel_id=1, source_target_pairs={{2,0},{4,2},{6,4},{8,6},{10,8},{12,10},{14,12},{16,14},{18,16},{20... | collective-permute-start | bytes 1179656 | tf_op jit(solution)/shard_map/ppermute | solution.py:540
  12.7 29.0 %collective-permute-start.2 = (bf16[12,32,512]{2,1,0:T(8,128)(2,1)}, bf16[12,32,512]{2,1,0:T(8,128)(2,1)S(1)}, u32[]{:S(2)}, u32[]{:S(2)}) collective-permute-start(bf16[12,32,512]{2,1,0:T(8,128)(2,1)} %get-tuple-element.25), channel_id=1, source_target_pairs={{0,1},{1,0},{2,3},{3,2},{4,5},{5,4},{6,7},{7,6},{8,9},{9,8},{10,11... | collective-permute-start | bytes 1179656 | tf_op jit(solution)/shard_map/ppermute | solution.py:545
  15.7 52.4 %all-to-all-start = ((bf16[16,96,512]{2,1,0:T(8,128)(2,1)}), bf16[16,96,512]{2,1,0:T(8,128)(2,1)S(1)}, u32[]{:S(2)}, u32[]{:S(2)}) async-start(bf16[16,96,512]{2,1,0:T(8,128)(2,1)} %get-tuple-element.32), calls=%async_computation | async-start | bytes 3145728 | tf_op jit(solution)/shard_map/all_to_all | solution.py:571
  24.1 6.8 %copy-start.2 = (bf16[6,32,512]{2,1,0:T(8,128)(2,1)S(1)}, bf16[6,32,512]{2,1,0:T(8,128)(2,1)}, u32[]{:S(2)}) copy-start(bf16[6,32,512]{2,1,0:T(8,128)(2,1)} %get-tuple-element.22.lower_ref) | copy-start | bytes 589828
  24.1 10.7 %copy-start.1 = (bf16[384,512]{1,0:T(8,128)(2,1)S(1)}, bf16[384,512]{1,0:T(8,128)(2,1)}, u32[]{:S(2)}) copy-start(bf16[384,512]{1,0:T(8,128)(2,1)} %get-tuple-element.23.late_ref) | copy-start | bytes 1179652
  32.7 26.8 %collective-permute-start.3 = (bf16[6,64,512]{2,1,0:T(8,128)(2,1)S(1)}, bf16[6,64,512]{2,1,0:T(8,128)(2,1)S(1)}, u32[]{:S(2)}, u32[]{:S(2)}) collective-permute-start(bf16[6,64,512]{2,1,0:T(8,128)(2,1)S(1)} %get-tuple-element.26), channel_id=1, source_target_pairs={{0,1},{1,0},{2,3},{3,2},{4,5},{5,4},{6,7},{7,6},{8,9},{9,8},{10,11... | collective-permute-start | bytes 1179656 | tf_op jit(solution)/shard_map/ppermute | solution.py:545
  33.4 19.3 %collective-permute-start.4 = (bf16[6,64,512]{2,1,0:T(8,128)(2,1)S(1)}, bf16[6,64,512]{2,1,0:T(8,128)(2,1)S(1)}, u32[]{:S(2)}, u32[]{:S(2)}) collective-permute-start(bf16[6,64,512]{2,1,0:T(8,128)(2,1)S(1)} %get-tuple-element.27), channel_id=1, source_target_pairs={{0,1},{1,0},{2,3},{3,2},{4,5},{5,4},{6,7},{7,6},{8,9},{9,8},{10,11... | collective-permute-start | bytes 1179656 | tf_op jit(solution)/shard_map/ppermute | solution.py:545
  52.6 6.9 %copy-start.4 = (bf16[256,256]{1,0:T(8,128)(2,1)S(1)}, bf16[256,256]{1,0:T(8,128)(2,1)}, u32[]{:S(2)}) copy-start(bf16[256,256]{1,0:T(8,128)(2,1)} %constant.33.clone.refs_1_.high_ref) | copy-start | bytes 393220
  59.5 8.6 %copy-start.5 = (bf16[256,256]{1,0:T(8,128)(2,1)S(1)}, bf16[256,256]{1,0:T(8,128)(2,1)}, u32[]{:S(2)}) copy-start(bf16[256,256]{1,0:T(8,128)(2,1)} %constant.34.clone.low_ref) | copy-start | bytes 393220
  59.5 8.6 %copy-start.6 = (s32[1024,1]{0,1:T(1,128)S(1)}, s32[1024,1]{0,1:T(1,128)}, u32[]{:S(2)}) copy-start(s32[1024,1]{0,1:T(1,128)} %param.9) | copy-start | bytes 12292
  70.2 4.0 %collective-permute-start.5 = (f32[32,256]{1,0:T(8,128)S(1)}, f32[32,256]{1,0:T(8,128)S(1)}, u32[]{:S(2)}, u32[]{:S(2)}) collective-permute-start(f32[32,256]{1,0:T(8,128)S(1)} %constant_dynamic-slice_fusion), channel_id=1, source_target_pairs={{0,1},{1,0},{2,3},{3,2},{4,5},{5,4},{6,7},{7,6},{8,9},{9,8},{10,11... | collective-permute-start | bytes 98312 | tf_op jit(solution)/shard_map/ppermute | solution.py:545

commit v4 on v2

--- a/solution.py
+++ b/solution.py
@@ -138,8 +138,8 @@
 
 
 def spectra_kernel(chan_ref, traces_ref, table_ref, quality_ref, owners_ref, places_ref, *refs):
-    early_ref, late_ref, outgoing_ref, *row_refs = refs[:-13]
-    traces, table, quality, owners, places, band, keep_rows, products, white, sent, selector, sems, out_sems = refs[-13:]
+    early_ref, late_ref, whitened_ref, outgoing_ref, *row_refs = refs[:-14]
+    traces, table, quality, owners, places, band, keep_rows, products, white, white_windows, sent, selector, sems, out_sems = refs[-14:]
     row_parts, chunks, rows, depth = traces.shape
     ch_dev = quality.shape[1]
     pair = 2 * ch_dev
@@ -201,6 +201,8 @@
             [parts[0] * near, parts[1] * near, parts[2] * far, parts[3] * far], axis=1
         ).astype(jnp.bfloat16)
         white[part] = values
+        if row_refs:
+            white_windows[part] = values.reshape(rows // ch_dev, ch_dev, values.shape[-1])
         for n in range(rows // pair):
             chosen = jnp.dot(
                 selector[...], values[pair * n : pair * (n + 1), :], preferred_element_type=jnp.float32
@@ -212,23 +214,23 @@
         copies = [
             (white.at[part], (early_ref, late_ref)[late].at[pl.ds(place * rows, rows), :]),
             (sent.at[part], outgoing_ref.at[:, pl.ds(part * slots, slots), :]),
+            (white.at[part], whitened_ref.at[pl.ds(part * rows, rows), :]),
         ]
         if row_refs:
             shared_ref, *lower_refs = row_refs
             height = shared_ref.shape[1]
             split = ch_dev - height
-            for w in range(rows // ch_dev):
-                first = w * ch_dev
-                copies += [
-                    (
-                        white.at[part, pl.ds(first + split, height), :],
-                        shared_ref.at[part * (rows // ch_dev) + w],
-                    ),
-                    (
-                        white.at[part, pl.ds(first, split), :],
-                        lower_refs[late].at[place * (rows // ch_dev) + w],
-                    ),
-                ]
+            count_here = rows // ch_dev
+            copies += [
+                (
+                    white_windows.at[part, :, pl.ds(split, height), :],
+                    shared_ref.at[pl.ds(part * count_here, count_here)],
+                ),
+                (
+                    white_windows.at[part, :, pl.ds(0, split), :],
+                    lower_refs[late].at[pl.ds(place * count_here, count_here)],
+                ),
+            ]
         for n, (source, target) in enumerate(copies):
             leaving.append(pltpu.make_async_copy(source, target, out_sems.at[part, n]))
             leaving[-1].start()
@@ -267,6 +269,7 @@
     out_shape = [
         jax.ShapeDtypeStruct((rows // 2, 2 * F), jnp.bfloat16),
         jax.ShapeDtypeStruct((rows // 2, 2 * F), jnp.bfloat16),
+        jax.ShapeDtypeStruct((rows, 2 * F), jnp.bfloat16),
         jax.ShapeDtypeStruct((chan_count, row_steps * slots, 2 * F), jnp.bfloat16),
     ]
     if own_count % 16 == 0:
@@ -291,10 +294,11 @@
             pltpu.VMEM((part, H), jnp.float32),
             pltpu.VMEM((2, QUARTERS * part, 2 * F), jnp.float32),
             pltpu.VMEM((row_steps, part, 2 * F), jnp.bfloat16),
+            pltpu.VMEM((row_steps, part // ch_dev, ch_dev, 2 * F), jnp.bfloat16),
             pltpu.VMEM((row_steps, chan_count, slots, 2 * F), jnp.bfloat16),
             pltpu.VMEM((chan_count * 2 * CAP, 2 * ch_dev), jnp.bfloat16),
             pltpu.SemaphoreType.DMA((row_steps + 1, QUARTERS)),
-            pltpu.SemaphoreType.DMA((row_steps, 2 + 2 * (part // ch_dev))),
+            pltpu.SemaphoreType.DMA((row_steps, 5)),
         ],
         compiler_params=pltpu.CompilerParams(vmem_limit_bytes=SPECTRA_VMEM_LIMIT),
         cost_estimate=pl.CostEstimate(
@@ -306,7 +310,7 @@
 
 def cross_kernel(last, with_sum, skipped, through, win_ref, *refs):
     refs = list(refs)
-    blocks = [refs.pop(0) for _ in range(2 if with_sum else 4)]
+    blocks = [refs.pop(0) for _ in range(2 if with_sum else 3)]
     refs = refs[through:]
     sum_ref = refs.pop(0) if with_sum else None
     if last:
@@ -331,8 +335,8 @@
         else:
             for half in range(2):
                 place = half * (windows // 2) + w
-                wide[place, :ch_dev, :] = blocks[half][w].astype(jnp.float32)
-                wide[place, ch_dev:, :] = blocks[2 + half][w].astype(jnp.float32)
+                wide[place, :ch_dev, :] = blocks[0][place].astype(jnp.float32)
+                wide[place, ch_dev:, :] = blocks[1 + half][w].astype(jnp.float32)
         return carry
 
     lax.fori_loop(0, windows if with_sum else windows // 2, widen, 0)
@@ -441,10 +445,10 @@
     )(*operands)
 
 
-def fold_kernel(chan_ref, incoming_ref, early_ref, late_ref, owners_ref, high_ref, low_ref, earlier_ref, out_ref):
+def fold_kernel(chan_ref, incoming_ref, own_ref, owners_ref, high_ref, low_ref, earlier_ref, out_ref):
     ch_dev = out_ref.shape[0]
     rows = 2 * ch_dev
-    pairs = 2 * early_ref.shape[0] // rows
+    pairs = own_ref.shape[0] // rows
     count, slots, columns = incoming_ref.shape
     owners = owners_ref[...].astype(jnp.float32)
     per_row = owners.shape[1] // ch_dev
@@ -466,8 +470,7 @@
     for n in range(pairs):
         arrived = incoming_ref[:, 2 * CAP * n : 2 * CAP * (n + 1), :].reshape(count * 2 * CAP, columns)
         right = jnp.dot(picker, arrived, preferred_element_type=jnp.float32)
-        late, place = divmod(n, pairs // 2)
-        left = (early_ref, late_ref)[late][rows * place : rows * (place + 1), :].astype(jnp.float32)
+        left = own_ref[rows * n : rows * (n + 1), :].astype(jnp.float32)
         l = [left[:, q * H : (q + 1) * H] for q in range(4)]
         r = [right[:, q * H : (q + 1) * H] for q in range(4)]
         terms = [
@@ -480,18 +483,18 @@
     out_ref[...] = lag_transform(stacks, high_ref[...], low_ref[...])
 
 
-def fold_call(chan, incoming, early, late, owners, ch_dev, tables, earlier):
+def fold_call(chan, incoming, own, owners, ch_dev, tables, earlier):
     return pl.pallas_call(
         fold_kernel,
-        in_specs=[smem_spec()] + [vmem_spec()] * 6 + [smem_spec()],
+        in_specs=[smem_spec()] + [vmem_spec()] * 5 + [smem_spec()],
         out_specs=vmem_spec(),
         out_shape=jax.ShapeDtypeStruct((ch_dev, NLAG), jnp.float32),
         compiler_params=pltpu.CompilerParams(vmem_limit_bytes=FOLD_VMEM_LIMIT),
         cost_estimate=pl.CostEstimate(
-            flops=4 * ch_dev * incoming.size, bytes_accessed=2 * (incoming.size + 2 * early.size), transcendentals=0
+            flops=4 * ch_dev * incoming.size, bytes_accessed=2 * (incoming.size + own.size), transcendentals=0
         ),
         name="fold",
-    )(chan, incoming, early, late, owners, *tables, earlier)
+    )(chan, incoming, own, owners, *tables, earlier)
 
 
 def from_above(block):
@@ -516,7 +519,7 @@
     tables = [jnp.asarray(t) for t in inverse_tables(1.0 / math.sqrt(F * win_dev * win_count))]
     owners = fold_block.reshape(-1, 2 * ch_dev)
     places = fold_offset.reshape(-1, 2 * ch_dev)
-    early, late, outgoing, *row_parts = spectra_call(
+    early, late, flat, outgoing, *row_parts = spectra_call(
         chan, traces.reshape(win_dev * ch_dev, length), quality.reshape(1, ch_dev), owners, places, chan_count, own_count
     )
     half = win_dev // 2
@@ -538,7 +541,7 @@
 
     sooner = [round_win(block, shift) for shift, block in enumerate(offers(0), 1)]
     sums, _, *waiting = cross_call(
-        win, halves + upper, win_dev, ch_dev, own_count, None, None, 0, 1.0, through=offers(1)
+        win, [flat.reshape(win_dev, ch_dev, 2 * F)] + upper, win_dev, ch_dev, own_count, None, None, 0, 1.0, through=offers(1)
     )
     later = [round_win(block, shift) for shift, block in enumerate(waiting, 1)]
     arrived = []
@@ -547,7 +550,7 @@
     for n, (blocks, skipped) in enumerate(arrived):
         ends = tables[0] if n == len(arrived) - 1 else None
         sums, done = cross_call(win, blocks, half, ch_dev, own_count, sums, ends, skipped, 0.5)
-    share = fold_call(chan, incoming, early, late, owners, ch_dev, tables, done)
+    share = fold_call(chan, incoming, flat, owners, ch_dev, tables, done)
     fold = lax.dynamic_slice_in_dim(share, window_part * own_count, own_count, 0)
     for shift in range(1, win_count):
         target = (window_part + shift) % win_count * own_count

time: 64.7 us -> 64.5 us (level)
  no operation moved by 1% of the time
where the time goes in v4:
time: 64.5 us; the launch traced here: 64.2 us
  Pallas kernels  35.6 us (55%)
  starting transfers between devices  18.1 us (28%)
  waiting for transfers between devices  8.9 us (14%)
  other arithmetic  0.79 us (1%)
  between operations  0.77 us (1%)
    pallas_call x3, Pallas kernels, cross_call(): pl.pallas_call(functools.partial(cross_kernel, last, with_sum, skipped, l...  25 us
    all_to_all x1, starting transfers between devices, local(): lax.all_to_all(outgoing, 'chan', split_axis=0, concat_axis=0, tiled=True)  9.39 us
    pallas_call x1, Pallas kernels, spectra_call(): pl.pallas_call(spectra_kernel, in_specs=[smem_spec()] + [anywhere] * 5, o...  9.21 us
    ppermute x4, waiting for transfers between devices, round_win(): lax.ppermute(block, 'win', [(i, (i + shift) % count) for i in range(count)])  8.89 us
    ppermute x4, starting transfers between devices, round_win(): lax.ppermute(block, 'win', [(i, (i + shift) % count) for i in range(count)])  6.17 us
    ppermute x2, starting transfers between devices, from_above(): return lax.ppermute(block, 'chan', [(i, i - 1) for i in range(1, count)])  2.58 us
    pallas_call x1, Pallas kernels, fold_call(): pl.pallas_call(fold_kernel, in_specs=[smem_spec()] + [vmem_spec()] * 5 +...  1.36 us
  transfers between devices with their start and end apart: 7, of which 3 were waited for; matrix products, arithmetic and copies ran while one was open for 0% of the time, Pallas kernels for 39%

profile of v4, /device:TPU:0, one launch (start us, length us, event | category | flops | bytes accessed | tf_op | source)
XLA Modules:
  0.0 64.2 jit_solution(9809649123261608705)
XLA Ops:
  0.6 9.2 %spectra.1 = (bf16[384,512]{1,0:T(8,128)(2,1)}, bf16[384,512]{1,0:T(8,128)(2,1)}, bf16[768,512]{1,0:T(8,128)(2,1)}, bf16[16,96,512]{2,1,0:T(8,128)(2,1)}, bf16[1...) custom-call(s32[1]{0:T(128)} %bitcast.1.chan_ref, bf16[768,4096]{1,0:T(8,128)(2,1)} %bitcast.12, ...), custom_call_target="tpu_custom_call" | custom-call | flops 3221225472 | bytes 6291456 | tf_op jit(solution)/shard_map/spectra/pallas_call | solution.py:282
  9.9 1.3 %collective-permute-start.1 = (bf16[6,64,512]{2,1,0:T(8,128)(2,1)}, bf16[6,64,512]{2,1,0:T(8,128)(2,1)S(1)}, u32[]{:S(2)}, u32[]{:S(2)}) collective-permute-start(bf16[6,64,512]{2,1,0:T(8,128)(2,1)} %bitcast.14), channel_id=1, source_target_pairs={{2,0},{4,2},{6,4},{8,6},{10,8},{12,10},{14,12},{16,14},{18,16},{20... | collective-permute-start | bytes 1179656 | tf_op jit(solution)/shard_map/ppermute | solution.py:502
  11.2 1.3 %collective-permute-start.2 = (bf16[6,64,512]{2,1,0:T(8,128)(2,1)}, bf16[6,64,512]{2,1,0:T(8,128)(2,1)S(1)}, u32[]{:S(2)}, u32[]{:S(2)}) collective-permute-start(bf16[6,64,512]{2,1,0:T(8,128)(2,1)} %bitcast.13), channel_id=1, source_target_pairs={{2,0},{4,2},{6,4},{8,6},{10,8},{12,10},{14,12},{16,14},{18,16},{20... | collective-permute-start | bytes 1179656 | tf_op jit(solution)/shard_map/ppermute | solution.py:502
  12.5 0.0 copy-start
  12.5 9.4 %all-to-all-start = ((bf16[16,96,512]{2,1,0:T(8,128)(2,1)}), bf16[16,96,512]{2,1,0:T(8,128)(2,1)S(1)}, u32[]{:S(2)}, u32[]{:S(2)}) async-start(bf16[16,96,512]{2,1,0:T(8,128)(2,1)} %get-tuple-element.24), calls=%async_computation | async-start | bytes 3145728 | tf_op jit(solution)/shard_map/all_to_all | solution.py:533
  21.9 1.5 %collective-permute-start = (bf16[12,32,512]{2,1,0:T(8,128)(2,1)}, bf16[12,32,512]{2,1,0:T(8,128)(2,1)S(1)}, u32[]{:S(2)}, u32[]{:S(2)}) collective-permute-start(bf16[12,32,512]{2,1,0:T(8,128)(2,1)} %get-tuple-element.14), channel_id=1, source_target_pairs={{0,1},{1,0},{2,3},{3,2},{4,5},{5,4},{6,7},{7,6},{8,9},{9,8},{10,11... | collective-permute-start | bytes 1179656 | tf_op jit(solution)/shard_map/ppermute | solution.py:507
  23.4 0.0 collective-permute-done.1.refs_1_
  23.4 0.1 fusion
  23.5 1.5 %collective-permute-start.4 = (bf16[6,64,512]{2,1,0:T(8,128)(2,1)S(1)}, bf16[6,64,512]{2,1,0:T(8,128)(2,1)S(1)}, u32[]{:S(2)}, u32[]{:S(2)}) collective-permute-start(bf16[6,64,512]{2,1,0:T(8,128)(2,1)S(1)} %fusion), channel_id=1, source_target_pairs={{0,1},{1,0},{2,3},{3,2},{4,5},{5,4},{6,7},{7,6},{8,9},{9,8},{10,11... | collective-permute-start | bytes 1179656 | tf_op jit(solution)/shard_map/ppermute | solution.py:507
  25.0 0.0 collective-permute-done.2.refs_2_
  25.0 0.1 fusion.1.refs_3_
  25.1 0.0 copy-done
  25.1 11.0 %cross.3 = (f32[32,72,256]{2,1,0:T(8,128)S(1)}, s32[1]{0:T(128)}, bf16[6,64,512]{2,1,0:T(8,128)(2,1)S(1)}) custom-call(s32[1]{0:T(128)} %bitcast.win_ref, bf16[12,64,512]{2,1,0:T(8,128)(2,1)S(1)} %bitcast.9, bf16[6,64,512]{2,1,0:T(8,128)(2,1)S(1)} %collective-permute-done.1.refs_1_, ...), custom_call_target="tpu_custom_call", output_to_operand_aliasing={{2}: (4, {})} | custom-call | flops 30000001024 | bytes 3932160 | tf_op jit(solution)/shard_map/cross/pallas_call | solution.py:433
  36.2 1.5 %collective-permute-start.3 = (bf16[6,64,512]{2,1,0:T(8,128)(2,1)S(1)}, bf16[6,64,512]{2,1,0:T(8,128)(2,1)S(1)}, u32[]{:S(2)}, u32[]{:S(2)}) collective-permute-start(bf16[6,64,512]{2,1,0:T(8,128)(2,1)S(1)} %get-tuple-element.19), channel_id=1, source_target_pairs={{0,1},{1,0},{2,3},{3,2},{4,5},{5,4},{6,7},{7,6},{8,9},{9,8},{10,11... | collective-permute-start | bytes 1179656 | tf_op jit(solution)/shard_map/ppermute | solution.py:507
  37.7 0.0 collective-permute-done.refs_0_
  37.7 4.8 %collective-permute-done.4.refs_1_ = bf16[6,64,512]{2,1,0:T(8,128)(2,1)S(1)} collective-permute-done((bf16[6,64,512]{2,1,0:T(8,128)(2,1)S(1)}, bf16[6,64,512]{2,1,0:T(8,128)(2,1)S(1)}, u32[]{:S(2)}, u32[]{:S(2)}) %collective-permute-start.4) | collective-permute-done | bytes 393248 | tf_op jit(solution)/shard_map/ppermute | solution.py:507
  42.5 0.0 copy-start.1
  42.5 6.2 %cross.4 = (f32[32,72,256]{2,1,0:T(8,128)S(1)}, s32[1]{0:T(128)}) custom-call(s32[1]{0:T(128)} %bitcast.win_ref, bf16[12,32,512]{2,1,0:T(8,128)(2,1)S(1)} %collective-permute-done.refs_0_, bf16[6,64,512]{2,1,0:T(8,128)(2,1)S(1)} %collective-permute-done.4.refs_1_, f32[32,72,256]{2,1,0:T(8,128)S(1)} %get-tuple-element.21.refs_2_), custom_call_target="tpu_custom_call" | custom-call | flops 15000000512 | bytes 3145728 | tf_op jit(solution)/shard_map/cross/pallas_call | solution.py:433
  48.7 1.7 %collective-permute-done.3.refs_1_ = bf16[6,64,512]{2,1,0:T(8,128)(2,1)S(1)} collective-permute-done((bf16[6,64,512]{2,1,0:T(8,128)(2,1)S(1)}, bf16[6,64,512]{2,1,0:T(8,128)(2,1)S(1)}, u32[]{:S(2)}, u32[]{:S(2)}) %collective-permute-start.3) | collective-permute-done | bytes 393248 | tf_op jit(solution)/shard_map/ppermute | solution.py:507
  50.4 0.0 copy-done.1
  50.4 0.0 copy-start.2
  50.4 0.0 copy-start.3
  50.4 7.8 %cross.5 = (f32[32,64,256]{2,1,0:T(8,128)}, s32[1]{0:T(128)}) custom-call(s32[1]{0:T(128)} %bitcast.win_ref, bf16[12,32,512]{2,1,0:T(8,128)(2,1)S(1)} %collective-permute-done.refs_0_, bf16[6,64,512]{2,1,0:T(8,128)(2,1)S(1)} %collective-permute-done.3.refs_1_, f32[32,72,256]{2,1,0:T(8,128)S(1)} %get-tuple-element.22.refs_2_, bf16[256,256]{1,0:T(8,128)(2,1)S(1)} %copy-done.1), custom_call_target="tpu_custom_call" | custom-call | flops 15000000512 | bytes 3145728 | tf_op jit(solution)/shard_map/cross/pallas_call | solution.py:433
  58.2 0.0 all-to-all-done.incoming_ref
  58.2 0.0 copy-done.2
  58.2 0.0 copy-done.3
  58.3 1.4 %fold.1 = f32[64,256]{1,0:T(8,128)S(1)} custom-call(s32[1]{0:T(128)} %bitcast.1.chan_ref, bf16[16,96,512]{2,1,0:T(8,128)(2,1)S(1)} %all-to-all-done.incoming_ref, bf16[768,512]{1,0:T(8,128)(2,1)S(1)} %copy-done, s32[8,128]{1,0:T(8,128)S(1)} %bitcast.11, bf16[256,256]{1,0:T(8,128)(2,1)S(1)} %copy-done.1, bf16[256,256]{1,0:T(8,128)(2,1)S(1)} %copy-done.2, ...), custom_call_target="tpu_custom_call" | custom-call | flops 201326592 | bytes 2359296 | tf_op jit(solution)/shard_map/fold/pallas_call | solution.py:487
  59.6 1.5 %collective-permute-start.5 = (f32[32,256]{1,0:T(8,128)S(1)}, f32[32,256]{1,0:T(8,128)S(1)}, u32[]{:S(2)}, u32[]{:S(2)}) collective-permute-start(f32[32,256]{1,0:T(8,128)S(1)} %constant_dynamic-slice_fusion), channel_id=1, source_target_pairs={{0,1},{1,0},{2,3},{3,2},{4,5},{5,4},{6,7},{7,6},{8,9},{9,8},{10,11... | collective-permute-start | bytes 98312 | tf_op jit(solution)/shard_map/ppermute | solution.py:507
  61.2 2.4 %collective-permute-done.5 = f32[32,256]{1,0:T(8,128)S(1)} collective-permute-done((f32[32,256]{1,0:T(8,128)S(1)}, f32[32,256]{1,0:T(8,128)S(1)}, u32[]{:S(2)}, u32[]{:S(2)}) %collective-permute-start.5) | collective-permute-done | bytes 32800 | tf_op jit(solution)/shard_map/ppermute | solution.py:507
  63.6 0.6 dynamic-slice_add_fusion
  (1 shorter events, 0.0 us)
Async XLA Ops:
  9.9 13.6 %collective-permute-start.1 = (bf16[6,64,512]{2,1,0:T(8,128)(2,1)}, bf16[6,64,512]{2,1,0:T(8,128)(2,1)S(1)}, u32[]{:S(2)}, u32[]{:S(2)}) collective-permute-start(bf16[6,64,512]{2,1,0:T(8,128)(2,1)} %bitcast.14), channel_id=1, source_target_pairs={{2,0},{4,2},{6,4},{8,6},{10,8},{12,10},{14,12},{16,14},{18,16},{20... | collective-permute-start | bytes 1179656 | tf_op jit(solution)/shard_map/ppermute | solution.py:502
  11.2 13.9 %collective-permute-start.2 = (bf16[6,64,512]{2,1,0:T(8,128)(2,1)}, bf16[6,64,512]{2,1,0:T(8,128)(2,1)S(1)}, u32[]{:S(2)}, u32[]{:S(2)}) collective-permute-start(bf16[6,64,512]{2,1,0:T(8,128)(2,1)} %bitcast.13), channel_id=1, source_target_pairs={{2,0},{4,2},{6,4},{8,6},{10,8},{12,10},{14,12},{16,14},{18,16},{20... | collective-permute-start | bytes 1179656 | tf_op jit(solution)/shard_map/ppermute | solution.py:502
  12.5 12.7 %copy-start = (bf16[768,512]{1,0:T(8,128)(2,1)S(1)}, bf16[768,512]{1,0:T(8,128)(2,1)}, u32[]{:S(2)}) copy-start(bf16[768,512]{1,0:T(8,128)(2,1)} %get-tuple-element.15.own_ref) | copy-start | bytes 2359300
  12.5 45.8 %all-to-all-start = ((bf16[16,96,512]{2,1,0:T(8,128)(2,1)}), bf16[16,96,512]{2,1,0:T(8,128)(2,1)S(1)}, u32[]{:S(2)}, u32[]{:S(2)}) async-start(bf16[16,96,512]{2,1,0:T(8,128)(2,1)} %get-tuple-element.24), calls=%async_computation | async-start | bytes 3145728 | tf_op jit(solution)/shard_map/all_to_all | solution.py:533
  21.9 15.9 %collective-permute-start = (bf16[12,32,512]{2,1,0:T(8,128)(2,1)}, bf16[12,32,512]{2,1,0:T(8,128)(2,1)S(1)}, u32[]{:S(2)}, u32[]{:S(2)}) collective-permute-start(bf16[12,32,512]{2,1,0:T(8,128)(2,1)} %get-tuple-element.14), channel_id=1, source_target_pairs={{0,1},{1,0},{2,3},{3,2},{4,5},{5,4},{6,7},{7,6},{8,9},{9,8},{10,11... | collective-permute-start | bytes 1179656 | tf_op jit(solution)/shard_map/ppermute | solution.py:507
  23.5 19.0 %collective-permute-start.4 = (bf16[6,64,512]{2,1,0:T(8,128)(2,1)S(1)}, bf16[6,64,512]{2,1,0:T(8,128)(2,1)S(1)}, u32[]{:S(2)}, u32[]{:S(2)}) collective-permute-start(bf16[6,64,512]{2,1,0:T(8,128)(2,1)S(1)} %fusion), channel_id=1, source_target_pairs={{0,1},{1,0},{2,3},{3,2},{4,5},{5,4},{6,7},{7,6},{8,9},{9,8},{10,11... | collective-permute-start | bytes 1179656 | tf_op jit(solution)/shard_map/ppermute | solution.py:507
  36.2 14.2 %collective-permute-start.3 = (bf16[6,64,512]{2,1,0:T(8,128)(2,1)S(1)}, bf16[6,64,512]{2,1,0:T(8,128)(2,1)S(1)}, u32[]{:S(2)}, u32[]{:S(2)}) collective-permute-start(bf16[6,64,512]{2,1,0:T(8,128)(2,1)S(1)} %get-tuple-element.19), channel_id=1, source_target_pairs={{0,1},{1,0},{2,3},{3,2},{4,5},{5,4},{6,7},{7,6},{8,9},{9,8},{10,11... | collective-permute-start | bytes 1179656 | tf_op jit(solution)/shard_map/ppermute | solution.py:507
  42.5 7.9 %copy-start.1 = (bf16[256,256]{1,0:T(8,128)(2,1)S(1)}, bf16[256,256]{1,0:T(8,128)(2,1)}, u32[]{:S(2)}) copy-start(bf16[256,256]{1,0:T(8,128)(2,1)} %constant.39.clone.refs_3_.high_ref) | copy-start | bytes 393220
  50.4 7.9 %copy-start.2 = (bf16[256,256]{1,0:T(8,128)(2,1)S(1)}, bf16[256,256]{1,0:T(8,128)(2,1)}, u32[]{:S(2)}) copy-start(bf16[256,256]{1,0:T(8,128)(2,1)} %constant.40.clone.low_ref) | copy-start | bytes 393220
  50.4 7.9 %copy-start.3 = (s32[1024,1]{0,1:T(1,128)S(1)}, s32[1024,1]{0,1:T(1,128)}, u32[]{:S(2)}) copy-start(s32[1024,1]{0,1:T(1,128)} %param.9) | copy-start | bytes 12292
  59.6 4.0 %collective-permute-start.5 = (f32[32,256]{1,0:T(8,128)S(1)}, f32[32,256]{1,0:T(8,128)S(1)}, u32[]{:S(2)}, u32[]{:S(2)}) collective-permute-start(f32[32,256]{1,0:T(8,128)S(1)} %constant_dynamic-slice_fusion), channel_id=1, source_target_pairs={{0,1},{1,0},{2,3},{3,2},{4,5},{5,4},{6,7},{7,6},{8,9},{9,8},{10,11... | collective-permute-start | bytes 98312 | tf_op jit(solution)/shard_map/ppermute | solution.py:507

commit v5 on v4

--- a/solution.py
+++ b/solution.py
@@ -308,35 +308,50 @@
     )(chan, traces, jnp.asarray(forward_table(length)), quality, owners, places)
 
 
-def cross_kernel(last, with_sum, skipped, through, win_ref, *refs):
+def cross_kernel(last, with_sum, skipped, through, kept, win_ref, *refs):
     refs = list(refs)
     blocks = [refs.pop(0) for _ in range(2 if with_sum else 3)]
     refs = refs[through:]
+    kept_ref = refs.pop(0) if kept else None
     sum_ref = refs.pop(0) if with_sum else None
     if last:
         table_ref, out_ref, zero_ref, wide, spread, total, lags, sems = refs
     else:
         total, zero_ref, *refs = refs
-        wide, spread = refs[through:]
+        if kept:
+            refs[through][...] = kept_ref[...]
+        wide, spread = refs[through + kept :]
     zero_ref[0] = 0
     windows, own_count = spread.shape[:2]
     ch_dev = wide.shape[1] // 2
     base = pl.multiple_of(win_ref[0] * own_count, 8)
 
+    def spread_out(rows):
+        kinds = []
+        for half in range(2):
+            re, im = rows[:, 2 * half * H : (2 * half + 1) * H], rows[:, (2 * half + 1) * H : (2 * half + 2) * H]
+            first = lanes_of(re.shape) == 0
+            kinds += [re, jnp.where(first, re - im, re + im), im - re]
+        return kinds
+
+    def put(w, at, rows):
+        for k, values in enumerate(spread_out(rows)):
+            wide[w, at, k * H : (k + 1) * H] = values
+
     def widen(w, carry):
         if with_sum:
             shared = ch_dev - own_count
-            wide[w, shared:ch_dev, :] = blocks[0][skipped + w].astype(jnp.float32)
+            put(w, pl.ds(shared, own_count), blocks[0][skipped + w].astype(jnp.float32))
             rows = blocks[1][w].astype(jnp.float32)
             for tile in range(ch_dev // 8):
                 at = base + 8 * tile
                 at = pl.multiple_of(jnp.where(at < shared, at, at + own_count), 8)
-                wide[w, pl.ds(at, 8), :] = rows[8 * tile : 8 * tile + 8]
+                put(w, pl.ds(at, 8), rows[8 * tile : 8 * tile + 8])
         else:
             for half in range(2):
                 place = half * (windows // 2) + w
-                wide[place, :ch_dev, :] = blocks[0][place].astype(jnp.float32)
-                wide[place, ch_dev:, :] = blocks[1 + half][w].astype(jnp.float32)
+                put(place, pl.ds(0, ch_dev), blocks[0][place].astype(jnp.float32))
+                put(place, pl.ds(ch_dev, ch_dev), blocks[1 + half][w].astype(jnp.float32))
         return carry
 
     lax.fori_loop(0, windows if with_sum else windows // 2, widen, 0)
@@ -344,43 +359,51 @@
     def repeat(w, carry):
         for tile in range(own_count // 8):
             rows = wide[w, pl.ds(pl.multiple_of(base + 8 * tile, 8), 8), :]
+            kinds = []
+            for half in range(2):
+                re, less = rows[:, 3 * half * H : (3 * half + 1) * H], rows[:, (3 * half + 2) * H : (3 * half + 3) * H]
+                im = re + less
+                second = jnp.where(lanes_of(re.shape) == 0, im, re)
+                kinds += [re + im, -second if half else second, im]
             for i in range(8):
-                for q in range(4):
-                    spread[w, 8 * tile + i, q] = jnp.broadcast_to(rows[i : i + 1, q * H : (q + 1) * H], (8, H))
+                for k, values in enumerate(kinds):
+                    spread[w, 8 * tile + i, k] = jnp.broadcast_to(values[i : i + 1, :], (8, H))
         return carry
 
     lax.fori_loop(0, windows, repeat, 0)
 
-    group, tiles = 4, 3
+    group, tiles = 2, 3
     rounds = SPAN // (8 * tiles)
 
     def block(index, carry):
         g = index // rounds
         j = index % rounds
-        start = pl.multiple_of(base + 8 * (g // 2) + 8 * tiles * j, 8)
+        start = pl.multiple_of(base + 8 * (g // (8 // group)) + 8 * tiles * j, 8)
 
         def add_window(w, sums):
             sums = list(sums)
             right = [
-                [wide[w, pl.ds(pl.multiple_of(start + 8 * t, 8), 8), q * H : (q + 1) * H] for q in range(4)]
+                [wide[w, pl.ds(pl.multiple_of(start + 8 * t, 8), 8), k * H : (k + 1) * H] for k in range(6)]
                 for t in range(tiles)
             ]
             for i in range(group):
-                left = [spread[w, group * g + i, q] for q in range(4)]
+                left = [spread[w, group * g + i, k] for k in range(6)]
                 for t in range(tiles):
-                    at = 3 * (i * tiles + t)
+                    at = 4 * (i * tiles + t)
                     r = right[t]
-                    sums[at] = sums[at] + (left[0] * r[0] + left[1] * r[1])
-                    sums[at + 1] = sums[at + 1] + (left[2] * r[2] + left[3] * r[3])
-                    sums[at + 2] = sums[at + 2] + ((left[1] * r[0] - left[0] * r[1]) + (left[2] * r[3] - left[3] * r[2]))
+                    sums[at] = sums[at] + left[0] * r[0]
+                    sums[at + 1] = sums[at + 1] + left[3] * r[3]
+                    sums[at + 2] = sums[at + 2] + (left[1] * r[1] + left[4] * r[4])
+                    sums[at + 3] = sums[at + 3] + (left[2] * r[2] + left[5] * r[5])
             return tuple(sums)
 
         zero = jnp.zeros((8, H), jnp.float32)
-        sums = lax.fori_loop(0, windows, add_window, (zero,) * (3 * group * tiles), unroll=2)
+        sums = lax.fori_loop(0, windows, add_window, (zero,) * (4 * group * tiles), unroll=2)
         for i in range(group):
             for t in range(tiles):
-                at = 3 * (i * tiles + t)
-                real, imag = fold_columns(sums[at], sums[at + 1], sums[at + 2])
+                near, far, turned, straight = sums[4 * (i * tiles + t) : 4 * (i * tiles + t) + 4]
+                real = (near + far) + straight
+                imag = (near - far) - turned
                 where = pl.ds(pl.multiple_of(8 * tiles * j + 8 * t, 8), 8)
                 if with_sum:
                     real = real + sum_ref[group * g + i, where, :H]
@@ -406,18 +429,18 @@
             copy.wait()
 
 
-def cross_call(win, blocks, windows, ch_dev, own_count, sums, table, skipped, share, through=()):
-    columns = 2 * F
+def cross_call(win, blocks, windows, ch_dev, own_count, sums, table, skipped, share, through=(), kept=()):
+    columns = 6 * H
     last = table is not None
     with_sum = sums is not None
-    operands = [win, *blocks, *through]
+    operands = [win, *blocks, *through, *kept]
     anywhere = [pl.BlockSpec(memory_space=pl.ANY)] * len(through)
     in_specs = [smem_spec()] + [vmem_spec()] * len(blocks) + anywhere
     if with_sum:
         operands.append(sums)
     scratch = [
         pltpu.VMEM((windows, 2 * ch_dev, columns), jnp.float32),
-        pltpu.VMEM((windows, own_count, 4, 8, H), jnp.float32),
+        pltpu.VMEM((windows, own_count, 6, 8, H), jnp.float32),
     ]
     if last:
         operands.append(table)
@@ -429,9 +452,10 @@
     shape = (own_count, REACH, NLAG) if last else (own_count, SPAN, F)
     out_shape = [jax.ShapeDtypeStruct(shape, jnp.float32), jax.ShapeDtypeStruct((1,), jnp.int32)]
     out_specs = [pl.BlockSpec(memory_space=pl.ANY) if last else vmem_spec(), smem_spec()] + anywhere
-    out_shape += [jax.ShapeDtypeStruct(array.shape, array.dtype) for array in through]
+    out_specs += [vmem_spec()] * len(kept)
+    out_shape += [jax.ShapeDtypeStruct(array.shape, array.dtype) for array in (*through, *kept)]
     return pl.pallas_call(
-        functools.partial(cross_kernel, last, with_sum, skipped, len(through)),
+        functools.partial(cross_kernel, last, with_sum, skipped, len(through), len(kept)),
         in_specs=in_specs + [vmem_spec()] * (len(operands) - len(in_specs)),
         input_output_aliases={1 + len(blocks) + n: 2 + n for n in range(len(through))},
         out_specs=out_specs,
@@ -549,7 +573,11 @@
         arrived += [([rows, block], n * half) for n, block in enumerate(others)]
     for n, (blocks, skipped) in enumerate(arrived):
         ends = tables[0] if n == len(arrived) - 1 else None
-        sums, done = cross_call(win, blocks, half, ch_dev, own_count, sums, ends, skipped, 0.5)
+        kept = [flat] if n == len(arrived) - 2 else []
+        sums, done, *copies = cross_call(
+            win, blocks, half, ch_dev, own_count, sums, ends, skipped, 0.5, kept=kept
+        )
+        flat = copies[0] if copies else flat
     share = fold_call(chan, incoming, flat, owners, ch_dev, tables, done)
     fold = lax.dynamic_slice_in_dim(share, window_part * own_count, own_count, 0)
     for shift in range(1, win_count):

time: 64.5 us -> 65.1 us (level)
  Pallas kernels: 35.6 us -> 37.9 us
  waiting for transfers between devices: 8.9 us -> 6.96 us
  local copies, waits for them, and re-layouts: 0.03 us -> 1.16 us
  starting transfers between devices: 18.1 us -> 17.2 us
    pallas_call x3, Pallas kernels: 25 us -> 27.3 us  [cross_call(): pl.pallas_call(functools.partial(cross_kernel, last, with_sum, skipped, l...]
    ppermute x4, waiting for transfers between devices: 8.89 us -> 6.95 us  [round_win(): lax.ppermute(block, 'win', [(i, (i + shift) % count) for i in range(count)])]
    unnamed x8 -> x14, local copies, waits for them, and re-layouts: 0.02 us -> 1.15 us
    ppermute x4, starting transfers between devices: 6.17 us -> 5.25 us  [round_win(): lax.ppermute(block, 'win', [(i, (i + shift) % count) for i in range(count)])]
  transfers between devices with their start and end apart: 7 -> 7, of which waited for: 3 -> 3; matrix products, arithmetic and copies ran while one was open for 0% -> 0% of each run, Pallas kernels for 39% -> 42%
where the time goes in v5:
time: 65.1 us; the launch traced here: 64.9 us
  Pallas kernels  37.9 us (58%)
  starting transfers between devices  17.2 us (26%)
  waiting for transfers between devices  6.96 us (11%)
  local copies, waits for them, and re-layouts  1.16 us (2%)
  other arithmetic  0.79 us (1%)
  between operations  0.79 us (1%)
    pallas_call x3, Pallas kernels, cross_call(): pl.pallas_call(functools.partial(cross_kernel, last, with_sum, skipped, l...  27.3 us
    all_to_all x1, starting transfers between devices, local(): lax.all_to_all(outgoing, 'chan', split_axis=0, concat_axis=0, tiled=True)  9.26 us
    pallas_call x1, Pallas kernels, spectra_call(): pl.pallas_call(spectra_kernel, in_specs=[smem_spec()] + [anywhere] * 5, o...  9.22 us
    ppermute x4, waiting for transfers between devices, round_win(): lax.ppermute(block, 'win', [(i, (i + shift) % count) for i in range(count)])  6.95 us
    ppermute x4, starting transfers between devices, round_win(): lax.ppermute(block, 'win', [(i, (i + shift) % count) for i in range(count)])  5.25 us
    ppermute x2, starting transfers between devices, from_above(): return lax.ppermute(block, 'chan', [(i, i - 1) for i in range(1, count)])  2.72 us
    pallas_call x1, Pallas kernels, fold_call(): pl.pallas_call(fold_kernel, in_specs=[smem_spec()] + [vmem_spec()] * 5 +...  1.41 us
  transfers between devices with their start and end apart: 7, of which 3 were waited for; matrix products, arithmetic and copies ran while one was open for 0% of the time, Pallas kernels for 42%

profile of v5, /device:TPU:0, one launch (start us, length us, event | category | flops | bytes accessed | tf_op | source)
XLA Modules:
  0.0 64.9 jit_solution(9113299803075806915)
XLA Ops:
  0.6 9.2 %spectra.1 = (bf16[384,512]{1,0:T(8,128)(2,1)}, bf16[384,512]{1,0:T(8,128)(2,1)}, bf16[768,512]{1,0:T(8,128)(2,1)}, bf16[16,96,512]{2,1,0:T(8,128)(2,1)}, bf16[1...) custom-call(s32[1]{0:T(128)} %bitcast.1.chan_ref, bf16[768,4096]{1,0:T(8,128)(2,1)} %bitcast.12, ...), custom_call_target="tpu_custom_call" | custom-call | flops 3221225472 | bytes 6291456 | tf_op jit(solution)/shard_map/spectra/pallas_call | solution.py:282
  9.9 0.0 copy-start.6
  9.9 0.0 copy-start.5
  9.9 0.0 copy-start.4
  9.9 1.4 %collective-permute-start.1 = (bf16[6,64,512]{2,1,0:T(8,128)(2,1)}, bf16[6,64,512]{2,1,0:T(8,128)(2,1)S(1)}, u32[]{:S(2)}, u32[]{:S(2)}) collective-permute-start(bf16[6,64,512]{2,1,0:T(8,128)(2,1)} %bitcast.14), channel_id=1, source_target_pairs={{2,0},{4,2},{6,4},{8,6},{10,8},{12,10},{14,12},{16,14},{18,16},{20... | collective-permute-start | bytes 1179656 | tf_op jit(solution)/shard_map/ppermute | solution.py:526
  11.3 1.3 %collective-permute-start.2 = (bf16[6,64,512]{2,1,0:T(8,128)(2,1)}, bf16[6,64,512]{2,1,0:T(8,128)(2,1)S(1)}, u32[]{:S(2)}, u32[]{:S(2)}) collective-permute-start(bf16[6,64,512]{2,1,0:T(8,128)(2,1)} %bitcast.13), channel_id=1, source_target_pairs={{2,0},{4,2},{6,4},{8,6},{10,8},{12,10},{14,12},{16,14},{18,16},{20... | collective-permute-start | bytes 1179656 | tf_op jit(solution)/shard_map/ppermute | solution.py:526
  12.6 9.3 %all-to-all-start = ((bf16[16,96,512]{2,1,0:T(8,128)(2,1)}), bf16[16,96,512]{2,1,0:T(8,128)(2,1)S(1)}, u32[]{:S(2)}, u32[]{:S(2)}) async-start(bf16[16,96,512]{2,1,0:T(8,128)(2,1)} %get-tuple-element.25), calls=%async_computation | async-start | bytes 3145728 | tf_op jit(solution)/shard_map/all_to_all | solution.py:557
  21.9 0.0 copy-done.6
  21.9 1.5 %collective-permute-start = (bf16[12,32,512]{2,1,0:T(8,128)(2,1)S(1)}, bf16[12,32,512]{2,1,0:T(8,128)(2,1)S(1)}, u32[]{:S(2)}, u32[]{:S(2)}) collective-permute-start(bf16[12,32,512]{2,1,0:T(8,128)(2,1)S(1)} %copy-done.6), channel_id=1, source_target_pairs={{0,1},{1,0},{2,3},{3,2},{4,5},{5,4},{6,7},{7,6},{8,9},{9,8},{10,11... | collective-permute-start | bytes 1179656 | tf_op jit(solution)/shard_map/ppermute | solution.py:531
  23.5 0.0 collective-permute-done.1.refs_1_
  23.5 0.0 copy-done.5
  23.5 0.1 fusion
  23.6 0.6 collective-permute-start.4
  24.2 0.0 collective-permute-done.2.refs_2_
  24.2 0.0 copy-done.4
  24.2 0.1 fusion.1.refs_3_
  24.3 0.0 copy-start.3
  24.3 1.1 %copy-done.3 = bf16[768,512]{1,0:T(8,128)(2,1)S(1)} copy-done((bf16[768,512]{1,0:T(8,128)(2,1)S(1)}, bf16[768,512]{1,0:T(8,128)(2,1)}, u32[]{:S(2)}) %copy-start.3) | copy-done | bytes 786456
  25.4 11.9 %cross.3 = (f32[32,72,256]{2,1,0:T(8,128)S(1)}, s32[1]{0:T(128)}, bf16[6,64,512]{2,1,0:T(8,128)(2,1)S(1)}) custom-call(s32[1]{0:T(128)} %bitcast.win_ref, bf16[12,64,512]{2,1,0:T(8,128)(2,1)S(1)} %bitcast.11, bf16[6,64,512]{2,1,0:T(8,128)(2,1)S(1)} %collective-permute-done.1.refs_1_, ...), custom_call_target="tpu_custom_call", output_to_operand_aliasing={{2}: (4, {})} | custom-call | flops 30000001024 | bytes 4718592 | tf_op jit(solution)/shard_map/cross/pallas_call | solution.py:457
  37.3 1.5 %collective-permute-start.3 = (bf16[6,64,512]{2,1,0:T(8,128)(2,1)S(1)}, bf16[6,64,512]{2,1,0:T(8,128)(2,1)S(1)}, u32[]{:S(2)}, u32[]{:S(2)}) collective-permute-start(bf16[6,64,512]{2,1,0:T(8,128)(2,1)S(1)} %get-tuple-element.20), channel_id=1, source_target_pairs={{0,1},{1,0},{2,3},{3,2},{4,5},{5,4},{6,7},{7,6},{8,9},{9,8},{10,11... | collective-permute-start | bytes 1179656 | tf_op jit(solution)/shard_map/ppermute | solution.py:531
  38.8 0.0 collective-permute-done.refs_0_
  38.8 3.5 %collective-permute-done.4.refs_1_ = bf16[6,64,512]{2,1,0:T(8,128)(2,1)S(1)} collective-permute-done((bf16[6,64,512]{2,1,0:T(8,128)(2,1)S(1)}, bf16[6,64,512]{2,1,0:T(8,128)(2,1)S(1)}, u32[]{:S(2)}, u32[]{:S(2)}) %collective-permute-start.4) | collective-permute-done | bytes 393248 | tf_op jit(solution)/shard_map/ppermute | solution.py:531
  42.3 0.0 copy-start
  42.3 6.9 %cross.4 = (f32[32,72,256]{2,1,0:T(8,128)S(1)}, s32[1]{0:T(128)}, bf16[768,512]{1,0:T(8,128)(2,1)S(1)}) custom-call(s32[1]{0:T(128)} %bitcast.win_ref, bf16[12,32,512]{2,1,0:T(8,128)(2,1)S(1)} %collective-permute-done.refs_0_, bf16[6,64,512]{2,1,0:T(8,128)(2,1)S(1)} %collective-permute-done.4.refs_1_, bf16[768,512]{1,0:T(8,128)(2,1)S(1)} %copy-done.3, ...), custom_call_target="tpu_custom_call" | custom-call | flops 15000000512 | bytes 3538944 | tf_op jit(solution)/shard_map/cross/pallas_call | solution.py:457
  49.2 1.0 %collective-permute-done.3.refs_1_ = bf16[6,64,512]{2,1,0:T(8,128)(2,1)S(1)} collective-permute-done((bf16[6,64,512]{2,1,0:T(8,128)(2,1)S(1)}, bf16[6,64,512]{2,1,0:T(8,128)(2,1)S(1)}, u32[]{:S(2)}, u32[]{:S(2)}) %collective-permute-start.3) | collective-permute-done | bytes 393248 | tf_op jit(solution)/shard_map/ppermute | solution.py:531
  50.3 0.0 copy-done
  50.3 0.0 copy-start.1
  50.3 0.0 copy-start.2
  50.3 8.5 %cross.5 = (f32[32,64,256]{2,1,0:T(8,128)}, s32[1]{0:T(128)}) custom-call(s32[1]{0:T(128)} %bitcast.win_ref, bf16[12,32,512]{2,1,0:T(8,128)(2,1)S(1)} %collective-permute-done.refs_0_, bf16[6,64,512]{2,1,0:T(8,128)(2,1)S(1)} %collective-permute-done.3.refs_1_, f32[32,72,256]{2,1,0:T(8,128)S(1)} %get-tuple-element.23.refs_2_, bf16[256,256]{1,0:T(8,128)(2,1)S(1)} %copy-done), custom_call_target="tpu_custom_call" | custom-call | flops 15000000512 | bytes 3538944 | tf_op jit(solution)/shard_map/cross/pallas_call | solution.py:457
  58.8 0.0 all-to-all-done.incoming_ref
  58.8 0.0 copy-done.1
  58.8 0.0 copy-done.2
  58.8 1.4 %fold.1 = f32[64,256]{1,0:T(8,128)S(1)} custom-call(s32[1]{0:T(128)} %bitcast.1.chan_ref, bf16[16,96,512]{2,1,0:T(8,128)(2,1)S(1)} %all-to-all-done.incoming_ref, bf16[768,512]{1,0:T(8,128)(2,1)S(1)} %get-tuple-element.26.own_ref, s32[8,128]{1,0:T(8,128)S(1)} %bitcast.10, bf16[256,256]{1,0:T(8,128)(2,1)S(1)} %copy-done, bf16[256,256]{1,0:T(8,128)(2,1)S(1)} %copy-done.1, ...), custom_call_target="tpu_custom_call" | custom-call | flops 201326592 | bytes 2359296 | tf_op jit(solution)/shard_map/fold/pallas_call | solution.py:511
  60.3 1.5 %collective-permute-start.5 = (f32[32,256]{1,0:T(8,128)S(1)}, f32[32,256]{1,0:T(8,128)S(1)}, u32[]{:S(2)}, u32[]{:S(2)}) collective-permute-start(f32[32,256]{1,0:T(8,128)S(1)} %constant_dynamic-slice_fusion), channel_id=1, source_target_pairs={{0,1},{1,0},{2,3},{3,2},{4,5},{5,4},{6,7},{7,6},{8,9},{9,8},{10,11... | collective-permute-start | bytes 98312 | tf_op jit(solution)/shard_map/ppermute | solution.py:531
  61.8 2.4 %collective-permute-done.5 = f32[32,256]{1,0:T(8,128)S(1)} collective-permute-done((f32[32,256]{1,0:T(8,128)S(1)}, f32[32,256]{1,0:T(8,128)S(1)}, u32[]{:S(2)}, u32[]{:S(2)}) %collective-permute-start.5) | collective-permute-done | bytes 32800 | tf_op jit(solution)/shard_map/ppermute | solution.py:531
  64.2 0.6 dynamic-slice_add_fusion
  (1 shorter events, 0.0 us)
Async XLA Ops:
  9.9 12.0 %copy-start.6 = (bf16[12,32,512]{2,1,0:T(8,128)(2,1)S(1)}, bf16[12,32,512]{2,1,0:T(8,128)(2,1)}, u32[]{:S(2)}) copy-start(bf16[12,32,512]{2,1,0:T(8,128)(2,1)} %get-tuple-element.15) | copy-start | bytes 1179652
  9.9 13.6 %copy-start.5 = (bf16[6,32,512]{2,1,0:T(8,128)(2,1)S(1)}, bf16[6,32,512]{2,1,0:T(8,128)(2,1)}, u32[]{:S(2)}) copy-start(bf16[6,32,512]{2,1,0:T(8,128)(2,1)} %get-tuple-element.21) | copy-start | bytes 589828
  9.9 14.3 %copy-start.4 = (bf16[6,32,512]{2,1,0:T(8,128)(2,1)S(1)}, bf16[6,32,512]{2,1,0:T(8,128)(2,1)}, u32[]{:S(2)}) copy-start(bf16[6,32,512]{2,1,0:T(8,128)(2,1)} %get-tuple-element.19) | copy-start | bytes 589828
  9.9 13.6 %collective-permute-start.1 = (bf16[6,64,512]{2,1,0:T(8,128)(2,1)}, bf16[6,64,512]{2,1,0:T(8,128)(2,1)S(1)}, u32[]{:S(2)}, u32[]{:S(2)}) collective-permute-start(bf16[6,64,512]{2,1,0:T(8,128)(2,1)} %bitcast.14), channel_id=1, source_target_pairs={{2,0},{4,2},{6,4},{8,6},{10,8},{12,10},{14,12},{16,14},{18,16},{20... | collective-permute-start | bytes 1179656 | tf_op jit(solution)/shard_map/ppermute | solution.py:526
  11.3 12.8 %collective-permute-start.2 = (bf16[6,64,512]{2,1,0:T(8,128)(2,1)}, bf16[6,64,512]{2,1,0:T(8,128)(2,1)S(1)}, u32[]{:S(2)}, u32[]{:S(2)}) collective-permute-start(bf16[6,64,512]{2,1,0:T(8,128)(2,1)} %bitcast.13), channel_id=1, source_target_pairs={{2,0},{4,2},{6,4},{8,6},{10,8},{12,10},{14,12},{16,14},{18,16},{20... | collective-permute-start | bytes 1179656 | tf_op jit(solution)/shard_map/ppermute | solution.py:526
  12.6 46.2 %all-to-all-start = ((bf16[16,96,512]{2,1,0:T(8,128)(2,1)}), bf16[16,96,512]{2,1,0:T(8,128)(2,1)S(1)}, u32[]{:S(2)}, u32[]{:S(2)}) async-start(bf16[16,96,512]{2,1,0:T(8,128)(2,1)} %get-tuple-element.25), calls=%async_computation | async-start | bytes 3145728 | tf_op jit(solution)/shard_map/all_to_all | solution.py:557
  21.9 16.9 %collective-permute-start = (bf16[12,32,512]{2,1,0:T(8,128)(2,1)S(1)}, bf16[12,32,512]{2,1,0:T(8,128)(2,1)S(1)}, u32[]{:S(2)}, u32[]{:S(2)}) collective-permute-start(bf16[12,32,512]{2,1,0:T(8,128)(2,1)S(1)} %copy-done.6), channel_id=1, source_target_pairs={{0,1},{1,0},{2,3},{3,2},{4,5},{5,4},{6,7},{7,6},{8,9},{9,8},{10,11... | collective-permute-start | bytes 1179656 | tf_op jit(solution)/shard_map/ppermute | solution.py:531
  23.6 18.8 %collective-permute-start.4 = (bf16[6,64,512]{2,1,0:T(8,128)(2,1)S(1)}, bf16[6,64,512]{2,1,0:T(8,128)(2,1)S(1)}, u32[]{:S(2)}, u32[]{:S(2)}) collective-permute-start(bf16[6,64,512]{2,1,0:T(8,128)(2,1)S(1)} %fusion), channel_id=1, source_target_pairs={{0,1},{1,0},{2,3},{3,2},{4,5},{5,4},{6,7},{7,6},{8,9},{9,8},{10,11... | collective-permute-start | bytes 1179656 | tf_op jit(solution)/shard_map/ppermute | solution.py:531
  24.3 1.1 %copy-start.3 = (bf16[768,512]{1,0:T(8,128)(2,1)S(1)}, bf16[768,512]{1,0:T(8,128)(2,1)}, u32[]{:S(2)}) copy-start(bf16[768,512]{1,0:T(8,128)(2,1)} %get-tuple-element.16.refs_2_) | copy-start | bytes 2359300
  37.3 13.0 %collective-permute-start.3 = (bf16[6,64,512]{2,1,0:T(8,128)(2,1)S(1)}, bf16[6,64,512]{2,1,0:T(8,128)(2,1)S(1)}, u32[]{:S(2)}, u32[]{:S(2)}) collective-permute-start(bf16[6,64,512]{2,1,0:T(8,128)(2,1)S(1)} %get-tuple-element.20), channel_id=1, source_target_pairs={{0,1},{1,0},{2,3},{3,2},{4,5},{5,4},{6,7},{7,6},{8,9},{9,8},{10,11... | collective-permute-start | bytes 1179656 | tf_op jit(solution)/shard_map/ppermute | solution.py:531
  42.3 8.0 %copy-start = (bf16[256,256]{1,0:T(8,128)(2,1)S(1)}, bf16[256,256]{1,0:T(8,128)(2,1)}, u32[]{:S(2)}) copy-start(bf16[256,256]{1,0:T(8,128)(2,1)} %constant.39.clone.refs_3_.high_ref) | copy-start | bytes 393220
  50.3 8.5 %copy-start.1 = (bf16[256,256]{1,0:T(8,128)(2,1)S(1)}, bf16[256,256]{1,0:T(8,128)(2,1)}, u32[]{:S(2)}) copy-start(bf16[256,256]{1,0:T(8,128)(2,1)} %constant.40.clone.low_ref) | copy-start | bytes 393220
  50.3 8.5 %copy-start.2 = (s32[1024,1]{0,1:T(1,128)S(1)}, s32[1024,1]{0,1:T(1,128)}, u32[]{:S(2)}) copy-start(s32[1024,1]{0,1:T(1,128)} %param.9) | copy-start | bytes 12292
  60.3 4.0 %collective-permute-start.5 = (f32[32,256]{1,0:T(8,128)S(1)}, f32[32,256]{1,0:T(8,128)S(1)}, u32[]{:S(2)}, u32[]{:S(2)}) collective-permute-start(f32[32,256]{1,0:T(8,128)S(1)} %constant_dynamic-slice_fusion), channel_id=1, source_target_pairs={{0,1},{1,0},{2,3},{3,2},{4,5},{5,4},{6,7},{7,6},{8,9},{9,8},{10,11... | collective-permute-start | bytes 98312 | tf_op jit(solution)/shard_map/ppermute | solution.py:531

commit v6 on v4

--- a/solution.py
+++ b/solution.py
@@ -137,7 +137,7 @@
     )
 
 
-def spectra_kernel(chan_ref, traces_ref, table_ref, quality_ref, owners_ref, places_ref, *refs):
+def spectra_kernel(traces_ref, table_ref, quality_ref, owners_ref, places_ref, *refs):
     early_ref, late_ref, whitened_ref, outgoing_ref, *row_refs = refs[:-14]
     traces, table, quality, owners, places, band, keep_rows, products, white, white_windows, sent, selector, sems, out_sems = refs[-14:]
     row_parts, chunks, rows, depth = traces.shape
@@ -174,7 +174,7 @@
             jnp.where(within(rows_of(shape), ch_dev) == lanes_of(shape), quality[...].astype(jnp.float32), 0.0),
             axis=1, keepdims=True,
         )
-        selector[...] = slot_selector(owners[...], places[...], chan_ref[0], ch_dev)
+        selector[...] = slot_selector(owners[...], places[...], lax.axis_index("chan"), ch_dev)
         keep_rows[...] = jnp.broadcast_to(keep, keep_rows.shape)
 
     def transform(part):
@@ -259,7 +259,7 @@
     return pl.BlockSpec(array.shape, lambda s: (0,) * array.ndim)
 
 
-def spectra_call(chan, traces, quality, owners, places, chan_count, own_count):
+def spectra_call(traces, quality, owners, places, chan_count, own_count):
     rows, length = traces.shape
     ch_dev = quality.shape[1]
     row_steps = rows // (2 * ch_dev)
@@ -281,7 +281,7 @@
         ]
     return pl.pallas_call(
         spectra_kernel,
-        in_specs=[smem_spec()] + [anywhere] * 5,
+        in_specs=[anywhere] * 5,
         out_specs=[anywhere] * len(out_shape),
         out_shape=out_shape,
         scratch_shapes=[
@@ -305,23 +305,23 @@
             flops=2 * rows * length * 2 * F, bytes_accessed=2 * rows * length, transcendentals=rows * F
         ),
         name="spectra",
-    )(chan, traces, jnp.asarray(forward_table(length)), quality, owners, places)
-
-
-def cross_kernel(last, with_sum, skipped, through, win_ref, *refs):
+    )(traces, jnp.asarray(forward_table(length)), quality, owners, places)
+
+
+def cross_kernel(last, with_sum, skipped, through, *refs):
     refs = list(refs)
     blocks = [refs.pop(0) for _ in range(2 if with_sum else 3)]
     refs = refs[through:]
     sum_ref = refs.pop(0) if with_sum else None
     if last:
-        table_ref, out_ref, zero_ref, wide, spread, total, lags, sems = refs
+        table_ref, out_ref, done_ref, wide, spread, total, lags, sems = refs
+        done_ref[...] = jnp.zeros_like(done_ref)
     else:
-        total, zero_ref, *refs = refs
+        total, *refs = refs
         wide, spread = refs[through:]
-    zero_ref[0] = 0
     windows, own_count = spread.shape[:2]
     ch_dev = wide.shape[1] // 2
-    base = pl.multiple_of(win_ref[0] * own_count, 8)
+    base = pl.multiple_of(lax.axis_index("win") * own_count, 8)
 
     def widen(w, carry):
         if with_sum:
@@ -406,13 +406,13 @@
             copy.wait()
 
 
-def cross_call(win, blocks, windows, ch_dev, own_count, sums, table, skipped, share, through=()):
+def cross_call(blocks, windows, ch_dev, own_count, sums, table, skipped, share, through=()):
     columns = 2 * F
     last = table is not None
     with_sum = sums is not None
-    operands = [win, *blocks, *through]
+    operands = [*blocks, *through]
     anywhere = [pl.BlockSpec(memory_space=pl.ANY)] * len(through)
-    in_specs = [smem_spec()] + [vmem_spec()] * len(blocks) + anywhere
+    in_specs = [vmem_spec()] * len(blocks) + anywhere
     if with_sum:
         operands.append(sums)
     scratch = [
@@ -427,13 +427,16 @@
             pltpu.SemaphoreType.DMA((own_count // 8,)),
         ]
     shape = (own_count, REACH, NLAG) if last else (own_count, SPAN, F)
-    out_shape = [jax.ShapeDtypeStruct(shape, jnp.float32), jax.ShapeDtypeStruct((1,), jnp.int32)]
-    out_specs = [pl.BlockSpec(memory_space=pl.ANY) if last else vmem_spec(), smem_spec()] + anywhere
+    out_shape = [jax.ShapeDtypeStruct(shape, jnp.float32)]
+    out_specs = [pl.BlockSpec(memory_space=pl.ANY) if last else vmem_spec()] + anywhere
+    if last:
+        out_shape.append(jax.ShapeDtypeStruct((8, H), jnp.float32))
+        out_specs.append(vmem_spec())
     out_shape += [jax.ShapeDtypeStruct(array.shape, array.dtype) for array in through]
     return pl.pallas_call(
         functools.partial(cross_kernel, last, with_sum, skipped, len(through)),
         in_specs=in_specs + [vmem_spec()] * (len(operands) - len(in_specs)),
-        input_output_aliases={1 + len(blocks) + n: 2 + n for n in range(len(through))},
+        input_output_aliases={len(blocks) + n: 1 + n for n in range(len(through))},
         out_specs=out_specs,
         out_shape=out_shape,
         scratch_shapes=scratch,
@@ -445,14 +448,14 @@
     )(*operands)
 
 
-def fold_kernel(chan_ref, incoming_ref, own_ref, owners_ref, high_ref, low_ref, earlier_ref, out_ref):
+def fold_kernel(incoming_ref, own_ref, owners_ref, high_ref, low_ref, earlier_ref, out_ref):
     ch_dev = out_ref.shape[0]
     rows = 2 * ch_dev
     pairs = own_ref.shape[0] // rows
     count, slots, columns = incoming_ref.shape
     owners = owners_ref[...].astype(jnp.float32)
     per_row = owners.shape[1] // ch_dev
-    device = chan_ref[0]
+    device = lax.axis_index("chan")
     line = jnp.sum(jnp.where(rows_of(owners.shape) == device // per_row, owners, 0.0), axis=0, keepdims=True)
     shape = (rows, owners.shape[1])
     line = jnp.broadcast_to(line, shape)
@@ -483,10 +486,10 @@
     out_ref[...] = lag_transform(stacks, high_ref[...], low_ref[...])
 
 
-def fold_call(chan, incoming, own, owners, ch_dev, tables, earlier):
+def fold_call(incoming, own, owners, ch_dev, tables, earlier):
     return pl.pallas_call(
         fold_kernel,
-        in_specs=[smem_spec()] + [vmem_spec()] * 5 + [smem_spec()],
+        in_specs=[vmem_spec()] * 5 + [pl.BlockSpec(memory_space=pl.ANY)],
         out_specs=vmem_spec(),
         out_shape=jax.ShapeDtypeStruct((ch_dev, NLAG), jnp.float32),
         compiler_params=pltpu.CompilerParams(vmem_limit_bytes=FOLD_VMEM_LIMIT),
@@ -494,7 +497,7 @@
             flops=4 * ch_dev * incoming.size, bytes_accessed=2 * (incoming.size + own.size), transcendentals=0
         ),
         name="fold",
-    )(chan, incoming, own, owners, *tables, earlier)
+    )(incoming, own, owners, *tables, earlier)
 
 
 def from_above(block):
@@ -514,13 +517,11 @@
     window_part = lax.axis_index("win")
     own_count = ch_dev // win_count
     shared = ch_dev - own_count
-    chan = lax.axis_index("chan").astype(jnp.int32).reshape(1)
-    win = window_part.astype(jnp.int32).reshape(1)
     tables = [jnp.asarray(t) for t in inverse_tables(1.0 / math.sqrt(F * win_dev * win_count))]
     owners = fold_block.reshape(-1, 2 * ch_dev)
     places = fold_offset.reshape(-1, 2 * ch_dev)
     early, late, flat, outgoing, *row_parts = spectra_call(
-        chan, traces.reshape(win_dev * ch_dev, length), quality.reshape(1, ch_dev), owners, places, chan_count, own_count
+        traces.reshape(win_dev * ch_dev, length), quality.reshape(1, ch_dev), owners, places, chan_count, own_count
     )
     half = win_dev // 2
     halves = [rows.reshape(half, ch_dev, 2 * F) for rows in (early, late)]
@@ -540,8 +541,8 @@
         ]
 
     sooner = [round_win(block, shift) for shift, block in enumerate(offers(0), 1)]
-    sums, _, *waiting = cross_call(
-        win, [flat.reshape(win_dev, ch_dev, 2 * F)] + upper, win_dev, ch_dev, own_count, None, None, 0, 1.0, through=offers(1)
+    sums, *waiting = cross_call(
+        [flat.reshape(win_dev, ch_dev, 2 * F)] + upper, win_dev, ch_dev, own_count, None, None, 0, 1.0, through=offers(1)
     )
     later = [round_win(block, shift) for shift, block in enumerate(waiting, 1)]
     arrived = []
@@ -549,8 +550,8 @@
         arrived += [([rows, block], n * half) for n, block in enumerate(others)]
     for n, (blocks, skipped) in enumerate(arrived):
         ends = tables[0] if n == len(arrived) - 1 else None
-        sums, done = cross_call(win, blocks, half, ch_dev, own_count, sums, ends, skipped, 0.5)
-    share = fold_call(chan, incoming, flat, owners, ch_dev, tables, done)
+        sums, *done = cross_call(blocks, half, ch_dev, own_count, sums, ends, skipped, 0.5)
+    share = fold_call(incoming, flat, owners, ch_dev, tables, done[0])
     fold = lax.dynamic_slice_in_dim(share, window_part * own_count, own_count, 0)
     for shift in range(1, win_count):
         target = (window_part + shift) % win_count * own_count

time: 64.5 us -> 63.4 us (0.983)
  Pallas kernels: 35.6 us -> 33.5 us
  waiting for transfers between devices: 8.9 us -> 9.87 us
    pallas_call x3, Pallas kernels: 25 us -> 23.5 us  [cross_call(): pl.pallas_call(functools.partial(cross_kernel, last, with_sum, skipped, l...]
    ppermute x4, waiting for transfers between devices: 8.89 us -> 9.87 us  [round_win(): lax.ppermute(block, 'win', [(i, (i + shift) % count) for i in range(count)])]
  transfers between devices with their start and end apart: 7 -> 7, of which waited for: 3 -> 3; matrix products, arithmetic and copies ran while one was open for 0% -> 0% of each run, Pallas kernels for 39% -> 37%
where the time goes in v6:
time: 63.4 us; the launch traced here: 63.1 us
  Pallas kernels  33.5 us (53%)
  starting transfers between devices  18.1 us (29%)
  waiting for transfers between devices  9.87 us (16%)
  other arithmetic  0.78 us (1%)
  between operations  0.77 us (1%)
    pallas_call x3, Pallas kernels, cross_call(): pl.pallas_call(functools.partial(cross_kernel, last, with_sum, skipped, l...  23.5 us
    ppermute x4, waiting for transfers between devices, round_win(): lax.ppermute(block, 'win', [(i, (i + shift) % count) for i in range(count)])  9.87 us
    all_to_all x1, starting transfers between devices, local(): lax.all_to_all(outgoing, 'chan', split_axis=0, concat_axis=0, tiled=True)  9.37 us
    pallas_call x1, Pallas kernels, spectra_call(): pl.pallas_call(spectra_kernel, in_specs=[anywhere] * 5, out_specs=[anywhe...  9.23 us
    ppermute x4, starting transfers between devices, round_win(): lax.ppermute(block, 'win', [(i, (i + shift) % count) for i in range(count)])  6.18 us
    ppermute x2, starting transfers between devices, from_above(): return lax.ppermute(block, 'chan', [(i, i - 1) for i in range(1, count)])  2.58 us
  transfers between devices with their start and end apart: 7, of which 3 were waited for; matrix products, arithmetic and copies ran while one was open for 0% of the time, Pallas kernels for 37%

profile of v6, /device:TPU:0, one launch (start us, length us, event | category | flops | bytes accessed | tf_op | source)
XLA Modules:
  0.0 63.1 jit_solution(14864073383404774077)
XLA Ops:
  0.6 9.2 %spectra.1 = (bf16[384,512]{1,0:T(8,128)(2,1)}, bf16[384,512]{1,0:T(8,128)(2,1)}, bf16[768,512]{1,0:T(8,128)(2,1)}, bf16[16,96,512]{2,1,0:T(8,128)(2,1)}, bf16[1...) custom-call(bf16[768,4096]{1,0:T(8,128)(2,1)} %bitcast.10, ...), custom_call_target="tpu_custom_call" | custom-call | flops 3221225472 | bytes 6291456 | tf_op jit(solution)/shard_map/spectra/pallas_call | solution.py:282
  9.9 1.3 %collective-permute-start.1 = (bf16[6,64,512]{2,1,0:T(8,128)(2,1)}, bf16[6,64,512]{2,1,0:T(8,128)(2,1)S(1)}, u32[]{:S(2)}, u32[]{:S(2)}) collective-permute-start(bf16[6,64,512]{2,1,0:T(8,128)(2,1)} %bitcast.12), channel_id=1, source_target_pairs={{2,0},{4,2},{6,4},{8,6},{10,8},{12,10},{14,12},{16,14},{18,16},{20... | collective-permute-start | bytes 1179656 | tf_op jit(solution)/shard_map/ppermute | solution.py:505
  11.2 1.3 %collective-permute-start.2 = (bf16[6,64,512]{2,1,0:T(8,128)(2,1)}, bf16[6,64,512]{2,1,0:T(8,128)(2,1)S(1)}, u32[]{:S(2)}, u32[]{:S(2)}) collective-permute-start(bf16[6,64,512]{2,1,0:T(8,128)(2,1)} %bitcast.11), channel_id=1, source_target_pairs={{2,0},{4,2},{6,4},{8,6},{10,8},{12,10},{14,12},{16,14},{18,16},{20... | collective-permute-start | bytes 1179656 | tf_op jit(solution)/shard_map/ppermute | solution.py:505
  12.5 0.0 copy-start
  12.5 9.4 %all-to-all-start = ((bf16[16,96,512]{2,1,0:T(8,128)(2,1)}), bf16[16,96,512]{2,1,0:T(8,128)(2,1)S(1)}, u32[]{:S(2)}, u32[]{:S(2)}) async-start(bf16[16,96,512]{2,1,0:T(8,128)(2,1)} %get-tuple-element.22), calls=%async_computation | async-start | bytes 3145728 | tf_op jit(solution)/shard_map/all_to_all | solution.py:534
  21.9 1.6 %collective-permute-start = (bf16[12,32,512]{2,1,0:T(8,128)(2,1)}, bf16[12,32,512]{2,1,0:T(8,128)(2,1)S(1)}, u32[]{:S(2)}, u32[]{:S(2)}) collective-permute-start(bf16[12,32,512]{2,1,0:T(8,128)(2,1)} %get-tuple-element.13), channel_id=1, source_target_pairs={{0,1},{1,0},{2,3},{3,2},{4,5},{5,4},{6,7},{7,6},{8,9},{9,8},{10,11... | collective-permute-start | bytes 1179656 | tf_op jit(solution)/shard_map/ppermute | solution.py:510
  23.4 0.0 collective-permute-done.1.refs_1_
  23.4 0.1 fusion
  23.5 1.5 %collective-permute-start.4 = (bf16[6,64,512]{2,1,0:T(8,128)(2,1)S(1)}, bf16[6,64,512]{2,1,0:T(8,128)(2,1)S(1)}, u32[]{:S(2)}, u32[]{:S(2)}) collective-permute-start(bf16[6,64,512]{2,1,0:T(8,128)(2,1)S(1)} %fusion), channel_id=1, source_target_pairs={{0,1},{1,0},{2,3},{3,2},{4,5},{5,4},{6,7},{7,6},{8,9},{9,8},{10,11... | collective-permute-start | bytes 1179656 | tf_op jit(solution)/shard_map/ppermute | solution.py:510
  25.0 0.0 collective-permute-done.2.refs_2_
  25.0 0.1 fusion.1.refs_3_
  25.1 0.0 copy-done
  25.1 10.5 %cross.3 = (f32[32,72,256]{2,1,0:T(8,128)S(1)}, bf16[6,64,512]{2,1,0:T(8,128)(2,1)S(1)}) custom-call(bf16[12,64,512]{2,1,0:T(8,128)(2,1)S(1)} %bitcast.7, bf16[6,64,512]{2,1,0:T(8,128)(2,1)S(1)} %collective-permute-done.1.refs_1_, bf16[6,64,512]{2,1,0:T(8,128)(2,1)S(1)} %collective-permute-done.2.refs_2_, ...), custom_call_target="tpu_custom_call", output_to_operand_aliasing={{1}: (3, {})} | custom-call | flops 30000001024 | bytes 3932160 | tf_op jit(solution)/shard_map/cross/pallas_call | solution.py:436
  35.7 1.6 %collective-permute-start.3 = (bf16[6,64,512]{2,1,0:T(8,128)(2,1)S(1)}, bf16[6,64,512]{2,1,0:T(8,128)(2,1)S(1)}, u32[]{:S(2)}, u32[]{:S(2)}) collective-permute-start(bf16[6,64,512]{2,1,0:T(8,128)(2,1)S(1)} %get-tuple-element.18), channel_id=1, source_target_pairs={{0,1},{1,0},{2,3},{3,2},{4,5},{5,4},{6,7},{7,6},{8,9},{9,8},{10,11... | collective-permute-start | bytes 1179656 | tf_op jit(solution)/shard_map/ppermute | solution.py:510
  37.2 0.0 collective-permute-done.refs_0_
  37.2 5.3 %collective-permute-done.4.refs_1_ = bf16[6,64,512]{2,1,0:T(8,128)(2,1)S(1)} collective-permute-done((bf16[6,64,512]{2,1,0:T(8,128)(2,1)S(1)}, bf16[6,64,512]{2,1,0:T(8,128)(2,1)S(1)}, u32[]{:S(2)}, u32[]{:S(2)}) %collective-permute-start.4) | collective-permute-done | bytes 393248 | tf_op jit(solution)/shard_map/ppermute | solution.py:510
  42.5 0.0 copy-start.1
  42.5 5.7 %cross.4.refs_2_ = f32[32,72,256]{2,1,0:T(8,128)S(1)} custom-call(bf16[12,32,512]{2,1,0:T(8,128)(2,1)S(1)} %collective-permute-done.refs_0_, bf16[6,64,512]{2,1,0:T(8,128)(2,1)S(1)} %collective-permute-done.4.refs_1_, f32[32,72,256]{2,1,0:T(8,128)S(1)} %get-tuple-element.20.refs_2_), custom_call_target="tpu_custom_call" | custom-call | flops 15000000512 | bytes 3145728 | tf_op jit(solution)/shard_map/cross/pallas_call | solution.py:436
  48.2 0.0 copy-start.2
  48.2 0.0 copy-start.3
  48.2 2.2 %collective-permute-done.3.refs_1_ = bf16[6,64,512]{2,1,0:T(8,128)(2,1)S(1)} collective-permute-done((bf16[6,64,512]{2,1,0:T(8,128)(2,1)S(1)}, bf16[6,64,512]{2,1,0:T(8,128)(2,1)S(1)}, u32[]{:S(2)}, u32[]{:S(2)}) %collective-permute-start.3) | collective-permute-done | bytes 393248 | tf_op jit(solution)/shard_map/ppermute | solution.py:510
  50.4 0.0 copy-done.1
  50.4 7.3 %cross.5 = (f32[32,64,256]{2,1,0:T(8,128)}, f32[8,128]{1,0:T(8,128)S(1)}) custom-call(bf16[12,32,512]{2,1,0:T(8,128)(2,1)S(1)} %collective-permute-done.refs_0_, bf16[6,64,512]{2,1,0:T(8,128)(2,1)S(1)} %collective-permute-done.3.refs_1_, f32[32,72,256]{2,1,0:T(8,128)S(1)} %cross.4.refs_2_, bf16[256,256]{1,0:T(8,128)(2,1)S(1)} %copy-done.1), custom_call_target="tpu_custom_call" | custom-call | flops 15000000512 | bytes 3145728 | tf_op jit(solution)/shard_map/cross/pallas_call | solution.py:436
  57.7 0.0 all-to-all-done.incoming_ref
  57.7 0.0 copy-done.2
  57.7 0.0 copy-done.3
  57.7 0.8 %fold.1 = f32[64,256]{1,0:T(8,128)S(1)} custom-call(bf16[16,96,512]{2,1,0:T(8,128)(2,1)S(1)} %all-to-all-done.incoming_ref, bf16[768,512]{1,0:T(8,128)(2,1)S(1)} %copy-done, s32[8,128]{1,0:T(8,128)S(1)} %bitcast.9, bf16[256,256]{1,0:T(8,128)(2,1)S(1)} %copy-done.1, bf16[256,256]{1,0:T(8,128)(2,1)S(1)} %copy-done.2, f32[8,128]{1,0:T(8,128)S(1)} %get-tuple-element.23.earlier_ref), custom_call_target="tpu_custom_call" | custom-call | flops 201326592 | bytes 2359296 | tf_op jit(solution)/shard_map/fold/pallas_call | solution.py:490
  58.5 1.6 %collective-permute-start.5 = (f32[32,256]{1,0:T(8,128)S(1)}, f32[32,256]{1,0:T(8,128)S(1)}, u32[]{:S(2)}, u32[]{:S(2)}) collective-permute-start(f32[32,256]{1,0:T(8,128)S(1)} %constant_dynamic-slice_fusion), channel_id=1, source_target_pairs={{0,1},{1,0},{2,3},{3,2},{4,5},{5,4},{6,7},{7,6},{8,9},{9,8},{10,11... | collective-permute-start | bytes 98312 | tf_op jit(solution)/shard_map/ppermute | solution.py:510
  60.1 2.4 %collective-permute-done.5 = f32[32,256]{1,0:T(8,128)S(1)} collective-permute-done((f32[32,256]{1,0:T(8,128)S(1)}, f32[32,256]{1,0:T(8,128)S(1)}, u32[]{:S(2)}, u32[]{:S(2)}) %collective-permute-start.5) | collective-permute-done | bytes 32800 | tf_op jit(solution)/shard_map/ppermute | solution.py:510
  62.5 0.6 dynamic-slice_add_fusion
  (1 shorter events, 0.0 us)
Async XLA Ops:
  9.9 13.5 %collective-permute-start.1 = (bf16[6,64,512]{2,1,0:T(8,128)(2,1)}, bf16[6,64,512]{2,1,0:T(8,128)(2,1)S(1)}, u32[]{:S(2)}, u32[]{:S(2)}) collective-permute-start(bf16[6,64,512]{2,1,0:T(8,128)(2,1)} %bitcast.12), channel_id=1, source_target_pairs={{2,0},{4,2},{6,4},{8,6},{10,8},{12,10},{14,12},{16,14},{18,16},{20... | collective-permute-start | bytes 1179656 | tf_op jit(solution)/shard_map/ppermute | solution.py:505
  11.2 13.9 %collective-permute-start.2 = (bf16[6,64,512]{2,1,0:T(8,128)(2,1)}, bf16[6,64,512]{2,1,0:T(8,128)(2,1)S(1)}, u32[]{:S(2)}, u32[]{:S(2)}) collective-permute-start(bf16[6,64,512]{2,1,0:T(8,128)(2,1)} %bitcast.11), channel_id=1, source_target_pairs={{2,0},{4,2},{6,4},{8,6},{10,8},{12,10},{14,12},{16,14},{18,16},{20... | collective-permute-start | bytes 1179656 | tf_op jit(solution)/shard_map/ppermute | solution.py:505
  12.5 12.7 %copy-start = (bf16[768,512]{1,0:T(8,128)(2,1)S(1)}, bf16[768,512]{1,0:T(8,128)(2,1)}, u32[]{:S(2)}) copy-start(bf16[768,512]{1,0:T(8,128)(2,1)} %get-tuple-element.14.own_ref) | copy-start | bytes 2359300
  12.5 45.2 %all-to-all-start = ((bf16[16,96,512]{2,1,0:T(8,128)(2,1)}), bf16[16,96,512]{2,1,0:T(8,128)(2,1)S(1)}, u32[]{:S(2)}, u32[]{:S(2)}) async-start(bf16[16,96,512]{2,1,0:T(8,128)(2,1)} %get-tuple-element.22), calls=%async_computation | async-start | bytes 3145728 | tf_op jit(solution)/shard_map/all_to_all | solution.py:534
  21.9 15.4 %collective-permute-start = (bf16[12,32,512]{2,1,0:T(8,128)(2,1)}, bf16[12,32,512]{2,1,0:T(8,128)(2,1)S(1)}, u32[]{:S(2)}, u32[]{:S(2)}) collective-permute-start(bf16[12,32,512]{2,1,0:T(8,128)(2,1)} %get-tuple-element.13), channel_id=1, source_target_pairs={{0,1},{1,0},{2,3},{3,2},{4,5},{5,4},{6,7},{7,6},{8,9},{9,8},{10,11... | collective-permute-start | bytes 1179656 | tf_op jit(solution)/shard_map/ppermute | solution.py:510
  23.5 19.0 %collective-permute-start.4 = (bf16[6,64,512]{2,1,0:T(8,128)(2,1)S(1)}, bf16[6,64,512]{2,1,0:T(8,128)(2,1)S(1)}, u32[]{:S(2)}, u32[]{:S(2)}) collective-permute-start(bf16[6,64,512]{2,1,0:T(8,128)(2,1)S(1)} %fusion), channel_id=1, source_target_pairs={{0,1},{1,0},{2,3},{3,2},{4,5},{5,4},{6,7},{7,6},{8,9},{9,8},{10,11... | collective-permute-start | bytes 1179656 | tf_op jit(solution)/shard_map/ppermute | solution.py:510
  35.7 14.7 %collective-permute-start.3 = (bf16[6,64,512]{2,1,0:T(8,128)(2,1)S(1)}, bf16[6,64,512]{2,1,0:T(8,128)(2,1)S(1)}, u32[]{:S(2)}, u32[]{:S(2)}) collective-permute-start(bf16[6,64,512]{2,1,0:T(8,128)(2,1)S(1)} %get-tuple-element.18), channel_id=1, source_target_pairs={{0,1},{1,0},{2,3},{3,2},{4,5},{5,4},{6,7},{7,6},{8,9},{9,8},{10,11... | collective-permute-start | bytes 1179656 | tf_op jit(solution)/shard_map/ppermute | solution.py:510
  42.5 7.9 %copy-start.1 = (bf16[256,256]{1,0:T(8,128)(2,1)S(1)}, bf16[256,256]{1,0:T(8,128)(2,1)}, u32[]{:S(2)}) copy-start(bf16[256,256]{1,0:T(8,128)(2,1)} %constant.35.clone.refs_3_.high_ref) | copy-start | bytes 393220
  48.2 9.5 %copy-start.2 = (bf16[256,256]{1,0:T(8,128)(2,1)S(1)}, bf16[256,256]{1,0:T(8,128)(2,1)}, u32[]{:S(2)}) copy-start(bf16[256,256]{1,0:T(8,128)(2,1)} %constant.36.clone.low_ref) | copy-start | bytes 393220
  48.2 9.5 %copy-start.3 = (s32[1024,1]{0,1:T(1,128)S(1)}, s32[1024,1]{0,1:T(1,128)}, u32[]{:S(2)}) copy-start(s32[1024,1]{0,1:T(1,128)} %param.9) | copy-start | bytes 12292
  58.5 4.0 %collective-permute-start.5 = (f32[32,256]{1,0:T(8,128)S(1)}, f32[32,256]{1,0:T(8,128)S(1)}, u32[]{:S(2)}, u32[]{:S(2)}) collective-permute-start(f32[32,256]{1,0:T(8,128)S(1)} %constant_dynamic-slice_fusion), channel_id=1, source_target_pairs={{0,1},{1,0},{2,3},{3,2},{4,5},{5,4},{6,7},{7,6},{8,9},{9,8},{10,11... | collective-permute-start | bytes 98312 | tf_op jit(solution)/shard_map/ppermute | solution.py:510

commit v7 on v6

--- a/solution.py
+++ b/solution.py
@@ -210,9 +210,8 @@
             sent[part, :, 2 * CAP * n : 2 * CAP * (n + 1), :] = chosen.reshape(count, 2 * CAP, chosen.shape[-1])
 
     def leave(part):
-        late, place = divmod(part, row_parts // 2)
+        pairs = rows // pair
         copies = [
-            (white.at[part], (early_ref, late_ref)[late].at[pl.ds(place * rows, rows), :]),
             (sent.at[part], outgoing_ref.at[:, pl.ds(part * slots, slots), :]),
             (white.at[part], whitened_ref.at[pl.ds(part * rows, rows), :]),
         ]
@@ -220,17 +219,21 @@
             shared_ref, *lower_refs = row_refs
             height = shared_ref.shape[1]
             split = ch_dev - height
-            count_here = rows // ch_dev
-            copies += [
-                (
-                    white_windows.at[part, :, pl.ds(split, height), :],
-                    shared_ref.at[pl.ds(part * count_here, count_here)],
-                ),
-                (
-                    white_windows.at[part, :, pl.ds(0, split), :],
-                    lower_refs[late].at[pl.ds(place * count_here, count_here)],
-                ),
-            ]
+            copies.append(
+                (white_windows.at[part, :, pl.ds(split, height), :], shared_ref.at[pl.ds(2 * pairs * part, 2 * pairs)])
+            )
+        for n in range(pairs):
+            late, place = divmod(part * pairs + n, row_parts * pairs // 2)
+            copies.append(
+                (white.at[part, pl.ds(n * pair, pair), :], (early_ref, late_ref)[late].at[pl.ds(place * pair, pair), :])
+            )
+            if row_refs:
+                copies.append(
+                    (
+                        white_windows.at[part, pl.ds(2 * n, 2), pl.ds(0, split), :],
+                        lower_refs[late].at[pl.ds(2 * place, 2)],
+                    )
+                )
         for n, (source, target) in enumerate(copies):
             leaving.append(pltpu.make_async_copy(source, target, out_sems.at[part, n]))
             leaving[-1].start()
@@ -262,7 +265,7 @@
 def spectra_call(traces, quality, owners, places, chan_count, own_count):
     rows, length = traces.shape
     ch_dev = quality.shape[1]
-    row_steps = rows // (2 * ch_dev)
+    row_steps = rows // (4 * ch_dev) if rows % (4 * ch_dev) == 0 else rows // (2 * ch_dev)
     part, depth = rows // row_steps, length // QUARTERS
     slots = part // (2 * ch_dev) * 2 * CAP
     anywhere = pl.BlockSpec(memory_space=pl.ANY)
@@ -298,7 +301,7 @@
             pltpu.VMEM((row_steps, chan_count, slots, 2 * F), jnp.bfloat16),
             pltpu.VMEM((chan_count * 2 * CAP, 2 * ch_dev), jnp.bfloat16),
             pltpu.SemaphoreType.DMA((row_steps + 1, QUARTERS)),
-            pltpu.SemaphoreType.DMA((row_steps, 5)),
+            pltpu.SemaphoreType.DMA((row_steps, 3 + 2 * (part // (2 * ch_dev)))),
         ],
         compiler_params=pltpu.CompilerParams(vmem_limit_bytes=SPECTRA_VMEM_LIMIT),
         cost_estimate=pl.CostEstimate(

time: 63.4 us -> 63.1 us (level)
  no operation moved by 1% of the time
where the time goes in v7:
time: 63.1 us; the launch traced here: 62.8 us
  Pallas kernels  33.2 us (53%)
  starting transfers between devices  18.1 us (29%)
  waiting for transfers between devices  9.88 us (16%)
  other arithmetic  0.78 us (1%)
  between operations  0.77 us (1%)
    pallas_call x3, Pallas kernels, cross_call(): pl.pallas_call(functools.partial(cross_kernel, last, with_sum, skipped, l...  23.5 us
    ppermute x4, waiting for transfers between devices, round_win(): lax.ppermute(block, 'win', [(i, (i + shift) % count) for i in range(count)])  9.87 us
    all_to_all x1, starting transfers between devices, local(): lax.all_to_all(outgoing, 'chan', split_axis=0, concat_axis=0, tiled=True)  9.38 us
    pallas_call x1, Pallas kernels, spectra_call(): pl.pallas_call(spectra_kernel, in_specs=[anywhere] * 5, out_specs=[anywhe...  8.92 us
    ppermute x4, starting transfers between devices, round_win(): lax.ppermute(block, 'win', [(i, (i + shift) % count) for i in range(count)])  6.17 us
    ppermute x2, starting transfers between devices, from_above(): return lax.ppermute(block, 'chan', [(i, i - 1) for i in range(1, count)])  2.58 us
  transfers between devices with their start and end apart: 7, of which 3 were waited for; matrix products, arithmetic and copies ran while one was open for 0% of the time, Pallas kernels for 37%

profile of v7, /device:TPU:0, one launch (start us, length us, event | category | flops | bytes accessed | tf_op | source)
XLA Modules:
  0.0 62.8 jit_solution(6058189268015974561)
XLA Ops:
  0.6 8.9 %spectra.1 = (bf16[384,512]{1,0:T(8,128)(2,1)}, bf16[384,512]{1,0:T(8,128)(2,1)}, bf16[768,512]{1,0:T(8,128)(2,1)}, bf16[16,96,512]{2,1,0:T(8,128)(2,1)}, bf16[1...) custom-call(bf16[768,4096]{1,0:T(8,128)(2,1)} %bitcast.10, ...), custom_call_target="tpu_custom_call" | custom-call | flops 3221225472 | bytes 6291456 | tf_op jit(solution)/shard_map/spectra/pallas_call | solution.py:285
  9.6 1.3 %collective-permute-start.1 = (bf16[6,64,512]{2,1,0:T(8,128)(2,1)}, bf16[6,64,512]{2,1,0:T(8,128)(2,1)S(1)}, u32[]{:S(2)}, u32[]{:S(2)}) collective-permute-start(bf16[6,64,512]{2,1,0:T(8,128)(2,1)} %bitcast.12), channel_id=1, source_target_pairs={{2,0},{4,2},{6,4},{8,6},{10,8},{12,10},{14,12},{16,14},{18,16},{20... | collective-permute-start | bytes 1179656 | tf_op jit(solution)/shard_map/ppermute | solution.py:508
  10.9 1.3 %collective-permute-start.2 = (bf16[6,64,512]{2,1,0:T(8,128)(2,1)}, bf16[6,64,512]{2,1,0:T(8,128)(2,1)S(1)}, u32[]{:S(2)}, u32[]{:S(2)}) collective-permute-start(bf16[6,64,512]{2,1,0:T(8,128)(2,1)} %bitcast.11), channel_id=1, source_target_pairs={{2,0},{4,2},{6,4},{8,6},{10,8},{12,10},{14,12},{16,14},{18,16},{20... | collective-permute-start | bytes 1179656 | tf_op jit(solution)/shard_map/ppermute | solution.py:508
  12.2 0.0 copy-start
  12.2 9.4 %all-to-all-start = ((bf16[16,96,512]{2,1,0:T(8,128)(2,1)}), bf16[16,96,512]{2,1,0:T(8,128)(2,1)S(1)}, u32[]{:S(2)}, u32[]{:S(2)}) async-start(bf16[16,96,512]{2,1,0:T(8,128)(2,1)} %get-tuple-element.22), calls=%async_computation | async-start | bytes 3145728 | tf_op jit(solution)/shard_map/all_to_all | solution.py:537
  21.6 1.6 %collective-permute-start = (bf16[12,32,512]{2,1,0:T(8,128)(2,1)}, bf16[12,32,512]{2,1,0:T(8,128)(2,1)S(1)}, u32[]{:S(2)}, u32[]{:S(2)}) collective-permute-start(bf16[12,32,512]{2,1,0:T(8,128)(2,1)} %get-tuple-element.13), channel_id=1, source_target_pairs={{0,1},{1,0},{2,3},{3,2},{4,5},{5,4},{6,7},{7,6},{8,9},{9,8},{10,11... | collective-permute-start | bytes 1179656 | tf_op jit(solution)/shard_map/ppermute | solution.py:513
  23.1 0.0 collective-permute-done.1.refs_1_
  23.1 0.1 fusion
  23.2 1.5 %collective-permute-start.4 = (bf16[6,64,512]{2,1,0:T(8,128)(2,1)S(1)}, bf16[6,64,512]{2,1,0:T(8,128)(2,1)S(1)}, u32[]{:S(2)}, u32[]{:S(2)}) collective-permute-start(bf16[6,64,512]{2,1,0:T(8,128)(2,1)S(1)} %fusion), channel_id=1, source_target_pairs={{0,1},{1,0},{2,3},{3,2},{4,5},{5,4},{6,7},{7,6},{8,9},{9,8},{10,11... | collective-permute-start | bytes 1179656 | tf_op jit(solution)/shard_map/ppermute | solution.py:513
  24.7 0.0 collective-permute-done.2.refs_2_
  24.7 0.1 fusion.1.refs_3_
  24.8 0.0 copy-done
  24.8 10.5 %cross.3 = (f32[32,72,256]{2,1,0:T(8,128)S(1)}, bf16[6,64,512]{2,1,0:T(8,128)(2,1)S(1)}) custom-call(bf16[12,64,512]{2,1,0:T(8,128)(2,1)S(1)} %bitcast.7, bf16[6,64,512]{2,1,0:T(8,128)(2,1)S(1)} %collective-permute-done.1.refs_1_, bf16[6,64,512]{2,1,0:T(8,128)(2,1)S(1)} %collective-permute-done.2.refs_2_, ...), custom_call_target="tpu_custom_call", output_to_operand_aliasing={{1}: (3, {})} | custom-call | flops 30000001024 | bytes 3932160 | tf_op jit(solution)/shard_map/cross/pallas_call | solution.py:439
  35.4 1.5 %collective-permute-start.3 = (bf16[6,64,512]{2,1,0:T(8,128)(2,1)S(1)}, bf16[6,64,512]{2,1,0:T(8,128)(2,1)S(1)}, u32[]{:S(2)}, u32[]{:S(2)}) collective-permute-start(bf16[6,64,512]{2,1,0:T(8,128)(2,1)S(1)} %get-tuple-element.18), channel_id=1, source_target_pairs={{0,1},{1,0},{2,3},{3,2},{4,5},{5,4},{6,7},{7,6},{8,9},{9,8},{10,11... | collective-permute-start | bytes 1179656 | tf_op jit(solution)/shard_map/ppermute | solution.py:513
  36.9 0.0 collective-permute-done.refs_0_
  36.9 5.3 %collective-permute-done.4.refs_1_ = bf16[6,64,512]{2,1,0:T(8,128)(2,1)S(1)} collective-permute-done((bf16[6,64,512]{2,1,0:T(8,128)(2,1)S(1)}, bf16[6,64,512]{2,1,0:T(8,128)(2,1)S(1)}, u32[]{:S(2)}, u32[]{:S(2)}) %collective-permute-start.4) | collective-permute-done | bytes 393248 | tf_op jit(solution)/shard_map/ppermute | solution.py:513
  42.2 0.0 copy-start.1
  42.2 5.7 %cross.4.refs_2_ = f32[32,72,256]{2,1,0:T(8,128)S(1)} custom-call(bf16[12,32,512]{2,1,0:T(8,128)(2,1)S(1)} %collective-permute-done.refs_0_, bf16[6,64,512]{2,1,0:T(8,128)(2,1)S(1)} %collective-permute-done.4.refs_1_, f32[32,72,256]{2,1,0:T(8,128)S(1)} %get-tuple-element.20.refs_2_), custom_call_target="tpu_custom_call" | custom-call | flops 15000000512 | bytes 3145728 | tf_op jit(solution)/shard_map/cross/pallas_call | solution.py:439
  47.9 0.0 copy-start.2
  47.9 0.0 copy-start.3
  47.9 2.2 %collective-permute-done.3.refs_1_ = bf16[6,64,512]{2,1,0:T(8,128)(2,1)S(1)} collective-permute-done((bf16[6,64,512]{2,1,0:T(8,128)(2,1)S(1)}, bf16[6,64,512]{2,1,0:T(8,128)(2,1)S(1)}, u32[]{:S(2)}, u32[]{:S(2)}) %collective-permute-start.3) | collective-permute-done | bytes 393248 | tf_op jit(solution)/shard_map/ppermute | solution.py:513
  50.0 0.0 copy-done.1
  50.1 7.3 %cross.5 = (f32[32,64,256]{2,1,0:T(8,128)}, f32[8,128]{1,0:T(8,128)S(1)}) custom-call(bf16[12,32,512]{2,1,0:T(8,128)(2,1)S(1)} %collective-permute-done.refs_0_, bf16[6,64,512]{2,1,0:T(8,128)(2,1)S(1)} %collective-permute-done.3.refs_1_, f32[32,72,256]{2,1,0:T(8,128)S(1)} %cross.4.refs_2_, bf16[256,256]{1,0:T(8,128)(2,1)S(1)} %copy-done.1), custom_call_target="tpu_custom_call" | custom-call | flops 15000000512 | bytes 3145728 | tf_op jit(solution)/shard_map/cross/pallas_call | solution.py:439
  57.4 0.0 all-to-all-done.incoming_ref
  57.4 0.0 copy-done.2
  57.4 0.0 copy-done.3
  57.4 0.8 %fold.1 = f32[64,256]{1,0:T(8,128)S(1)} custom-call(bf16[16,96,512]{2,1,0:T(8,128)(2,1)S(1)} %all-to-all-done.incoming_ref, bf16[768,512]{1,0:T(8,128)(2,1)S(1)} %copy-done, s32[8,128]{1,0:T(8,128)S(1)} %bitcast.9, bf16[256,256]{1,0:T(8,128)(2,1)S(1)} %copy-done.1, bf16[256,256]{1,0:T(8,128)(2,1)S(1)} %copy-done.2, f32[8,128]{1,0:T(8,128)S(1)} %get-tuple-element.23.earlier_ref), custom_call_target="tpu_custom_call" | custom-call | flops 201326592 | bytes 2359296 | tf_op jit(solution)/shard_map/fold/pallas_call | solution.py:493
  58.2 1.6 %collective-permute-start.5 = (f32[32,256]{1,0:T(8,128)S(1)}, f32[32,256]{1,0:T(8,128)S(1)}, u32[]{:S(2)}, u32[]{:S(2)}) collective-permute-start(f32[32,256]{1,0:T(8,128)S(1)} %constant_dynamic-slice_fusion), channel_id=1, source_target_pairs={{0,1},{1,0},{2,3},{3,2},{4,5},{5,4},{6,7},{7,6},{8,9},{9,8},{10,11... | collective-permute-start | bytes 98312 | tf_op jit(solution)/shard_map/ppermute | solution.py:513
  59.8 2.4 %collective-permute-done.5 = f32[32,256]{1,0:T(8,128)S(1)} collective-permute-done((f32[32,256]{1,0:T(8,128)S(1)}, f32[32,256]{1,0:T(8,128)S(1)}, u32[]{:S(2)}, u32[]{:S(2)}) %collective-permute-start.5) | collective-permute-done | bytes 32800 | tf_op jit(solution)/shard_map/ppermute | solution.py:513
  62.2 0.6 dynamic-slice_add_fusion
  (1 shorter events, 0.0 us)
Async XLA Ops:
  9.6 13.6 %collective-permute-start.1 = (bf16[6,64,512]{2,1,0:T(8,128)(2,1)}, bf16[6,64,512]{2,1,0:T(8,128)(2,1)S(1)}, u32[]{:S(2)}, u32[]{:S(2)}) collective-permute-start(bf16[6,64,512]{2,1,0:T(8,128)(2,1)} %bitcast.12), channel_id=1, source_target_pairs={{2,0},{4,2},{6,4},{8,6},{10,8},{12,10},{14,12},{16,14},{18,16},{20... | collective-permute-start | bytes 1179656 | tf_op jit(solution)/shard_map/ppermute | solution.py:508
  10.9 13.9 %collective-permute-start.2 = (bf16[6,64,512]{2,1,0:T(8,128)(2,1)}, bf16[6,64,512]{2,1,0:T(8,128)(2,1)S(1)}, u32[]{:S(2)}, u32[]{:S(2)}) collective-permute-start(bf16[6,64,512]{2,1,0:T(8,128)(2,1)} %bitcast.11), channel_id=1, source_target_pairs={{2,0},{4,2},{6,4},{8,6},{10,8},{12,10},{14,12},{16,14},{18,16},{20... | collective-permute-start | bytes 1179656 | tf_op jit(solution)/shard_map/ppermute | solution.py:508
  12.2 12.7 %copy-start = (bf16[768,512]{1,0:T(8,128)(2,1)S(1)}, bf16[768,512]{1,0:T(8,128)(2,1)}, u32[]{:S(2)}) copy-start(bf16[768,512]{1,0:T(8,128)(2,1)} %get-tuple-element.14.own_ref) | copy-start | bytes 2359300
  12.2 45.2 %all-to-all-start = ((bf16[16,96,512]{2,1,0:T(8,128)(2,1)}), bf16[16,96,512]{2,1,0:T(8,128)(2,1)S(1)}, u32[]{:S(2)}, u32[]{:S(2)}) async-start(bf16[16,96,512]{2,1,0:T(8,128)(2,1)} %get-tuple-element.22), calls=%async_computation | async-start | bytes 3145728 | tf_op jit(solution)/shard_map/all_to_all | solution.py:537
  21.6 15.3 %collective-permute-start = (bf16[12,32,512]{2,1,0:T(8,128)(2,1)}, bf16[12,32,512]{2,1,0:T(8,128)(2,1)S(1)}, u32[]{:S(2)}, u32[]{:S(2)}) collective-permute-start(bf16[12,32,512]{2,1,0:T(8,128)(2,1)} %get-tuple-element.13), channel_id=1, source_target_pairs={{0,1},{1,0},{2,3},{3,2},{4,5},{5,4},{6,7},{7,6},{8,9},{9,8},{10,11... | collective-permute-start | bytes 1179656 | tf_op jit(solution)/shard_map/ppermute | solution.py:513
  23.2 19.0 %collective-permute-start.4 = (bf16[6,64,512]{2,1,0:T(8,128)(2,1)S(1)}, bf16[6,64,512]{2,1,0:T(8,128)(2,1)S(1)}, u32[]{:S(2)}, u32[]{:S(2)}) collective-permute-start(bf16[6,64,512]{2,1,0:T(8,128)(2,1)S(1)} %fusion), channel_id=1, source_target_pairs={{0,1},{1,0},{2,3},{3,2},{4,5},{5,4},{6,7},{7,6},{8,9},{9,8},{10,11... | collective-permute-start | bytes 1179656 | tf_op jit(solution)/shard_map/ppermute | solution.py:513
  35.4 14.7 %collective-permute-start.3 = (bf16[6,64,512]{2,1,0:T(8,128)(2,1)S(1)}, bf16[6,64,512]{2,1,0:T(8,128)(2,1)S(1)}, u32[]{:S(2)}, u32[]{:S(2)}) collective-permute-start(bf16[6,64,512]{2,1,0:T(8,128)(2,1)S(1)} %get-tuple-element.18), channel_id=1, source_target_pairs={{0,1},{1,0},{2,3},{3,2},{4,5},{5,4},{6,7},{7,6},{8,9},{9,8},{10,11... | collective-permute-start | bytes 1179656 | tf_op jit(solution)/shard_map/ppermute | solution.py:513
  42.2 7.9 %copy-start.1 = (bf16[256,256]{1,0:T(8,128)(2,1)S(1)}, bf16[256,256]{1,0:T(8,128)(2,1)}, u32[]{:S(2)}) copy-start(bf16[256,256]{1,0:T(8,128)(2,1)} %constant.35.clone.refs_3_.high_ref) | copy-start | bytes 393220
  47.9 9.5 %copy-start.2 = (bf16[256,256]{1,0:T(8,128)(2,1)S(1)}, bf16[256,256]{1,0:T(8,128)(2,1)}, u32[]{:S(2)}) copy-start(bf16[256,256]{1,0:T(8,128)(2,1)} %constant.36.clone.low_ref) | copy-start | bytes 393220
  47.9 9.5 %copy-start.3 = (s32[1024,1]{0,1:T(1,128)S(1)}, s32[1024,1]{0,1:T(1,128)}, u32[]{:S(2)}) copy-start(s32[1024,1]{0,1:T(1,128)} %param.9) | copy-start | bytes 12292
  58.2 4.0 %collective-permute-start.5 = (f32[32,256]{1,0:T(8,128)S(1)}, f32[32,256]{1,0:T(8,128)S(1)}, u32[]{:S(2)}, u32[]{:S(2)}) collective-permute-start(f32[32,256]{1,0:T(8,128)S(1)} %constant_dynamic-slice_fusion), channel_id=1, source_target_pairs={{0,1},{1,0},{2,3},{3,2},{4,5},{5,4},{6,7},{7,6},{8,9},{9,8},{10,11... | collective-permute-start | bytes 98312 | tf_op jit(solution)/shard_map/ppermute | solution.py:513

commit v8 on v7

--- a/solution.py
+++ b/solution.py
@@ -265,7 +265,7 @@
 def spectra_call(traces, quality, owners, places, chan_count, own_count):
     rows, length = traces.shape
     ch_dev = quality.shape[1]
-    row_steps = rows // (4 * ch_dev) if rows % (4 * ch_dev) == 0 else rows // (2 * ch_dev)
+    row_steps = rows // (6 * ch_dev) if rows % (6 * ch_dev) == 0 else rows // (2 * ch_dev)
     part, depth = rows // row_steps, length // QUARTERS
     slots = part // (2 * ch_dev) * 2 * CAP
     anywhere = pl.BlockSpec(memory_space=pl.ANY)
@@ -379,7 +379,7 @@
             return tuple(sums)
 
         zero = jnp.zeros((8, H), jnp.float32)
-        sums = lax.fori_loop(0, windows, add_window, (zero,) * (3 * group * tiles), unroll=2)
+        sums = lax.fori_loop(0, windows, add_window, (zero,) * (3 * group * tiles), unroll=3)
         for i in range(group):
             for t in range(tiles):
                 at = 3 * (i * tiles + t)

time: 63.1 us -> 63.2 us (level)
  waiting for transfers between devices: 9.88 us -> 10.8 us
  Pallas kernels: 33.2 us -> 32.4 us
    pallas_call x3, Pallas kernels: 23.5 us -> 22.3 us  [cross_call(): pl.pallas_call(functools.partial(cross_kernel, last, with_sum, skipped, l...]
    ppermute x4, waiting for transfers between devices: 9.87 us -> 10.8 us  [round_win(): lax.ppermute(block, 'win', [(i, (i + shift) % count) for i in range(count)])]
  transfers between devices with their start and end apart: 7 -> 7, of which waited for: 3 -> 3; matrix products, arithmetic and copies ran while one was open for 0% -> 0% of each run, Pallas kernels for 37% -> 35%
where the time goes in v8:
time: 63.2 us; the launch traced here: 63 us
  Pallas kernels  32.4 us (51%)
  starting transfers between devices  18.2 us (29%)
  waiting for transfers between devices  10.8 us (17%)
  other arithmetic  0.78 us (1%)
  between operations  0.78 us (1%)
    pallas_call x3, Pallas kernels, cross_call(): pl.pallas_call(functools.partial(cross_kernel, last, with_sum, skipped, l...  22.3 us
    ppermute x4, waiting for transfers between devices, round_win(): lax.ppermute(block, 'win', [(i, (i + shift) % count) for i in range(count)])  10.8 us
    all_to_all x1, starting transfers between devices, local(): lax.all_to_all(outgoing, 'chan', split_axis=0, concat_axis=0, tiled=True)  9.39 us
    pallas_call x1, Pallas kernels, spectra_call(): pl.pallas_call(spectra_kernel, in_specs=[anywhere] * 5, out_specs=[anywhe...  9.36 us
    ppermute x4, starting transfers between devices, round_win(): lax.ppermute(block, 'win', [(i, (i + shift) % count) for i in range(count)])  6.18 us
    ppermute x2, starting transfers between devices, from_above(): return lax.ppermute(block, 'chan', [(i, i - 1) for i in range(1, count)])  2.58 us
  transfers between devices with their start and end apart: 7, of which 3 were waited for; matrix products, arithmetic and copies ran while one was open for 0% of the time, Pallas kernels for 35%

profile of v8, /device:TPU:0, one launch (start us, length us, event | category | flops | bytes accessed | tf_op | source)
XLA Modules:
  0.0 63.0 jit_solution(16520720912136416611)
XLA Ops:
  0.6 9.4 %spectra.1 = (bf16[384,512]{1,0:T(8,128)(2,1)}, bf16[384,512]{1,0:T(8,128)(2,1)}, bf16[768,512]{1,0:T(8,128)(2,1)}, bf16[16,96,512]{2,1,0:T(8,128)(2,1)}, bf16[1...) custom-call(bf16[768,4096]{1,0:T(8,128)(2,1)} %bitcast.10, ...), custom_call_target="tpu_custom_call" | custom-call | flops 3221225472 | bytes 6291456 | tf_op jit(solution)/shard_map/spectra/pallas_call | solution.py:285
  10.0 1.3 %collective-permute-start.1 = (bf16[6,64,512]{2,1,0:T(8,128)(2,1)}, bf16[6,64,512]{2,1,0:T(8,128)(2,1)S(1)}, u32[]{:S(2)}, u32[]{:S(2)}) collective-permute-start(bf16[6,64,512]{2,1,0:T(8,128)(2,1)} %bitcast.12), channel_id=1, source_target_pairs={{2,0},{4,2},{6,4},{8,6},{10,8},{12,10},{14,12},{16,14},{18,16},{20... | collective-permute-start | bytes 1179656 | tf_op jit(solution)/shard_map/ppermute | solution.py:508
  11.3 1.3 %collective-permute-start.2 = (bf16[6,64,512]{2,1,0:T(8,128)(2,1)}, bf16[6,64,512]{2,1,0:T(8,128)(2,1)S(1)}, u32[]{:S(2)}, u32[]{:S(2)}) collective-permute-start(bf16[6,64,512]{2,1,0:T(8,128)(2,1)} %bitcast.11), channel_id=1, source_target_pairs={{2,0},{4,2},{6,4},{8,6},{10,8},{12,10},{14,12},{16,14},{18,16},{20... | collective-permute-start | bytes 1179656 | tf_op jit(solution)/shard_map/ppermute | solution.py:508
  12.6 0.0 copy-start
  12.6 9.4 %all-to-all-start = ((bf16[16,96,512]{2,1,0:T(8,128)(2,1)}), bf16[16,96,512]{2,1,0:T(8,128)(2,1)S(1)}, u32[]{:S(2)}, u32[]{:S(2)}) async-start(bf16[16,96,512]{2,1,0:T(8,128)(2,1)} %get-tuple-element.22), calls=%async_computation | async-start | bytes 3145728 | tf_op jit(solution)/shard_map/all_to_all | solution.py:537
  22.0 1.6 %collective-permute-start = (bf16[12,32,512]{2,1,0:T(8,128)(2,1)}, bf16[12,32,512]{2,1,0:T(8,128)(2,1)S(1)}, u32[]{:S(2)}, u32[]{:S(2)}) collective-permute-start(bf16[12,32,512]{2,1,0:T(8,128)(2,1)} %get-tuple-element.13), channel_id=1, source_target_pairs={{0,1},{1,0},{2,3},{3,2},{4,5},{5,4},{6,7},{7,6},{8,9},{9,8},{10,11... | collective-permute-start | bytes 1179656 | tf_op jit(solution)/shard_map/ppermute | solution.py:513
  23.6 0.0 collective-permute-done.1.refs_1_
  23.6 0.1 fusion
  23.6 1.5 %collective-permute-start.4 = (bf16[6,64,512]{2,1,0:T(8,128)(2,1)S(1)}, bf16[6,64,512]{2,1,0:T(8,128)(2,1)S(1)}, u32[]{:S(2)}, u32[]{:S(2)}) collective-permute-start(bf16[6,64,512]{2,1,0:T(8,128)(2,1)S(1)} %fusion), channel_id=1, source_target_pairs={{0,1},{1,0},{2,3},{3,2},{4,5},{5,4},{6,7},{7,6},{8,9},{9,8},{10,11... | collective-permute-start | bytes 1179656 | tf_op jit(solution)/shard_map/ppermute | solution.py:513
  25.2 0.0 collective-permute-done.2.refs_2_
  25.2 0.1 fusion.1.refs_3_
  25.3 0.0 copy-done
  25.3 9.9 %cross.3 = (f32[32,72,256]{2,1,0:T(8,128)S(1)}, bf16[6,64,512]{2,1,0:T(8,128)(2,1)S(1)}) custom-call(bf16[12,64,512]{2,1,0:T(8,128)(2,1)S(1)} %bitcast.7, bf16[6,64,512]{2,1,0:T(8,128)(2,1)S(1)} %collective-permute-done.1.refs_1_, bf16[6,64,512]{2,1,0:T(8,128)(2,1)S(1)} %collective-permute-done.2.refs_2_, ...), custom_call_target="tpu_custom_call", output_to_operand_aliasing={{1}: (3, {})} | custom-call | flops 30000001024 | bytes 3932160 | tf_op jit(solution)/shard_map/cross/pallas_call | solution.py:439
  35.2 1.5 %collective-permute-start.3 = (bf16[6,64,512]{2,1,0:T(8,128)(2,1)S(1)}, bf16[6,64,512]{2,1,0:T(8,128)(2,1)S(1)}, u32[]{:S(2)}, u32[]{:S(2)}) collective-permute-start(bf16[6,64,512]{2,1,0:T(8,128)(2,1)S(1)} %get-tuple-element.18), channel_id=1, source_target_pairs={{0,1},{1,0},{2,3},{3,2},{4,5},{5,4},{6,7},{7,6},{8,9},{9,8},{10,11... | collective-permute-start | bytes 1179656 | tf_op jit(solution)/shard_map/ppermute | solution.py:513
  36.7 0.0 collective-permute-done.refs_0_
  36.7 5.9 %collective-permute-done.4.refs_1_ = bf16[6,64,512]{2,1,0:T(8,128)(2,1)S(1)} collective-permute-done((bf16[6,64,512]{2,1,0:T(8,128)(2,1)S(1)}, bf16[6,64,512]{2,1,0:T(8,128)(2,1)S(1)}, u32[]{:S(2)}, u32[]{:S(2)}) %collective-permute-start.4) | collective-permute-done | bytes 393248 | tf_op jit(solution)/shard_map/ppermute | solution.py:513
  42.6 0.0 copy-start.1
  42.6 5.4 %cross.4.refs_2_ = f32[32,72,256]{2,1,0:T(8,128)S(1)} custom-call(bf16[12,32,512]{2,1,0:T(8,128)(2,1)S(1)} %collective-permute-done.refs_0_, bf16[6,64,512]{2,1,0:T(8,128)(2,1)S(1)} %collective-permute-done.4.refs_1_, f32[32,72,256]{2,1,0:T(8,128)S(1)} %get-tuple-element.20.refs_2_), custom_call_target="tpu_custom_call" | custom-call | flops 15000000512 | bytes 3145728 | tf_op jit(solution)/shard_map/cross/pallas_call | solution.py:439
  48.0 0.0 copy-start.2
  48.0 0.0 copy-start.3
  48.0 2.5 %collective-permute-done.3.refs_1_ = bf16[6,64,512]{2,1,0:T(8,128)(2,1)S(1)} collective-permute-done((bf16[6,64,512]{2,1,0:T(8,128)(2,1)S(1)}, bf16[6,64,512]{2,1,0:T(8,128)(2,1)S(1)}, u32[]{:S(2)}, u32[]{:S(2)}) %collective-permute-start.3) | collective-permute-done | bytes 393248 | tf_op jit(solution)/shard_map/ppermute | solution.py:513
  50.5 0.0 copy-done.1
  50.5 7.0 %cross.5 = (f32[32,64,256]{2,1,0:T(8,128)}, f32[8,128]{1,0:T(8,128)S(1)}) custom-call(bf16[12,32,512]{2,1,0:T(8,128)(2,1)S(1)} %collective-permute-done.refs_0_, bf16[6,64,512]{2,1,0:T(8,128)(2,1)S(1)} %collective-permute-done.3.refs_1_, f32[32,72,256]{2,1,0:T(8,128)S(1)} %cross.4.refs_2_, bf16[256,256]{1,0:T(8,128)(2,1)S(1)} %copy-done.1), custom_call_target="tpu_custom_call" | custom-call | flops 15000000512 | bytes 3145728 | tf_op jit(solution)/shard_map/cross/pallas_call | solution.py:439
  57.5 0.0 all-to-all-done.incoming_ref
  57.5 0.0 copy-done.2
  57.6 0.0 copy-done.3
  57.6 0.8 %fold.1 = f32[64,256]{1,0:T(8,128)S(1)} custom-call(bf16[16,96,512]{2,1,0:T(8,128)(2,1)S(1)} %all-to-all-done.incoming_ref, bf16[768,512]{1,0:T(8,128)(2,1)S(1)} %copy-done, s32[8,128]{1,0:T(8,128)S(1)} %bitcast.9, bf16[256,256]{1,0:T(8,128)(2,1)S(1)} %copy-done.1, bf16[256,256]{1,0:T(8,128)(2,1)S(1)} %copy-done.2, f32[8,128]{1,0:T(8,128)S(1)} %get-tuple-element.23.earlier_ref), custom_call_target="tpu_custom_call" | custom-call | flops 201326592 | bytes 2359296 | tf_op jit(solution)/shard_map/fold/pallas_call | solution.py:493
  58.4 1.6 %collective-permute-start.5 = (f32[32,256]{1,0:T(8,128)S(1)}, f32[32,256]{1,0:T(8,128)S(1)}, u32[]{:S(2)}, u32[]{:S(2)}) collective-permute-start(f32[32,256]{1,0:T(8,128)S(1)} %constant_dynamic-slice_fusion), channel_id=1, source_target_pairs={{0,1},{1,0},{2,3},{3,2},{4,5},{5,4},{6,7},{7,6},{8,9},{9,8},{10,11... | collective-permute-start | bytes 98312 | tf_op jit(solution)/shard_map/ppermute | solution.py:513
  59.9 2.4 %collective-permute-done.5 = f32[32,256]{1,0:T(8,128)S(1)} collective-permute-done((f32[32,256]{1,0:T(8,128)S(1)}, f32[32,256]{1,0:T(8,128)S(1)}, u32[]{:S(2)}, u32[]{:S(2)}) %collective-permute-start.5) | collective-permute-done | bytes 32800 | tf_op jit(solution)/shard_map/ppermute | solution.py:513
  62.4 0.6 dynamic-slice_add_fusion
  (1 shorter events, 0.0 us)
Async XLA Ops:
  10.0 13.6 %collective-permute-start.1 = (bf16[6,64,512]{2,1,0:T(8,128)(2,1)}, bf16[6,64,512]{2,1,0:T(8,128)(2,1)S(1)}, u32[]{:S(2)}, u32[]{:S(2)}) collective-permute-start(bf16[6,64,512]{2,1,0:T(8,128)(2,1)} %bitcast.12), channel_id=1, source_target_pairs={{2,0},{4,2},{6,4},{8,6},{10,8},{12,10},{14,12},{16,14},{18,16},{20... | collective-permute-start | bytes 1179656 | tf_op jit(solution)/shard_map/ppermute | solution.py:508
  11.3 13.9 %collective-permute-start.2 = (bf16[6,64,512]{2,1,0:T(8,128)(2,1)}, bf16[6,64,512]{2,1,0:T(8,128)(2,1)S(1)}, u32[]{:S(2)}, u32[]{:S(2)}) collective-permute-start(bf16[6,64,512]{2,1,0:T(8,128)(2,1)} %bitcast.11), channel_id=1, source_target_pairs={{2,0},{4,2},{6,4},{8,6},{10,8},{12,10},{14,12},{16,14},{18,16},{20... | collective-permute-start | bytes 1179656 | tf_op jit(solution)/shard_map/ppermute | solution.py:508
  12.6 12.7 %copy-start = (bf16[768,512]{1,0:T(8,128)(2,1)S(1)}, bf16[768,512]{1,0:T(8,128)(2,1)}, u32[]{:S(2)}) copy-start(bf16[768,512]{1,0:T(8,128)(2,1)} %get-tuple-element.14.own_ref) | copy-start | bytes 2359300
  12.6 44.9 %all-to-all-start = ((bf16[16,96,512]{2,1,0:T(8,128)(2,1)}), bf16[16,96,512]{2,1,0:T(8,128)(2,1)S(1)}, u32[]{:S(2)}, u32[]{:S(2)}) async-start(bf16[16,96,512]{2,1,0:T(8,128)(2,1)} %get-tuple-element.22), calls=%async_computation | async-start | bytes 3145728 | tf_op jit(solution)/shard_map/all_to_all | solution.py:537
  22.0 14.7 %collective-permute-start = (bf16[12,32,512]{2,1,0:T(8,128)(2,1)}, bf16[12,32,512]{2,1,0:T(8,128)(2,1)S(1)}, u32[]{:S(2)}, u32[]{:S(2)}) collective-permute-start(bf16[12,32,512]{2,1,0:T(8,128)(2,1)} %get-tuple-element.13), channel_id=1, source_target_pairs={{0,1},{1,0},{2,3},{3,2},{4,5},{5,4},{6,7},{7,6},{8,9},{9,8},{10,11... | collective-permute-start | bytes 1179656 | tf_op jit(solution)/shard_map/ppermute | solution.py:513
  23.6 19.0 %collective-permute-start.4 = (bf16[6,64,512]{2,1,0:T(8,128)(2,1)S(1)}, bf16[6,64,512]{2,1,0:T(8,128)(2,1)S(1)}, u32[]{:S(2)}, u32[]{:S(2)}) collective-permute-start(bf16[6,64,512]{2,1,0:T(8,128)(2,1)S(1)} %fusion), channel_id=1, source_target_pairs={{0,1},{1,0},{2,3},{3,2},{4,5},{5,4},{6,7},{7,6},{8,9},{9,8},{10,11... | collective-permute-start | bytes 1179656 | tf_op jit(solution)/shard_map/ppermute | solution.py:513
  35.2 15.3 %collective-permute-start.3 = (bf16[6,64,512]{2,1,0:T(8,128)(2,1)S(1)}, bf16[6,64,512]{2,1,0:T(8,128)(2,1)S(1)}, u32[]{:S(2)}, u32[]{:S(2)}) collective-permute-start(bf16[6,64,512]{2,1,0:T(8,128)(2,1)S(1)} %get-tuple-element.18), channel_id=1, source_target_pairs={{0,1},{1,0},{2,3},{3,2},{4,5},{5,4},{6,7},{7,6},{8,9},{9,8},{10,11... | collective-permute-start | bytes 1179656 | tf_op jit(solution)/shard_map/ppermute | solution.py:513
  42.6 7.9 %copy-start.1 = (bf16[256,256]{1,0:T(8,128)(2,1)S(1)}, bf16[256,256]{1,0:T(8,128)(2,1)}, u32[]{:S(2)}) copy-start(bf16[256,256]{1,0:T(8,128)(2,1)} %constant.35.clone.refs_3_.high_ref) | copy-start | bytes 393220
  48.0 9.5 %copy-start.2 = (bf16[256,256]{1,0:T(8,128)(2,1)S(1)}, bf16[256,256]{1,0:T(8,128)(2,1)}, u32[]{:S(2)}) copy-start(bf16[256,256]{1,0:T(8,128)(2,1)} %constant.36.clone.low_ref) | copy-start | bytes 393220
  48.0 9.5 %copy-start.3 = (s32[1024,1]{0,1:T(1,128)S(1)}, s32[1024,1]{0,1:T(1,128)}, u32[]{:S(2)}) copy-start(s32[1024,1]{0,1:T(1,128)} %param.9) | copy-start | bytes 12292
  58.4 4.0 %collective-permute-start.5 = (f32[32,256]{1,0:T(8,128)S(1)}, f32[32,256]{1,0:T(8,128)S(1)}, u32[]{:S(2)}, u32[]{:S(2)}) collective-permute-start(f32[32,256]{1,0:T(8,128)S(1)} %constant_dynamic-slice_fusion), channel_id=1, source_target_pairs={{0,1},{1,0},{2,3},{3,2},{4,5},{5,4},{6,7},{7,6},{8,9},{9,8},{10,11... | collective-permute-start | bytes 98312 | tf_op jit(solution)/shard_map/ppermute | solution.py:513

commit v9 on v8

--- a/solution.py
+++ b/solution.py
@@ -265,7 +265,7 @@
 def spectra_call(traces, quality, owners, places, chan_count, own_count):
     rows, length = traces.shape
     ch_dev = quality.shape[1]
-    row_steps = rows // (6 * ch_dev) if rows % (6 * ch_dev) == 0 else rows // (2 * ch_dev)
+    row_steps = rows // (4 * ch_dev) if rows % (4 * ch_dev) == 0 else rows // (2 * ch_dev)
     part, depth = rows // row_steps, length // QUARTERS
     slots = part // (2 * ch_dev) * 2 * CAP
     anywhere = pl.BlockSpec(memory_space=pl.ANY)

time: 63.2 us -> 62.8 us (level)
  transfers between devices with their start and end apart: 7 -> 7, of which waited for: 3 -> 3; matrix products, arithmetic and copies ran while one was open for 0% -> 0% of each run, Pallas kernels for 35% -> 36%
where the time goes in v9:
time: 62.8 us; the launch traced here: 62.5 us
  Pallas kernels  32 us (51%)
  starting transfers between devices  18.1 us (29%)
  waiting for transfers between devices  10.8 us (17%)
  other arithmetic  0.78 us (1%)
  between operations  0.78 us (1%)
    pallas_call x3, Pallas kernels, cross_call(): pl.pallas_call(functools.partial(cross_kernel, last, with_sum, skipped, l...  22.3 us
    ppermute x4, waiting for transfers between devices, round_win(): lax.ppermute(block, 'win', [(i, (i + shift) % count) for i in range(count)])  10.8 us
    all_to_all x1, starting transfers between devices, local(): lax.all_to_all(outgoing, 'chan', split_axis=0, concat_axis=0, tiled=True)  9.38 us
    pallas_call x1, Pallas kernels, spectra_call(): pl.pallas_call(spectra_kernel, in_specs=[anywhere] * 5, out_specs=[anywhe...  8.92 us
    ppermute x4, starting transfers between devices, round_win(): lax.ppermute(block, 'win', [(i, (i + shift) % count) for i in range(count)])  6.17 us
    ppermute x2, starting transfers between devices, from_above(): return lax.ppermute(block, 'chan', [(i, i - 1) for i in range(1, count)])  2.58 us
  transfers between devices with their start and end apart: 7, of which 3 were waited for; matrix products, arithmetic and copies ran while one was open for 0% of the time, Pallas kernels for 36%

profile of v9, /device:TPU:0, one launch (start us, length us, event | category | flops | bytes accessed | tf_op | source)
XLA Modules:
  0.0 62.5 jit_solution(18416642124414041601)
XLA Ops:
  0.6 8.9 %spectra.1 = (bf16[384,512]{1,0:T(8,128)(2,1)}, bf16[384,512]{1,0:T(8,128)(2,1)}, bf16[768,512]{1,0:T(8,128)(2,1)}, bf16[16,96,512]{2,1,0:T(8,128)(2,1)}, bf16[1...) custom-call(bf16[768,4096]{1,0:T(8,128)(2,1)} %bitcast.10, ...), custom_call_target="tpu_custom_call" | custom-call | flops 3221225472 | bytes 6291456 | tf_op jit(solution)/shard_map/spectra/pallas_call | solution.py:285
  9.6 1.3 %collective-permute-start.1 = (bf16[6,64,512]{2,1,0:T(8,128)(2,1)}, bf16[6,64,512]{2,1,0:T(8,128)(2,1)S(1)}, u32[]{:S(2)}, u32[]{:S(2)}) collective-permute-start(bf16[6,64,512]{2,1,0:T(8,128)(2,1)} %bitcast.12), channel_id=1, source_target_pairs={{2,0},{4,2},{6,4},{8,6},{10,8},{12,10},{14,12},{16,14},{18,16},{20... | collective-permute-start | bytes 1179656 | tf_op jit(solution)/shard_map/ppermute | solution.py:508
  10.9 1.3 %collective-permute-start.2 = (bf16[6,64,512]{2,1,0:T(8,128)(2,1)}, bf16[6,64,512]{2,1,0:T(8,128)(2,1)S(1)}, u32[]{:S(2)}, u32[]{:S(2)}) collective-permute-start(bf16[6,64,512]{2,1,0:T(8,128)(2,1)} %bitcast.11), channel_id=1, source_target_pairs={{2,0},{4,2},{6,4},{8,6},{10,8},{12,10},{14,12},{16,14},{18,16},{20... | collective-permute-start | bytes 1179656 | tf_op jit(solution)/shard_map/ppermute | solution.py:508
  12.2 0.0 copy-start
  12.2 9.4 %all-to-all-start = ((bf16[16,96,512]{2,1,0:T(8,128)(2,1)}), bf16[16,96,512]{2,1,0:T(8,128)(2,1)S(1)}, u32[]{:S(2)}, u32[]{:S(2)}) async-start(bf16[16,96,512]{2,1,0:T(8,128)(2,1)} %get-tuple-element.22), calls=%async_computation | async-start | bytes 3145728 | tf_op jit(solution)/shard_map/all_to_all | solution.py:537
  21.6 1.6 %collective-permute-start = (bf16[12,32,512]{2,1,0:T(8,128)(2,1)}, bf16[12,32,512]{2,1,0:T(8,128)(2,1)S(1)}, u32[]{:S(2)}, u32[]{:S(2)}) collective-permute-start(bf16[12,32,512]{2,1,0:T(8,128)(2,1)} %get-tuple-element.13), channel_id=1, source_target_pairs={{0,1},{1,0},{2,3},{3,2},{4,5},{5,4},{6,7},{7,6},{8,9},{9,8},{10,11... | collective-permute-start | bytes 1179656 | tf_op jit(solution)/shard_map/ppermute | solution.py:513
  23.1 0.0 collective-permute-done.1.refs_1_
  23.1 0.1 fusion
  23.2 1.5 %collective-permute-start.4 = (bf16[6,64,512]{2,1,0:T(8,128)(2,1)S(1)}, bf16[6,64,512]{2,1,0:T(8,128)(2,1)S(1)}, u32[]{:S(2)}, u32[]{:S(2)}) collective-permute-start(bf16[6,64,512]{2,1,0:T(8,128)(2,1)S(1)} %fusion), channel_id=1, source_target_pairs={{0,1},{1,0},{2,3},{3,2},{4,5},{5,4},{6,7},{7,6},{8,9},{9,8},{10,11... | collective-permute-start | bytes 1179656 | tf_op jit(solution)/shard_map/ppermute | solution.py:513
  24.7 0.0 collective-permute-done.2.refs_2_
  24.7 0.1 fusion.1.refs_3_
  24.8 0.0 copy-done
  24.8 9.9 %cross.3 = (f32[32,72,256]{2,1,0:T(8,128)S(1)}, bf16[6,64,512]{2,1,0:T(8,128)(2,1)S(1)}) custom-call(bf16[12,64,512]{2,1,0:T(8,128)(2,1)S(1)} %bitcast.7, bf16[6,64,512]{2,1,0:T(8,128)(2,1)S(1)} %collective-permute-done.1.refs_1_, bf16[6,64,512]{2,1,0:T(8,128)(2,1)S(1)} %collective-permute-done.2.refs_2_, ...), custom_call_target="tpu_custom_call", output_to_operand_aliasing={{1}: (3, {})} | custom-call | flops 30000001024 | bytes 3932160 | tf_op jit(solution)/shard_map/cross/pallas_call | solution.py:439
  34.7 1.5 %collective-permute-start.3 = (bf16[6,64,512]{2,1,0:T(8,128)(2,1)S(1)}, bf16[6,64,512]{2,1,0:T(8,128)(2,1)S(1)}, u32[]{:S(2)}, u32[]{:S(2)}) collective-permute-start(bf16[6,64,512]{2,1,0:T(8,128)(2,1)S(1)} %get-tuple-element.18), channel_id=1, source_target_pairs={{0,1},{1,0},{2,3},{3,2},{4,5},{5,4},{6,7},{7,6},{8,9},{9,8},{10,11... | collective-permute-start | bytes 1179656 | tf_op jit(solution)/shard_map/ppermute | solution.py:513
  36.3 0.0 collective-permute-done.refs_0_
  36.3 5.9 %collective-permute-done.4.refs_1_ = bf16[6,64,512]{2,1,0:T(8,128)(2,1)S(1)} collective-permute-done((bf16[6,64,512]{2,1,0:T(8,128)(2,1)S(1)}, bf16[6,64,512]{2,1,0:T(8,128)(2,1)S(1)}, u32[]{:S(2)}, u32[]{:S(2)}) %collective-permute-start.4) | collective-permute-done | bytes 393248 | tf_op jit(solution)/shard_map/ppermute | solution.py:513
  42.2 0.0 copy-start.1
  42.2 5.4 %cross.4.refs_2_ = f32[32,72,256]{2,1,0:T(8,128)S(1)} custom-call(bf16[12,32,512]{2,1,0:T(8,128)(2,1)S(1)} %collective-permute-done.refs_0_, bf16[6,64,512]{2,1,0:T(8,128)(2,1)S(1)} %collective-permute-done.4.refs_1_, f32[32,72,256]{2,1,0:T(8,128)S(1)} %get-tuple-element.20.refs_2_), custom_call_target="tpu_custom_call" | custom-call | flops 15000000512 | bytes 3145728 | tf_op jit(solution)/shard_map/cross/pallas_call | solution.py:439
  47.6 0.0 copy-start.2
  47.6 0.0 copy-start.3
  47.6 2.5 %collective-permute-done.3.refs_1_ = bf16[6,64,512]{2,1,0:T(8,128)(2,1)S(1)} collective-permute-done((bf16[6,64,512]{2,1,0:T(8,128)(2,1)S(1)}, bf16[6,64,512]{2,1,0:T(8,128)(2,1)S(1)}, u32[]{:S(2)}, u32[]{:S(2)}) %collective-permute-start.3) | collective-permute-done | bytes 393248 | tf_op jit(solution)/shard_map/ppermute | solution.py:513
  50.0 0.0 copy-done.1
  50.1 7.0 %cross.5 = (f32[32,64,256]{2,1,0:T(8,128)}, f32[8,128]{1,0:T(8,128)S(1)}) custom-call(bf16[12,32,512]{2,1,0:T(8,128)(2,1)S(1)} %collective-permute-done.refs_0_, bf16[6,64,512]{2,1,0:T(8,128)(2,1)S(1)} %collective-permute-done.3.refs_1_, f32[32,72,256]{2,1,0:T(8,128)S(1)} %cross.4.refs_2_, bf16[256,256]{1,0:T(8,128)(2,1)S(1)} %copy-done.1), custom_call_target="tpu_custom_call" | custom-call | flops 15000000512 | bytes 3145728 | tf_op jit(solution)/shard_map/cross/pallas_call | solution.py:439
  57.1 0.0 all-to-all-done.incoming_ref
  57.1 0.0 copy-done.2
  57.1 0.0 copy-done.3
  57.1 0.8 %fold.1 = f32[64,256]{1,0:T(8,128)S(1)} custom-call(bf16[16,96,512]{2,1,0:T(8,128)(2,1)S(1)} %all-to-all-done.incoming_ref, bf16[768,512]{1,0:T(8,128)(2,1)S(1)} %copy-done, s32[8,128]{1,0:T(8,128)S(1)} %bitcast.9, bf16[256,256]{1,0:T(8,128)(2,1)S(1)} %copy-done.1, bf16[256,256]{1,0:T(8,128)(2,1)S(1)} %copy-done.2, f32[8,128]{1,0:T(8,128)S(1)} %get-tuple-element.23.earlier_ref), custom_call_target="tpu_custom_call" | custom-call | flops 201326592 | bytes 2359296 | tf_op jit(solution)/shard_map/fold/pallas_call | solution.py:493
  57.9 1.5 %collective-permute-start.5 = (f32[32,256]{1,0:T(8,128)S(1)}, f32[32,256]{1,0:T(8,128)S(1)}, u32[]{:S(2)}, u32[]{:S(2)}) collective-permute-start(f32[32,256]{1,0:T(8,128)S(1)} %constant_dynamic-slice_fusion), channel_id=1, source_target_pairs={{0,1},{1,0},{2,3},{3,2},{4,5},{5,4},{6,7},{7,6},{8,9},{9,8},{10,11... | collective-permute-start | bytes 98312 | tf_op jit(solution)/shard_map/ppermute | solution.py:513
  59.5 2.4 %collective-permute-done.5 = f32[32,256]{1,0:T(8,128)S(1)} collective-permute-done((f32[32,256]{1,0:T(8,128)S(1)}, f32[32,256]{1,0:T(8,128)S(1)}, u32[]{:S(2)}, u32[]{:S(2)}) %collective-permute-start.5) | collective-permute-done | bytes 32800 | tf_op jit(solution)/shard_map/ppermute | solution.py:513
  61.9 0.6 dynamic-slice_add_fusion
  (1 shorter events, 0.0 us)
Async XLA Ops:
  9.6 13.6 %collective-permute-start.1 = (bf16[6,64,512]{2,1,0:T(8,128)(2,1)}, bf16[6,64,512]{2,1,0:T(8,128)(2,1)S(1)}, u32[]{:S(2)}, u32[]{:S(2)}) collective-permute-start(bf16[6,64,512]{2,1,0:T(8,128)(2,1)} %bitcast.12), channel_id=1, source_target_pairs={{2,0},{4,2},{6,4},{8,6},{10,8},{12,10},{14,12},{16,14},{18,16},{20... | collective-permute-start | bytes 1179656 | tf_op jit(solution)/shard_map/ppermute | solution.py:508
  10.9 13.9 %collective-permute-start.2 = (bf16[6,64,512]{2,1,0:T(8,128)(2,1)}, bf16[6,64,512]{2,1,0:T(8,128)(2,1)S(1)}, u32[]{:S(2)}, u32[]{:S(2)}) collective-permute-start(bf16[6,64,512]{2,1,0:T(8,128)(2,1)} %bitcast.11), channel_id=1, source_target_pairs={{2,0},{4,2},{6,4},{8,6},{10,8},{12,10},{14,12},{16,14},{18,16},{20... | collective-permute-start | bytes 1179656 | tf_op jit(solution)/shard_map/ppermute | solution.py:508
  12.2 12.7 %copy-start = (bf16[768,512]{1,0:T(8,128)(2,1)S(1)}, bf16[768,512]{1,0:T(8,128)(2,1)}, u32[]{:S(2)}) copy-start(bf16[768,512]{1,0:T(8,128)(2,1)} %get-tuple-element.14.own_ref) | copy-start | bytes 2359300
  12.2 44.9 %all-to-all-start = ((bf16[16,96,512]{2,1,0:T(8,128)(2,1)}), bf16[16,96,512]{2,1,0:T(8,128)(2,1)S(1)}, u32[]{:S(2)}, u32[]{:S(2)}) async-start(bf16[16,96,512]{2,1,0:T(8,128)(2,1)} %get-tuple-element.22), calls=%async_computation | async-start | bytes 3145728 | tf_op jit(solution)/shard_map/all_to_all | solution.py:537
  21.6 14.7 %collective-permute-start = (bf16[12,32,512]{2,1,0:T(8,128)(2,1)}, bf16[12,32,512]{2,1,0:T(8,128)(2,1)S(1)}, u32[]{:S(2)}, u32[]{:S(2)}) collective-permute-start(bf16[12,32,512]{2,1,0:T(8,128)(2,1)} %get-tuple-element.13), channel_id=1, source_target_pairs={{0,1},{1,0},{2,3},{3,2},{4,5},{5,4},{6,7},{7,6},{8,9},{9,8},{10,11... | collective-permute-start | bytes 1179656 | tf_op jit(solution)/shard_map/ppermute | solution.py:513
  23.2 19.0 %collective-permute-start.4 = (bf16[6,64,512]{2,1,0:T(8,128)(2,1)S(1)}, bf16[6,64,512]{2,1,0:T(8,128)(2,1)S(1)}, u32[]{:S(2)}, u32[]{:S(2)}) collective-permute-start(bf16[6,64,512]{2,1,0:T(8,128)(2,1)S(1)} %fusion), channel_id=1, source_target_pairs={{0,1},{1,0},{2,3},{3,2},{4,5},{5,4},{6,7},{7,6},{8,9},{9,8},{10,11... | collective-permute-start | bytes 1179656 | tf_op jit(solution)/shard_map/ppermute | solution.py:513
  34.7 15.3 %collective-permute-start.3 = (bf16[6,64,512]{2,1,0:T(8,128)(2,1)S(1)}, bf16[6,64,512]{2,1,0:T(8,128)(2,1)S(1)}, u32[]{:S(2)}, u32[]{:S(2)}) collective-permute-start(bf16[6,64,512]{2,1,0:T(8,128)(2,1)S(1)} %get-tuple-element.18), channel_id=1, source_target_pairs={{0,1},{1,0},{2,3},{3,2},{4,5},{5,4},{6,7},{7,6},{8,9},{9,8},{10,11... | collective-permute-start | bytes 1179656 | tf_op jit(solution)/shard_map/ppermute | solution.py:513
  42.2 7.9 %copy-start.1 = (bf16[256,256]{1,0:T(8,128)(2,1)S(1)}, bf16[256,256]{1,0:T(8,128)(2,1)}, u32[]{:S(2)}) copy-start(bf16[256,256]{1,0:T(8,128)(2,1)} %constant.35.clone.refs_3_.high_ref) | copy-start | bytes 393220
  47.6 9.5 %copy-start.2 = (bf16[256,256]{1,0:T(8,128)(2,1)S(1)}, bf16[256,256]{1,0:T(8,128)(2,1)}, u32[]{:S(2)}) copy-start(bf16[256,256]{1,0:T(8,128)(2,1)} %constant.36.clone.low_ref) | copy-start | bytes 393220
  47.6 9.5 %copy-start.3 = (s32[1024,1]{0,1:T(1,128)S(1)}, s32[1024,1]{0,1:T(1,128)}, u32[]{:S(2)}) copy-start(s32[1024,1]{0,1:T(1,128)} %param.9) | copy-start | bytes 12292
  57.9 4.0 %collective-permute-start.5 = (f32[32,256]{1,0:T(8,128)S(1)}, f32[32,256]{1,0:T(8,128)S(1)}, u32[]{:S(2)}, u32[]{:S(2)}) collective-permute-start(f32[32,256]{1,0:T(8,128)S(1)} %constant_dynamic-slice_fusion), channel_id=1, source_target_pairs={{0,1},{1,0},{2,3},{3,2},{4,5},{5,4},{6,7},{7,6},{8,9},{9,8},{10,11... | collective-permute-start | bytes 98312 | tf_op jit(solution)/shard_map/ppermute | solution.py:513
